TPU v7x, 32 devices: a whole 2x2x4 slice. The times are simulated.
32 devices in a mesh: ctx: 16 (over z, x, core), head: 2 (over y).
Axes of the slice: x: 2, y: 2, z: 4, core: 2. Of those that a mesh axis runs over, the one named last changes fastest.
Arguments:
- query: bfloat16 [2048, 4096], P('ctx', 'head'), may hold values from -12 to 12
- key: bfloat16 [2048, 1024], P('ctx', 'head'), may hold values from -6 to 6
- value: bfloat16 [2048, 1024], P('ctx', 'head'), may hold values from -6 to 6
- held_kv: bfloat16 [2, 2048, 1024], P(None, 'ctx', 'head'), may hold values from -6 to 6
- plan: int32 [16, 4], replicated, may hold values from 0 to 15
Outputs:
- attended: bfloat16 [2048, 4096], P(('ctx', 'head'))
- log_total: float32 [32, 2048], P('head', 'ctx')
All inputs are finite; a program needn't handle non-finite values.
Results may differ from a plain program's by a relative error of at most 0.012.
Values may be sent and summed in bfloat16 or wider, within the bound.
No kernel may reach another device: no remote copies, remote signals or barrier semaphores. Data moves between devices by JAX's collectives and lax.ppermute only.
A program may use at most 64 MiB of HBM per device.

v0:
```python
import math

import jax
import jax.numpy as jnp
from jax import lax
from jax.sharding import PartitionSpec as P

HD = 128
QB = 4
STEPS = 3


def shifted(block, axis, distance):
    devices = range(lax.axis_size(axis))
    route = [((i - distance) % len(devices), i) for i in devices]
    return lax.ppermute(block, axis, route)


def from_behind(value, axis, steps):
    count = lax.axis_size(axis)
    first, last = (max(0, -steps), min(count, count - steps))
    return lax.ppermute(value, axis, [(source, source + steps) for source in range(first, last)])


def attend_block(query_part, key_part, value_part, key_mask):
    score_scale = 1.0 / math.sqrt(query_part.shape[-1])
    scores = (
        jnp.einsum("rkhd,skd->khrs", query_part, key_part, preferred_element_type=jnp.float32)
        * score_scale
    )
    if key_mask is not None:
        scores = jnp.where(key_mask, scores, -jnp.inf)
    highest = jnp.max(scores, axis=-1, keepdims=True)
    weights = jnp.exp(scores - highest)
    totals = jnp.sum(weights, axis=-1)
    mixed = jnp.einsum(
        "khrs,skd->rkhd",
        weights.astype(jnp.bfloat16),
        value_part,
        preferred_element_type=jnp.float32,
    )
    norm_rows = jnp.transpose(totals, (2, 0, 1))
    log_rows = jnp.transpose(highest[..., 0], (2, 0, 1)) + jnp.log(norm_rows)
    return (mixed / norm_rows[..., None], log_rows)


def combine_parts(first, second):
    joined = jnp.logaddexp(first[1], second[1])
    mixed = (
        first[0] * jnp.exp(first[1] - joined)[..., None]
        + second[0] * jnp.exp(second[1] - joined)[..., None]
    )
    return (mixed, joined)


def shards(query, key, value, held_kv, plan):
    rows = query.shape[0]
    kv_local = key.shape[1] // HD
    q_local = query.shape[1] // HD
    group = q_local // kv_local
    sub_rows = rows // QB
    query_heads = query.reshape(rows, kv_local, group, HD)
    key_rows = key.reshape(rows, kv_local, HD)
    value_rows = value.reshape(rows, kv_local, HD)
    positions = jnp.arange(rows)
    causal = positions[:, None] >= positions[None, :]
    running = attend_block(query_heads, key_rows, value_rows, causal)
    cycle_size = lax.axis_size("ctx")
    device = lax.axis_index("ctx")
    half_cycle = cycle_size // 2
    first_step = half_cycle - 2
    sched_step = plan[:, 0]
    sched_owner = plan[:, 2]
    sched_block = plan[:, 3]
    held_now = held_kv.reshape(2, rows, kv_local, HD)
    empty_out = jnp.zeros((sub_rows, kv_local, group, HD), jnp.float32)
    empty_log = jnp.zeros((sub_rows, kv_local, group), jnp.float32)
    for cycle_step in range(STEPS):
        if cycle_step > 0:
            held_now = shifted(held_now, "ctx", 1)
        regular_ok = device >= first_step + cycle_step
        running = lax.cond(
            regular_ok,
            lambda current: combine_parts(
                current, attend_block(query_heads, held_now[0], held_now[1], None)
            ),
            lambda current: current,
            running,
        )
        owner_match = (sched_step == cycle_step) & (sched_owner == device)
        owner_flag = jnp.any(owner_match)
        owner_block = jnp.sum(jnp.where(owner_match, sched_block, 0))
        own_rows = lax.dynamic_slice_in_dim(query_heads, owner_block * sub_rows, sub_rows, 0)
        far_pair = from_behind(held_now, "ctx", half_cycle)
        extra = lax.cond(
            owner_flag,
            lambda: attend_block(own_rows, far_pair[0], far_pair[1], None),
            lambda: (empty_out, empty_log),
        )

        def merge_owned(current):
            old_out = lax.dynamic_slice_in_dim(current[0], owner_block * sub_rows, sub_rows, 0)
            old_log = lax.dynamic_slice_in_dim(current[1], owner_block * sub_rows, sub_rows, 0)
            new_out, new_log = combine_parts((old_out, old_log), (extra[0], extra[1]))
            whole_out = lax.dynamic_update_slice_in_dim(
                current[0], new_out, owner_block * sub_rows, 0
            )
            whole_log = lax.dynamic_update_slice_in_dim(
                current[1], new_log, owner_block * sub_rows, 0
            )
            return (whole_out, whole_log)

        running = lax.cond(owner_flag, merge_owned, lambda current: current, running)
    out_rows = running[0].astype(jnp.bfloat16).reshape(rows, q_local * HD)
    attended = lax.all_to_all(out_rows, "head", split_axis=0, concat_axis=1, tiled=True)
    log_rows = jnp.transpose(running[1].reshape(rows, q_local))
    return (attended, log_rows)


def solution(mesh):
    return jax.shard_map(
        shards,
        mesh=mesh,
        in_specs=(
            P("ctx", "head"),
            P("ctx", "head"),
            P("ctx", "head"),
            P(None, "ctx", "head"),
            P(),
        ),
        out_specs=(P(("ctx", "head"), None), P("head", "ctx")),
        check_vma=False,
    )
```

profile of v0, /device:TPU:16, one launch (start us, length us, event | category | flops | bytes accessed | tf_op | source)
XLA Modules:
  0.0 114.9 jit_solution(10774761106777529262)
XLA Ops:
  0.6 1.8 %copy.146 = bf16[2,128,512]{1,2,0:T(8,128)(2,1)} copy(bf16[2,128,512]{2,1,0:T(8,128)(2,1)} %param.26) | data formatting | bytes 524288 | tf_op args[3]
  6.1 19.8 %collective-permute-done.1 = bf16[2,128,4,128]{1,3,2,0:T(8,128)(2,1)} collective-permute-done((bf16[2,128,4,128]{1,3,2,0:T(8,128)(2,1)}, bf16[2,128,4,128]{1,3,2,0:T(8,128)(2,1)}, u32[]{:S(2)}, u32[]{:S(2)}) %collective-permute-start.1) | collective-permute-done | bytes 262176 | tf_op jit(solution)/shard_map/ppermute | solution.py:16
  27.8 12.7 %collective-permute-done.3 = bf16[2,128,4,128]{1,3,2,0:T(8,128)(2,1)} collective-permute-done((bf16[2,128,4,128]{1,3,2,0:T(8,128)(2,1)}, bf16[2,128,4,128]{1,3,2,0:T(8,128)(2,1)}, u32[]{:S(2)}, u32[]{:S(2)}) %collective-permute-start.3) | collective-permute-done | bytes 262176 | tf_op jit(solution)/shard_map/ppermute | solution.py:16
  45.0 5.7 %conditional.9 = (f32[128,4,4,128]{3,0,2,1:T(8,128)S(1)}, f32[128,4,4]{0,2,1:T(4,128)S(1)}, (f32[128,4,4,128]{3,2,1,0:T(4,128)}, f32[128,4,4]{2,1,0:T(4,128)})) conditional(s32[]{:T(128)} %convert_element_type.56, (f32[128,4,4,128]{3,0,2,1:T(8,128)S(1)}, f32[128,4,4]{0,2,1:T(4,128)S(1)}) %tuple.84, (bf16[2,128,4,128]{1,3,2,0:T(8,128)(2,1)}, ...), branch_computations={%region_5.0_spmd.clone, %region_6.9_spmd.clone} | conditional | flops 136859648 | bytes 8798248 | solution.py:82
  48.2 1.7 %copy.236 = f32[128,4,4,128]{3,2,1,0:T(4,128)} copy(f32[128,4,4,128]{3,0,2,1:T(8,128)S(1)} %fusion.28) | data formatting | bytes 2097152 | tf_op jit(solution)/shard_map/cond | solution.py:82
  50.7 4.3 %conditional.11 = (f32[128,4,4,128]{3,2,1,0:T(4,128)}, f32[128,4,4]{2,1,0:T(4,128)}, (f32[128,4,4,128]{3,0,2,1:T(8,128)}, f32[128,4,4]{0,2,1:T(4,128)})) conditional(s32[]{:T(128)} %convert_element_type.55, (f32[128,4,4,128]{3,2,1,0:T(4,128)}, f32[128,4,4]{2,1,0:T(4,128)}) %get-tuple-element.458, (s32[]{:T(128)}, ...), branch_computations={%region_14.15_spmd.clone, %region_15.16_spmd.clone} | conditional | flops 201732 | bytes 5159006 | solution.py:113
  50.7 2.6 %copy.238 = f32[128,4,4,128]{3,0,2,1:T(8,128)} copy(f32[128,4,4,128]{3,2,1,0:T(4,128)} %get-tuple-element.587) | data formatting | bytes 2097152 | tf_op jit(solution)/shard_map/cond | solution.py:113
  55.0 11.5 %conditional.12 = (f32[128,4,4,128]{3,0,2,1:T(8,128)}, f32[128,4,4]{0,2,1:T(4,128)}, (f32[128,4,4,128]{3,2,1,0:T(4,128)}, f32[128,4,4]{2,1,0:T(4,128)})) conditional(s32[]{:T(128)} %convert_element_type.54, (f32[128,4,4,128]{3,0,2,1:T(8,128)}, f32[128,4,4]{0,2,1:T(4,128)}) %get-tuple-element.462, (bf16[2,128,4,128]{1,3,2,0:T(8,128)(2,1)}, ...), branch_computations={%region_16.17_spmd.clone, %region_17.20_spmd.clone} | conditional | flops 136859648 | bytes 8814632 | solution.py:82
  59.0 3.0 %fusion.38 = f32[128,4,4,128]{3,0,2,1:T(8,128)} fusion(f32[128,4,4,128]{3,2,1,0:T(4,128)} %get-tuple-element.508, f32[4,4,128,128]{2,3,1,0:T(8,128)S(1)} %get-tuple-element.568, f32[128,4,4]{0,2,1:T(4,128)S(1)} %subtract_exponential_fusion.11, f32[128,4,4]{0,2,1:T(4,128)S(1)} %bitcast.232, f32[128,4,4]{0,2,1:T(4,128)S(1)} %get-tuple-element.545, ...), kind=kOutput, calls=%fused_computation.72 | convolution fusion | flops 68681728 | bytes 3309568 | tf_op jit(solution)/shard_map/cond/branch_1_fun/khrs,skd->rkhd/dot_general | solution.py:36
  62.1 2.9 %copy.251 = f32[128,4,4,128]{3,2,1,0:T(4,128)} copy(f32[128,4,4,128]{3,0,2,1:T(8,128)} %fusion.38) | data formatting | bytes 2097152 | tf_op jit(solution)/shard_map/cond | solution.py:82
  66.5 2.0 %conditional.13 = (f32[32,4,4,128]{3,0,2,1:T(8,128)S(1)}, f32[32,4,4]{0,2,1:T(4,128)S(1)}) conditional(s32[]{:T(128)} %convert_element_type.53, () %tuple.90, (s32[]{:T(128)}, bf16[128,4,4,128]{0,3,2,1:T(8,128)(2,1)S(1)}, bf16[2,128,4,128]{1,3,2,0:T(8,128)(2,1)S(1)}) %tuple.264), branch_computations={%region_21.22_spmd, %region_22.25_spmd} | conditional | flops 34012676 | bytes 3043394 | solution.py:95
  68.5 13.2 %conditional.14 = (f32[128,4,4,128]{3,2,1,0:T(4,128)}, f32[128,4,4]{2,1,0:T(4,128)}, (f32[128,4,4,128]{3,0,2,1:T(8,128)}, f32[128,4,4]{0,2,1:T(4,128)})) conditional(s32[]{:T(128)} %convert_element_type.53, (f32[128,4,4,128]{3,2,1,0:T(4,128)}, f32[128,4,4]{2,1,0:T(4,128)}) %get-tuple-element.466, (s32[]{:T(128)}, ...), branch_computations={%region_25.26_spmd.clone, %region_26.27_spmd.clone} | conditional | flops 201732 | bytes 5159006 | solution.py:113
  72.5 2.9 %copy.255 = f32[128,4,4,128]{3,2,1,0:T(4,128)} copy(f32[128,4,4,128]{3,0,2,1:T(8,128)} %get-tuple-element.518) | data formatting | bytes 2097152 | tf_op jit(solution)/shard_map
  75.4 2.0 %fusion.45 = f32[128,4,4,128]{3,2,1,0:T(4,128)} fusion(f32[128,4,4,128]{3,2,1,0:T(4,128)} %copy.255, s32[]{:T(128)S(6)} %select_n.79, f32[32,4,4,128]{3,0,2,1:T(8,128)S(1)} %get-tuple-element.521, f32[32,4,4]{2,1,0:T(4,128)S(1)} %get-tuple-element.564, f32[32,4,4]{2,1,0:T(4,128)S(1)} %get-tuple-element.563), kind=kLoop, calls=%fused_computation.88 | loop fusion | flops 196608 | bytes 790532 | tf_op jit(solution)/shard_map/cond/branch_1_fun/dynamic_update_slice | solution.py:105
  77.4 2.6 %copy.259 = f32[128,4,4,128]{3,0,2,1:T(8,128)} copy(f32[128,4,4,128]{3,2,1,0:T(4,128)} %fusion.45) | data formatting | bytes 2097152 | tf_op jit(solution)/shard_map/cond | solution.py:113
  81.7 10.8 %conditional.15 = (f32[128,4,4,128]{3,0,2,1:T(8,128)}, f32[128,4,4]{0,2,1:T(4,128)}, (f32[128,4,4,128]{3,2,1,0:T(4,128)}, f32[128,4,4]{2,1,0:T(4,128)S(1)})) conditional(s32[]{:T(128)} %convert_element_type.52, (f32[128,4,4,128]{3,0,2,1:T(8,128)}, f32[128,4,4]{0,2,1:T(4,128)}) %get-tuple-element.470, ...), branch_computations={%region_27.28_spmd.clone, %region_28.31_spmd.clone} | conditional | flops 136859648 | bytes 8814632 | solution.py:82
  85.7 3.0 %fusion.48 = f32[128,4,4,128]{3,0,2,1:T(8,128)} fusion(f32[128,4,4,128]{3,2,1,0:T(4,128)} %get-tuple-element.533, f32[4,4,128,128]{2,3,1,0:T(8,128)S(1)} %get-tuple-element.570, f32[128,4,4]{0,2,1:T(4,128)S(1)} %subtract_exponential_fusion.16, f32[128,4,4]{0,2,1:T(4,128)S(1)} %bitcast.233, f32[128,4,4]{0,2,1:T(4,128)S(1)} %get-tuple-element.547, ...), kind=kOutput, calls=%fused_computation.96 | convolution fusion | flops 68681728 | bytes 3309568 | tf_op jit(solution)/shard_map/cond/branch_1_fun/khrs,skd->rkhd/dot_general | solution.py:36
  88.7 2.9 %copy.266 = f32[128,4,4,128]{3,2,1,0:T(4,128)} copy(f32[128,4,4,128]{3,0,2,1:T(8,128)} %fusion.48) | data formatting | bytes 2097152 | tf_op jit(solution)/shard_map/cond | solution.py:82
  92.5 2.0 %conditional.16 = (f32[32,4,4,128]{3,0,2,1:T(8,128)S(1)}, f32[32,4,4]{0,2,1:T(4,128)S(1)}) conditional(s32[]{:T(128)} %convert_element_type.51, () %tuple.94, (s32[]{:T(128)}, bf16[128,4,4,128]{0,3,2,1:T(8,128)(2,1)S(1)}, bf16[2,128,4,128]{1,3,2,0:T(8,128)(2,1)S(1)}) %tuple.266), branch_computations={%region_32.33_spmd, %region_33.36_spmd} | conditional | flops 34012676 | bytes 3043394 | solution.py:95
  94.5 6.9 %conditional.17 = ((f32[128,4,4,128]{3,2,1,0:T(4,128)}, f32[128,4,4]{2,1,0:T(4,128)S(1)})) conditional(s32[]{:T(128)} %convert_element_type.51, (f32[128,4,4,128]{3,2,1,0:T(4,128)}, f32[128,4,4]{2,1,0:T(4,128)S(1)}) %get-tuple-element.474, (s32[]{:T(128)}, f32[128,4,4,128]{3,0,2,1:T(8,128)}, f32[128,4,4]{0,2,1:T(4,128)}, ...), branch_computations={%region_36.37_spmd, %region_37.38_spmd} | conditional | flops 201732 | bytes 3301510 | solution.py:113
  96.3 3.0 %copy.181 = f32[128,4,4,128]{3,2,1,0:T(4,128)} copy(f32[128,4,4,128]{3,0,2,1:T(8,128)} %get-tuple-element.451) | data formatting | bytes 2097152 | tf_op jit(solution)/shard_map
  99.4 2.0 %fusion.25 = f32[128,4,4,128]{3,2,1,0:T(4,128)} fusion(f32[128,4,4,128]{3,2,1,0:T(4,128)} %copy.181, s32[]{:T(128)S(6)} %select_n.65, f32[32,4,4,128]{3,0,2,1:T(8,128)S(1)} %get-tuple-element.454, f32[32,4,4]{2,1,0:T(4,128)S(1)} %get-tuple-element.558, f32[32,4,4]{2,1,0:T(4,128)S(1)} %get-tuple-element.557), kind=kLoop, calls=%fused_computation.41 | loop fusion | flops 196608 | bytes 790532 | tf_op jit(solution)/shard_map/cond/branch_1_fun/dynamic_update_slice | solution.py:105
  104.0 3.5 %all-to-all-start = ((bf16[2,64,2048]{2,1,0:T(8,128)(2,1)}), bf16[2,64,2048]{2,1,0:T(8,128)(2,1)S(1)}, u32[]{:S(2)}, u32[]{:S(2)}) async-start(bf16[2,64,2048]{2,1,0:T(8,128)(2,1)} %all_to_all.14), calls=%async_computation | async-start | bytes 1048576 | tf_op jit(solution)/shard_map/all_to_all | solution.py:115
  108.2 5.8 %all-to-all-done = bf16[2,64,2048]{2,1,0:T(8,128)(2,1)S(1)} async-done(((bf16[2,64,2048]{2,1,0:T(8,128)(2,1)}), bf16[2,64,2048]{2,1,0:T(8,128)(2,1)S(1)}, u32[]{:S(2)}, u32[]{:S(2)}) %all-to-all-start) | async-done | bytes 524320 | tf_op jit(solution)/shard_map/all_to_all | solution.py:115
  (78 shorter events, 37.0 us)
Async XLA Ops:
  0.6 3.2 %copy-start.2 = (bf16[128,2048]{1,0:T(8,128)(2,1)S(1)}, bf16[128,2048]{1,0:T(8,128)(2,1)}, u32[]{:S(2)}) copy-start(bf16[128,2048]{1,0:T(8,128)(2,1)} %param.23) | copy-start | bytes 1572868
  2.5 48.2 %collective-permute-start = (bf16[2,128,4,128]{1,3,2,0:T(8,128)(2,1)}, bf16[2,128,4,128]{1,3,2,0:T(8,128)(2,1)S(1)}, u32[]{:S(2)}, u32[]{:S(2)}) collective-permute-start(bf16[2,128,4,128]{1,3,2,0:T(8,128)(2,1)} %bitcast.67), channel_id=1, source_target_pairs={{0,16},{2,18},{4,20},{6,22},{8,24},{10,26},{12,28},{14,30},{1,17},... | collective-permute-start | bytes 786440 | tf_op jit(solution)/shard_map/ppermute | solution.py:22
  3.8 22.1 %collective-permute-start.1 = (bf16[2,128,4,128]{1,3,2,0:T(8,128)(2,1)}, bf16[2,128,4,128]{1,3,2,0:T(8,128)(2,1)}, u32[]{:S(2)}, u32[]{:S(2)}) collective-permute-start(bf16[2,128,4,128]{1,3,2,0:T(8,128)(2,1)} %bitcast.67), channel_id=1, source_target_pairs={{30,0},{0,2},{2,4},{4,6},{6,8},{8,10},{10,12},{12,14},{14,16},{16,... | collective-permute-start | bytes 786440 | tf_op jit(solution)/shard_map/ppermute | solution.py:16
  3.9 0.9 copy-start.3
  5.1 0.9 copy-start.4
  25.9 14.7 %collective-permute-start.3 = (bf16[2,128,4,128]{1,3,2,0:T(8,128)(2,1)}, bf16[2,128,4,128]{1,3,2,0:T(8,128)(2,1)}, u32[]{:S(2)}, u32[]{:S(2)}) collective-permute-start(bf16[2,128,4,128]{1,3,2,0:T(8,128)(2,1)} %collective-permute-done.1), channel_id=1, source_target_pairs={{30,0},{0,2},{2,4},{4,6},{6,8},{8,10},{10,12},{12,14},{14,16},{16,... | collective-permute-start | bytes 786440 | tf_op jit(solution)/shard_map/ppermute | solution.py:16
  26.5 15.3 %copy-start.5 = (s32[16,4]{0,1:T(4,128)S(1)}, s32[16,4]{0,1:T(4,128)}, u32[]{:S(2)}) copy-start(s32[16,4]{0,1:T(4,128)} %param.27) | copy-start | bytes 772
  26.5 40.0 %collective-permute-start.2 = (bf16[2,128,4,128]{1,3,2,0:T(8,128)(2,1)}, bf16[2,128,4,128]{1,3,2,0:T(8,128)(2,1)S(1)}, u32[]{:S(2)}, u32[]{:S(2)}) collective-permute-start(bf16[2,128,4,128]{1,3,2,0:T(8,128)(2,1)} %collective-permute-done.1), channel_id=1, source_target_pairs={{0,16},{2,18},{4,20},{6,22},{8,24},{10,26},{12,28},{14,30},{1,17},... | collective-permute-start | bytes 786440 | tf_op jit(solution)/shard_map/ppermute | solution.py:22
  40.5 52.0 %collective-permute-start.4 = (bf16[2,128,4,128]{1,3,2,0:T(8,128)(2,1)}, bf16[2,128,4,128]{1,3,2,0:T(8,128)(2,1)S(1)}, u32[]{:S(2)}, u32[]{:S(2)}) collective-permute-start(bf16[2,128,4,128]{1,3,2,0:T(8,128)(2,1)} %collective-permute-done.3), channel_id=1, source_target_pairs={{0,16},{2,18},{4,20},{6,22},{8,24},{10,26},{12,28},{14,30},{1,17},... | collective-permute-start | bytes 786440 | tf_op jit(solution)/shard_map/ppermute | solution.py:22
  96.3 3.0 %copy-start = (f32[128,4,4]{2,1,0:T(4,128)}, f32[128,4,4]{2,1,0:T(4,128)S(1)}, u32[]{:S(2)}) copy-start(f32[128,4,4]{2,1,0:T(4,128)S(1)} %get-tuple-element.638) | copy-start | bytes 24580 | tf_op jit(solution)/shard_map/cond
  99.4 2.0 %copy-start.1 = (f32[128,4,4]{2,1,0:T(4,128)S(1)}, f32[128,4,4]{2,1,0:T(4,128)}, u32[]{:S(2)}) copy-start(f32[128,4,4]{2,1,0:T(4,128)} %copy-done) | copy-start | bytes 24580 | tf_op jit(solution)/shard_map/cond
  104.0 10.1 %all-to-all-start = ((bf16[2,64,2048]{2,1,0:T(8,128)(2,1)}), bf16[2,64,2048]{2,1,0:T(8,128)(2,1)S(1)}, u32[]{:S(2)}, u32[]{:S(2)}) async-start(bf16[2,64,2048]{2,1,0:T(8,128)(2,1)} %all_to_all.14), calls=%async_computation | async-start | bytes 1048576 | tf_op jit(solution)/shard_map/all_to_all | solution.py:115
where the time goes:
time: 116 us; the launch traced here: 115 us
  local copies, waits for them, and re-layouts  40.4 us (35%)
  waiting for transfers between devices  38.3 us (33%)
  other arithmetic  12.6 us (11%)
  matrix products  10.5 us (9%)
  starting transfers between devices  7.4 us (6%)
  loops' own time  2.94 us (3%)
  between operations  2.63 us (2%)
    ppermute x2, waiting for transfers between devices, shifted(): return lax.ppermute(block, axis, route)  32.5 us
    another operation x15, local copies, waits for them, and re-layouts  14.9 us
    cond x6, local copies, waits for them, and re-layouts, shards(): lax.cond(regular_ok, lambda current: combine_parts(current, attend_block(...  10.7 us
    cond x5, local copies, waits for them, and re-layouts, shards(): lax.cond(owner_flag, merge_owned, lambda current: current, running)  9.19 us
    dot_general x6, matrix products, attend_block(): jnp.einsum('khrs,skd->rkhd', weights.astype(jnp.bfloat16), value_part, pr...  8.68 us
    all_to_all x1, waiting for transfers between devices, shards(): lax.all_to_all(out_rows, 'head', split_axis=0, concat_axis=1, tiled=True)  5.84 us
    dynamic_update_slice x2, other arithmetic, merge_owned(): lax.dynamic_update_slice_in_dim(current[0], new_out, owner_block * sub_ro...  4.05 us
    ppermute x3, starting transfers between devices, from_behind(): lax.ppermute(value, axis, [(source, source + steps) for source in range(f...  3.85 us
  transfers between devices with their start and end apart: 6, of which 3 were waited for; matrix products, arithmetic and copies ran while one was open for 43% of the time, Pallas kernels for 0%

commit v1 on v0

v1 whole, which is shorter than its diff:
```python
import functools
import math

import jax
import jax.numpy as jnp
from jax import lax
from jax.experimental import pallas as pl
from jax.experimental.pallas import tpu as pltpu
from jax.sharding import PartitionSpec as P

HD = 128
QB = 4
STEPS = 3
CHUNKS = ((0, 2), (2, 2))
SCALE = 1.0 / math.sqrt(HD)
LOG2E = math.log2(math.e)
NEG = -math.inf

SMEM = pl.BlockSpec(memory_space=pltpu.SMEM)
VMEM = pl.BlockSpec(memory_space=pltpu.VMEM)
ANY = pl.BlockSpec(memory_space=pl.ANY)


def stacked(q_ref, kv_head, group):
    first = kv_head * group
    return jnp.concatenate(
        [q_ref[:, (first + j) * HD : (first + j + 1) * HD] for j in range(group)], axis=0
    )


def scores_of(keys, queries):
    return lax.dot_general(
        keys, queries, (((1,), (1,)), ((), ())), preferred_element_type=jnp.float32
    )


def mix(values, weights):
    return lax.dot_general(
        values,
        weights.astype(jnp.bfloat16),
        (((0,), (0,)), ((), ())),
        preferred_element_type=jnp.float32,
    )


def local_kernel(half, entries, idx_ref, plan_ref, q_ref, k_ref, v_ref, held_ref, acc_ref, stat_ref, meta_ref):
    rows = q_ref.shape[0]
    kv_heads = k_ref.shape[1] // HD
    group = q_ref.shape[1] // k_ref.shape[1]
    device = idx_ref[0]
    for t in range(STEPS):
        meta_ref[t] = -1

    def scan(i, carry):
        @pl.when(plan_ref[i, 2] == device)
        def _():
            meta_ref[plan_ref[i, 0]] = plan_ref[i, 3]

        return carry

    lax.fori_loop(0, entries, scan, 0)
    held_bias = jnp.where(device >= half - 2, 0.0, NEG)
    key_pos = lax.broadcasted_iota(jnp.int32, (rows, group * rows), 0)
    row_pos = lax.broadcasted_iota(jnp.int32, (rows, group * rows), 1) % rows
    causal = key_pos <= row_pos
    for g in range(kv_heads):
        cols = slice(g * HD, (g + 1) * HD)
        queries = stacked(q_ref, g, group)
        own = jnp.where(causal, scores_of(k_ref[:, cols], queries), NEG)
        held = scores_of(held_ref[0, :, cols], queries) + held_bias
        top = jnp.maximum(
            jnp.max(own, axis=0, keepdims=True), jnp.max(held, axis=0, keepdims=True)
        )
        w_own = jnp.exp2((own - top) * (SCALE * LOG2E))
        w_held = jnp.exp2((held - top) * (SCALE * LOG2E))
        stat_ref[g, 0:1, :] = top
        stat_ref[g, 1:2, :] = jnp.sum(w_own, axis=0, keepdims=True) + jnp.sum(
            w_held, axis=0, keepdims=True
        )
        acc_ref[g] = mix(v_ref[:, cols], w_own) + mix(held_ref[1, :, cols], w_held)


def final_kernel(
    half, first, count,
    idx_ref, meta_ref, q_ref, acc_ref, stat_ref,
    n2, sx, sn2, w, sw, f, h, sf, sh,
    mine_ref, send_ref, log_ref,
    kv, sem,
):
    rows = q_ref.shape[0]
    group = q_ref.shape[1] // (count * HD)
    device = idx_ref[0]
    head = idx_ref[1]
    even = device % 2 == 0
    wide = pl.ds(first * HD, count * HD)
    step_a = jnp.where(meta_ref[0] >= 0, 0, 1)
    step_b = jnp.where(meta_ref[2] >= 0, 2, 1)

    def pick(slot, source, when, whole):
        @pl.when(when)
        def _():
            part = source.at[:, :, wide] if whole else source
            pltpu.make_async_copy(part, kv.at[slot], sem.at[slot]).start()

    pick(0, sn2, even, True)
    pick(0, sx, jnp.logical_not(even), True)
    pick(1, n2, device >= 0, True)
    for slot, step in ((2, step_a), (3, step_b)):
        if slot == 2:
            pick(slot, f, step == 0, False)
        else:
            pick(slot, w, (step == 2) & (device <= half + 1), True)
            pick(slot, h, (step == 2) & (device > half + 1), False)
        pick(slot, sf, (step == 1) & jnp.logical_not(even), False)
        pick(slot, sw, (step == 1) & even & (device <= half), True)
        pick(slot, sh, (step == 1) & even & (device > half), False)
    for slot in range(4):
        pltpu.make_async_copy(f, kv.at[slot], sem.at[slot]).wait()

    lane = lax.broadcasted_iota(jnp.int32, (1, group * rows), 1)
    sub = (lane % rows) // (rows // QB)
    biases = [
        jnp.where(device >= half - 1, 0.0, NEG),
        jnp.where(device >= half, 0.0, NEG),
        jnp.where(sub == meta_ref[step_a], 0.0, NEG),
        jnp.where(sub == meta_ref[step_b], 0.0, NEG),
    ]
    for g in range(count):
        cols = slice(g * HD, (g + 1) * HD)
        queries = stacked(q_ref, g, group)
        scores = [scores_of(kv[s, 0, :, cols], queries) + biases[s] for s in range(4)]
        old_top = stat_ref[g, 0:1, :]
        top = old_top
        for s in scores:
            top = jnp.maximum(top, jnp.max(s, axis=0, keepdims=True))
        keep = jnp.exp2((old_top - top) * (SCALE * LOG2E))
        total = stat_ref[g, 1:2, :] * keep
        mixed = acc_ref[g] * keep
        for slot, s in enumerate(scores):
            weights = jnp.exp2((s - top) * (SCALE * LOG2E))
            total = total + jnp.sum(weights, axis=0, keepdims=True)
            mixed = mixed + mix(kv[slot, 1, :, cols], weights)
        mixed = mixed * (1.0 / total)
        logs = top * SCALE + jnp.log(total)
        for j in range(group):
            out = jnp.transpose(mixed[:, j * rows : (j + 1) * rows]).astype(jnp.bfloat16)
            low, high = out[: rows // 2], out[rows // 2 :]
            at = slice((g * group + j) * HD, (g * group + j + 1) * HD)
            mine_ref[:, at] = jnp.where(head == 0, low, high)
            send_ref[:, at] = jnp.where(head == 0, high, low)
            log_ref[g * group + j : g * group + j + 1, :] = logs[:, j * rows : (j + 1) * rows]


def shards(query, key, value, held_kv, plan):
    rows = query.shape[0]
    kv_heads = key.shape[1] // HD
    group = query.shape[1] // key.shape[1]
    size = lax.axis_size("ctx")
    half = size // 2
    device = lax.axis_index("ctx")
    head = lax.axis_index("head")
    idx = jnp.stack([device, head]).astype(jnp.int32)

    def send(x, route):
        return lax.ppermute(x, "ctx", route)

    owners = range(half, size)
    n2 = send(held_kv, [(b - 2, b) for b in owners])
    sx = send(held_kv, [(b, b + 1) for b in range(half - 2, size, 2)])
    w = send(held_kv, [(size - 2, half), (size - 1, half + 1)])
    sw = send(w, [(half + 1, half)])
    sn2 = send(n2, [(b + 1, b) for b in range(half, size, 2)])

    acc, stat, meta = pl.pallas_call(
        functools.partial(local_kernel, half, plan.shape[0]),
        out_shape=(
            jax.ShapeDtypeStruct((kv_heads, HD, group * rows), jnp.float32),
            jax.ShapeDtypeStruct((kv_heads, 2, group * rows), jnp.float32),
            jax.ShapeDtypeStruct((STEPS,), jnp.int32),
        ),
        in_specs=[SMEM, SMEM, VMEM, VMEM, VMEM, VMEM],
        out_specs=(VMEM, VMEM, SMEM),
        name="local",
    )(idx, plan, query, key, value, held_kv)

    pieces = []
    for first, count in CHUNKS:
        part = held_kv[:, :, first * HD : (first + count) * HD]
        f = send(part, [(b - half, b) for b in range(half, size - 1)])
        h = send(f, [(b - 2, b) for b in range(half + 2, size)])
        sf = send(f, [(b, b + 1) for b in range(half, size, 2)])
        sh = send(h, [(b + 1, b) for b in range(half + 2, size, 2)])
        wide = count * group * HD
        at = first // count
        mine, away, logs = pl.pallas_call(
            functools.partial(final_kernel, half, first, count),
            grid=(1,),
            out_shape=(
                jax.ShapeDtypeStruct((rows // 2, wide), jnp.bfloat16),
                jax.ShapeDtypeStruct((rows // 2, wide), jnp.bfloat16),
                jax.ShapeDtypeStruct((count * group, rows), jnp.float32),
            ),
            in_specs=[
                SMEM,
                SMEM,
                pl.BlockSpec((rows, wide), lambda i, at=at: (0, at)),
                pl.BlockSpec((count, HD, group * rows), lambda i, at=at: (at, 0, 0)),
                pl.BlockSpec((count, 2, group * rows), lambda i, at=at: (at, 0, 0)),
            ]
            + [ANY] * 9,
            out_specs=(
                pl.BlockSpec((rows // 2, wide), lambda i: (0, 0)),
                pl.BlockSpec((rows // 2, wide), lambda i: (0, 0)),
                pl.BlockSpec((count * group, rows), lambda i: (0, 0)),
            ),
            scratch_shapes=[
                pltpu.VMEM((4, 2, rows, count * HD), jnp.bfloat16),
                pltpu.SemaphoreType.DMA((4,)),
            ],
            name="final",
        )(idx, meta, query, acc, stat, n2, sx, sn2, w, sw, f, h, sf, sh)
        there = lax.ppermute(away, "head", [(0, 1), (1, 0)])
        pieces.append((mine, there, logs))
    mine = jnp.concatenate([p[0] for p in pieces], axis=1)
    there = jnp.concatenate([p[1] for p in pieces], axis=1)
    attended = jnp.where(
        head == 0,
        jnp.concatenate([mine, there], axis=1),
        jnp.concatenate([there, mine], axis=1),
    )
    return (attended, jnp.concatenate([p[2] for p in pieces], axis=0))


def solution(mesh):
    return jax.shard_map(
        shards,
        mesh=mesh,
        in_specs=(
            P("ctx", "head"),
            P("ctx", "head"),
            P("ctx", "head"),
            P(None, "ctx", "head"),
            P(),
        ),
        out_specs=(P(("ctx", "head"), None), P("head", "ctx")),
        check_vma=False,
    )
```

time: 116 us -> 64.7 us (0.56)
  the two profiles are of different devices: /device:TPU:16 before, /device:TPU:19 now
where the time goes in v1:
time: 64.7 us; the launch traced here: 64.1 us
  starting transfers between devices  34.9 us (54%)
  Pallas kernels  12.9 us (20%)
  waiting for transfers between devices  6.6 us (10%)
  local copies, waits for them, and re-layouts  4.87 us (8%)
  other arithmetic  3.76 us (6%)
  between operations  1.02 us (2%)
    ppermute x13, starting transfers between devices, send(): return lax.ppermute(x, 'ctx', route)  33.4 us
    pallas_call x2, Pallas kernels, shards(): pl.pallas_call(functools.partial(final_kernel, half, first, count), grid=...  8.85 us
    pallas_call x1, Pallas kernels, shards(): pl.pallas_call(functools.partial(local_kernel, half, plan.shape[0]), out_...  4.04 us
    unnamed x35, local copies, waits for them, and re-layouts  3.88 us
    ppermute x2, waiting for transfers between devices, shards(): there = lax.ppermute(away, 'head', [(0, 1), (1, 0)])  3.71 us
    ppermute x13, waiting for transfers between devices, send(): return lax.ppermute(x, 'ctx', route)  2.89 us
    select_n x1, other arithmetic, shards(): jnp.where(head == 0, jnp.concatenate([mine, there], axis=1), jnp.concaten...  1.9 us
    ppermute x2, starting transfers between devices, shards(): there = lax.ppermute(away, 'head', [(0, 1), (1, 0)])  1.59 us
  transfers between devices with their start and end apart: 15, of which 3 were waited for; matrix products, arithmetic and copies ran while one was open for 6% of the time, Pallas kernels for 20%

profile of v1, /device:TPU:19, one launch (start us, length us, event | category | flops | bytes accessed | tf_op | source)
XLA Modules:
  0.0 64.1 jit_solution(9604790866843945712)
XLA Ops:
  0.6 3.3 %collective-permute-start = (bf16[2,128,512]{2,1,0:T(8,128)(2,1)}, bf16[2,128,512]{2,1,0:T(8,128)(2,1)S(1)}, u32[]{:S(2)}, u32[]{:S(2)}) collective-permute-start(bf16[2,128,512]{2,1,0:T(8,128)(2,1)} %held_ref.1), channel_id=1, source_target_pairs={{12,16},{14,18},{16,20},{18,22},{20,24},{22,26},{24,28},{26,30},{1... | collective-permute-start | bytes 786440 | tf_op jit(solution)/shard_map/ppermute | solution.py:165
  4.0 0.7 %collective-permute-start.3 = (bf16[2,128,512]{2,1,0:T(8,128)(2,1)}, bf16[2,128,512]{2,1,0:T(8,128)(2,1)S(1)}, u32[]{:S(2)}, u32[]{:S(2)}) collective-permute-start(bf16[2,128,512]{2,1,0:T(8,128)(2,1)} %held_ref.1), channel_id=1, source_target_pairs={{28,16},{30,18},{29,17},{31,19}} | collective-permute-start | bytes 786440 | tf_op jit(solution)/shard_map/ppermute | solution.py:165
  4.6 1.0 %fusion = (bf16[2,128,256]{2,1,0:T(8,128)(2,1)S(1)}, bf16[2,128,256]{2,1,0:T(8,128)(2,1)S(1)}) fusion(bf16[2,128,512]{2,1,0:T(8,128)(2,1)} %held_ref.1), kind=kLoop, calls=%fused_computation.3 | loop fusion | bytes 524288 | tf_op jit(solution)/shard_map/slice | solution.py:188
  5.6 1.3 %collective-permute-start.5 = (bf16[2,128,256]{2,1,0:T(8,128)(2,1)S(1)}, bf16[2,128,256]{2,1,0:T(8,128)(2,1)S(1)}, u32[]{:S(2)}, u32[]{:S(2)}) collective-permute-start(bf16[2,128,256]{2,1,0:T(8,128)(2,1)S(1)} %get-tuple-element.20), channel_id=1, source_target_pairs={{0,16},{2,18},{4,20},{6,22},{8,24},{10,26},{12,28},{1,17},{3,19},{... | collective-permute-start | bytes 393224 | tf_op jit(solution)/shard_map/ppermute | solution.py:165
  6.9 1.3 %collective-permute-start.9 = (bf16[2,128,256]{2,1,0:T(8,128)(2,1)S(1)}, bf16[2,128,256]{2,1,0:T(8,128)(2,1)S(1)}, u32[]{:S(2)}, u32[]{:S(2)}) collective-permute-start(bf16[2,128,256]{2,1,0:T(8,128)(2,1)S(1)} %get-tuple-element.21), channel_id=1, source_target_pairs={{0,16},{2,18},{4,20},{6,22},{8,24},{10,26},{12,28},{1,17},{3,19},{... | collective-permute-start | bytes 393224 | tf_op jit(solution)/shard_map/ppermute | solution.py:165
  8.2 1.3 %collective-permute-start.1 = (bf16[2,128,512]{2,1,0:T(8,128)(2,1)S(1)}, bf16[2,128,512]{2,1,0:T(8,128)(2,1)S(1)}, u32[]{:S(2)}, u32[]{:S(2)}) collective-permute-start(bf16[2,128,512]{2,1,0:T(8,128)(2,1)S(1)} %copy-done.5), channel_id=1, source_target_pairs={{12,14},{16,18},{20,22},{24,26},{28,30},{13,15},{17,19},{21,23},{2... | collective-permute-start | bytes 786440 | tf_op jit(solution)/shard_map/ppermute | solution.py:165
  9.5 2.8 %collective-permute-done.5.f = bf16[2,128,256]{2,1,0:T(8,128)(2,1)S(1)} collective-permute-done((bf16[2,128,256]{2,1,0:T(8,128)(2,1)S(1)}, bf16[2,128,256]{2,1,0:T(8,128)(2,1)S(1)}, u32[]{:S(2)}, u32[]{:S(2)}) %collective-permute-start.5) | collective-permute-done | bytes 131104 | tf_op jit(solution)/shard_map/ppermute | solution.py:165
  12.3 9.7 %collective-permute-start.6 = (bf16[2,128,256]{2,1,0:T(8,128)(2,1)S(1)}, bf16[2,128,256]{2,1,0:T(8,128)(2,1)S(1)}, u32[]{:S(2)}, u32[]{:S(2)}) collective-permute-start(bf16[2,128,256]{2,1,0:T(8,128)(2,1)S(1)} %collective-permute-done.5.f), channel_id=1, source_target_pairs={{16,20},{18,22},{20,24},{22,26},{24,28},{26,30},{17,21},{19,23},{2... | collective-permute-start | bytes 393224 | tf_op jit(solution)/shard_map/ppermute | solution.py:165
  22.0 1.3 %collective-permute-start.7 = (bf16[2,128,256]{2,1,0:T(8,128)(2,1)S(1)}, bf16[2,128,256]{2,1,0:T(8,128)(2,1)S(1)}, u32[]{:S(2)}, u32[]{:S(2)}) collective-permute-start(bf16[2,128,256]{2,1,0:T(8,128)(2,1)S(1)} %collective-permute-done.5.f), channel_id=1, source_target_pairs={{16,18},{20,22},{24,26},{28,30},{17,19},{21,23},{25,27},{29,31}} | collective-permute-start | bytes 393224 | tf_op jit(solution)/shard_map/ppermute | solution.py:165
  23.4 3.9 %collective-permute-start.2 = (bf16[2,128,512]{2,1,0:T(8,128)(2,1)S(1)}, bf16[2,128,512]{2,1,0:T(8,128)(2,1)S(1)}, u32[]{:S(2)}, u32[]{:S(2)}) collective-permute-start(bf16[2,128,512]{2,1,0:T(8,128)(2,1)S(1)} %collective-permute-done.n2), channel_id=1, source_target_pairs={{18,16},{22,20},{26,24},{30,28},{19,17},{23,21},{27,25},{31,29}} | collective-permute-start | bytes 786440 | tf_op jit(solution)/shard_map/ppermute | solution.py:165
  27.3 0.7 %collective-permute-start.4 = (bf16[2,128,512]{2,1,0:T(8,128)(2,1)S(1)}, bf16[2,128,512]{2,1,0:T(8,128)(2,1)S(1)}, u32[]{:S(2)}, u32[]{:S(2)}) collective-permute-start(bf16[2,128,512]{2,1,0:T(8,128)(2,1)S(1)} %collective-permute-done.3.w), channel_id=1, source_target_pairs={{18,16},{19,17}} | collective-permute-start | bytes 786440 | tf_op jit(solution)/shard_map/ppermute | solution.py:165
  28.0 1.9 %collective-permute-start.10 = (bf16[2,128,256]{2,1,0:T(8,128)(2,1)S(1)}, bf16[2,128,256]{2,1,0:T(8,128)(2,1)S(1)}, u32[]{:S(2)}, u32[]{:S(2)}) collective-permute-start(bf16[2,128,256]{2,1,0:T(8,128)(2,1)S(1)} %collective-permute-done.9.f), channel_id=1, source_target_pairs={{16,20},{18,22},{20,24},{22,26},{24,28},{26,30},{17,21},{19,23},{2... | collective-permute-start | bytes 393224 | tf_op jit(solution)/shard_map/ppermute | solution.py:165
  30.0 3.7 %collective-permute-start.8 = (bf16[2,128,256]{2,1,0:T(8,128)(2,1)S(1)}, bf16[2,128,256]{2,1,0:T(8,128)(2,1)S(1)}, u32[]{:S(2)}, u32[]{:S(2)}) collective-permute-start(bf16[2,128,256]{2,1,0:T(8,128)(2,1)S(1)} %collective-permute-done.6.h), channel_id=1, source_target_pairs={{22,20},{26,24},{30,28},{23,21},{27,25},{31,29}} | collective-permute-start | bytes 393224 | tf_op jit(solution)/shard_map/ppermute | solution.py:165
  33.7 1.3 %collective-permute-start.11 = (bf16[2,128,256]{2,1,0:T(8,128)(2,1)S(1)}, bf16[2,128,256]{2,1,0:T(8,128)(2,1)S(1)}, u32[]{:S(2)}, u32[]{:S(2)}) collective-permute-start(bf16[2,128,256]{2,1,0:T(8,128)(2,1)S(1)} %collective-permute-done.9.f), channel_id=1, source_target_pairs={{16,18},{20,22},{24,26},{28,30},{17,19},{21,23},{25,27},{29,31}} | collective-permute-start | bytes 393224 | tf_op jit(solution)/shard_map/ppermute | solution.py:165
  35.1 3.0 %collective-permute-start.12 = (bf16[2,128,256]{2,1,0:T(8,128)(2,1)S(1)}, bf16[2,128,256]{2,1,0:T(8,128)(2,1)S(1)}, u32[]{:S(2)}, u32[]{:S(2)}) collective-permute-start(bf16[2,128,256]{2,1,0:T(8,128)(2,1)S(1)} %collective-permute-done.10.h), channel_id=1, source_target_pairs={{22,20},{26,24},{30,28},{23,21},{27,25},{31,29}} | collective-permute-start | bytes 393224 | tf_op jit(solution)/shard_map/ppermute | solution.py:165
  38.1 0.7 %copy-done.16 = s32[16,4]{0,1:T(4,128)S(1)} copy-done((s32[16,4]{0,1:T(4,128)S(1)}, s32[16,4]{0,1:T(4,128)}, u32[]{:S(2)}) %copy-start.16) | copy-done | bytes 280
  38.8 0.7 %copy.7.plan_ref = s32[16,4]{1,0:T(8,128)} copy(s32[16,4]{0,1:T(4,128)S(1)} %copy-done.16) | data formatting | bytes 512 | tf_op args[4]
  40.0 4.0 %local.1 = (f32[4,128,512]{2,1,0:T(8,128)}, f32[4,2,512]{2,1,0:T(2,128)}, s32[3]{0:T(128)}) custom-call(s32[2]{0:T(128)} %pad_add_fusion.idx_ref, s32[16,4]{1,0:T(8,128)} %copy.7.plan_ref, bf16[128,2048]{1,0:T(8,128)(2,1)} %q_ref.5, bf16[128,512]{1,0:T(8,128)(2,1)} %k_ref.1, bf16[128,512]{1,0:T(8,128)(2,1)} %v_ref.1, bf16[2,128,512]{2,1,0:T(8,128)(2,1)} %held_ref.1), custom_call_target="tpu_custom_call" | custom-call | tf_op jit(solution)/shard_map/local/pallas_call | solution.py:174
  45.0 4.4 %final.2 = (bf16[64,1024]{1,0:T(8,128)(2,1)}, bf16[64,1024]{1,0:T(8,128)(2,1)}, f32[8,128]{1,0:T(8,128)}) custom-call(s32[2]{0:T(128)} %pad_add_fusion.idx_ref, s32[3]{0:T(128)} %get-tuple-element.11.meta_ref, bf16[128,2048]{1,0:T(8,128)(2,1)} %q_ref.5, f32[4,128,512]{2,1,0:T(8,128)} %get-tuple-element.12.acc_ref, f32[4,2,512]{2,1,0:T(2,128)} %get-tuple-element.13.stat_ref, ...), custom_call_target="tpu_custom_call" | custom-call | tf_op jit(solution)/shard_map/final/pallas_call | solution.py:195
  49.5 1.3 %collective-permute-start.13 = (bf16[64,1024]{1,0:T(8,128)(2,1)}, bf16[64,1024]{1,0:T(8,128)(2,1)S(1)}, u32[]{:S(2)}, u32[]{:S(2)}) collective-permute-start(bf16[64,1024]{1,0:T(8,128)(2,1)} %get-tuple-element.16), channel_id=1, source_target_pairs={{0,1},{1,0},{2,3},{3,2},{4,5},{5,4},{6,7},{7,6},{8,9},{9,8},{10,11... | collective-permute-start | bytes 393224 | tf_op jit(solution)/shard_map/ppermute | solution.py:222
  52.1 4.4 %final.3 = (bf16[64,1024]{1,0:T(8,128)(2,1)}, bf16[64,1024]{1,0:T(8,128)(2,1)}, f32[8,128]{1,0:T(8,128)}) custom-call(s32[2]{0:T(128)} %pad_add_fusion.idx_ref, s32[3]{0:T(128)} %get-tuple-element.11.meta_ref, bf16[128,2048]{1,0:T(8,128)(2,1)} %q_ref.5, f32[4,128,512]{2,1,0:T(8,128)} %get-tuple-element.12.acc_ref, f32[4,2,512]{2,1,0:T(2,128)} %get-tuple-element.13.stat_ref, ...), custom_call_target="tpu_custom_call" | custom-call | tf_op jit(solution)/shard_map/final/pallas_call | solution.py:195
  57.2 1.3 %pad_maximum_fusion = f32[16,128]{1,0:T(8,128)} fusion(f32[8,128]{1,0:T(8,128)} %get-tuple-element.19, f32[8,128]{1,0:T(8,128)S(1)} %copy-done.15), kind=kLoop, calls=%fused_computation.1 | loop fusion | flops 2048 | bytes 16384 | tf_op jit(solution)/shard_map/concatenate | solution.py:231
  58.5 3.7 %collective-permute-done.14 = bf16[64,1024]{1,0:T(8,128)(2,1)S(1)} collective-permute-done((bf16[64,1024]{1,0:T(8,128)(2,1)}, bf16[64,1024]{1,0:T(8,128)(2,1)S(1)}, u32[]{:S(2)}, u32[]{:S(2)}) %collective-permute-start.14) | collective-permute-done | bytes 131104 | tf_op jit(solution)/shard_map/ppermute | solution.py:222
  62.2 1.9 %maximum_select_fusion = bf16[64,4096]{1,0:T(8,128)(2,1)} fusion(bf16[64,1024]{1,0:T(8,128)(2,1)S(1)} %collective-permute-done.14, bf16[64,1024]{1,0:T(8,128)(2,1)S(1)} %collective-permute-done.13, bf16[64,1024]{1,0:T(8,128)(2,1)} %get-tuple-element.15, bf16[64,1024]{1,0:T(8,128)(2,1)S(1)} %copy-done.14, pred[]{:T(512)S(6)} %eq.3), kind=kLoop, calls=%fused_computation | loop fusion | flops 4456448 | bytes 1048577 | tf_op jit(solution)/shard_map/jit(_where)/select_n | solution.py:226
  (48 shorter events, 3.5 us)
Async XLA Ops:
  0.6 22.7 %collective-permute-start = (bf16[2,128,512]{2,1,0:T(8,128)(2,1)}, bf16[2,128,512]{2,1,0:T(8,128)(2,1)S(1)}, u32[]{:S(2)}, u32[]{:S(2)}) collective-permute-start(bf16[2,128,512]{2,1,0:T(8,128)(2,1)} %held_ref.1), channel_id=1, source_target_pairs={{12,16},{14,18},{16,20},{18,22},{20,24},{22,26},{24,28},{26,30},{1... | collective-permute-start | bytes 786440 | tf_op jit(solution)/shard_map/ppermute | solution.py:165
  4.0 23.3 %collective-permute-start.3 = (bf16[2,128,512]{2,1,0:T(8,128)(2,1)}, bf16[2,128,512]{2,1,0:T(8,128)(2,1)S(1)}, u32[]{:S(2)}, u32[]{:S(2)}) collective-permute-start(bf16[2,128,512]{2,1,0:T(8,128)(2,1)} %held_ref.1), channel_id=1, source_target_pairs={{28,16},{30,18},{29,17},{31,19}} | collective-permute-start | bytes 786440 | tf_op jit(solution)/shard_map/ppermute | solution.py:165
  5.6 6.7 %collective-permute-start.5 = (bf16[2,128,256]{2,1,0:T(8,128)(2,1)S(1)}, bf16[2,128,256]{2,1,0:T(8,128)(2,1)S(1)}, u32[]{:S(2)}, u32[]{:S(2)}) collective-permute-start(bf16[2,128,256]{2,1,0:T(8,128)(2,1)S(1)} %get-tuple-element.20), channel_id=1, source_target_pairs={{0,16},{2,18},{4,20},{6,22},{8,24},{10,26},{12,28},{1,17},{3,19},{... | collective-permute-start | bytes 393224 | tf_op jit(solution)/shard_map/ppermute | solution.py:165
  6.9 15.1 %collective-permute-start.9 = (bf16[2,128,256]{2,1,0:T(8,128)(2,1)S(1)}, bf16[2,128,256]{2,1,0:T(8,128)(2,1)S(1)}, u32[]{:S(2)}, u32[]{:S(2)}) collective-permute-start(bf16[2,128,256]{2,1,0:T(8,128)(2,1)S(1)} %get-tuple-element.21), channel_id=1, source_target_pairs={{0,16},{2,18},{4,20},{6,22},{8,24},{10,26},{12,28},{1,17},{3,19},{... | collective-permute-start | bytes 393224 | tf_op jit(solution)/shard_map/ppermute | solution.py:165
  8.2 25.5 %collective-permute-start.1 = (bf16[2,128,512]{2,1,0:T(8,128)(2,1)S(1)}, bf16[2,128,512]{2,1,0:T(8,128)(2,1)S(1)}, u32[]{:S(2)}, u32[]{:S(2)}) collective-permute-start(bf16[2,128,512]{2,1,0:T(8,128)(2,1)S(1)} %copy-done.5), channel_id=1, source_target_pairs={{12,14},{16,18},{20,22},{24,26},{28,30},{13,15},{17,19},{21,23},{2... | collective-permute-start | bytes 786440 | tf_op jit(solution)/shard_map/ppermute | solution.py:165
  12.3 31.8 %copy-start.7 = (bf16[2,128,256]{2,1,0:T(8,128)(2,1)}, bf16[2,128,256]{2,1,0:T(8,128)(2,1)S(1)}, u32[]{:S(2)}) copy-start(bf16[2,128,256]{2,1,0:T(8,128)(2,1)S(1)} %collective-permute-done.5.f) | copy-start | bytes 393220
  12.3 15.6 %collective-permute-start.6 = (bf16[2,128,256]{2,1,0:T(8,128)(2,1)S(1)}, bf16[2,128,256]{2,1,0:T(8,128)(2,1)S(1)}, u32[]{:S(2)}, u32[]{:S(2)}) collective-permute-start(bf16[2,128,256]{2,1,0:T(8,128)(2,1)S(1)} %collective-permute-done.5.f), channel_id=1, source_target_pairs={{16,20},{18,22},{20,24},{22,26},{24,28},{26,30},{17,21},{19,23},{2... | collective-permute-start | bytes 393224 | tf_op jit(solution)/shard_map/ppermute | solution.py:165
  22.0 22.1 %copy-start.6 = (bf16[2,128,256]{2,1,0:T(8,128)(2,1)}, bf16[2,128,256]{2,1,0:T(8,128)(2,1)S(1)}, u32[]{:S(2)}) copy-start(bf16[2,128,256]{2,1,0:T(8,128)(2,1)S(1)} %collective-permute-done.9.f) | copy-start | bytes 393220
  22.0 7.9 %collective-permute-start.7 = (bf16[2,128,256]{2,1,0:T(8,128)(2,1)S(1)}, bf16[2,128,256]{2,1,0:T(8,128)(2,1)S(1)}, u32[]{:S(2)}, u32[]{:S(2)}) collective-permute-start(bf16[2,128,256]{2,1,0:T(8,128)(2,1)S(1)} %collective-permute-done.5.f), channel_id=1, source_target_pairs={{16,18},{20,22},{24,26},{28,30},{17,19},{21,23},{25,27},{29,31}} | collective-permute-start | bytes 393224 | tf_op jit(solution)/shard_map/ppermute | solution.py:165
  23.4 20.8 %copy-start = (bf16[2,128,512]{2,1,0:T(8,128)(2,1)}, bf16[2,128,512]{2,1,0:T(8,128)(2,1)S(1)}, u32[]{:S(2)}) copy-start(bf16[2,128,512]{2,1,0:T(8,128)(2,1)S(1)} %collective-permute-done.n2) | copy-start | bytes 786436
  23.4 20.8 %collective-permute-start.2 = (bf16[2,128,512]{2,1,0:T(8,128)(2,1)S(1)}, bf16[2,128,512]{2,1,0:T(8,128)(2,1)S(1)}, u32[]{:S(2)}, u32[]{:S(2)}) collective-permute-start(bf16[2,128,512]{2,1,0:T(8,128)(2,1)S(1)} %collective-permute-done.n2), channel_id=1, source_target_pairs={{18,16},{22,20},{26,24},{30,28},{19,17},{23,21},{27,25},{31,29}} | collective-permute-start | bytes 786440 | tf_op jit(solution)/shard_map/ppermute | solution.py:165
  27.3 16.8 %copy-start.1 = (bf16[2,128,512]{2,1,0:T(8,128)(2,1)}, bf16[2,128,512]{2,1,0:T(8,128)(2,1)S(1)}, u32[]{:S(2)}) copy-start(bf16[2,128,512]{2,1,0:T(8,128)(2,1)S(1)} %collective-permute-done.3.w) | copy-start | bytes 786436
  27.3 16.9 %collective-permute-start.4 = (bf16[2,128,512]{2,1,0:T(8,128)(2,1)S(1)}, bf16[2,128,512]{2,1,0:T(8,128)(2,1)S(1)}, u32[]{:S(2)}, u32[]{:S(2)}) collective-permute-start(bf16[2,128,512]{2,1,0:T(8,128)(2,1)S(1)} %collective-permute-done.3.w), channel_id=1, source_target_pairs={{18,16},{19,17}} | collective-permute-start | bytes 786440 | tf_op jit(solution)/shard_map/ppermute | solution.py:165
  28.0 16.1 %copy-start.8 = (bf16[2,128,256]{2,1,0:T(8,128)(2,1)}, bf16[2,128,256]{2,1,0:T(8,128)(2,1)S(1)}, u32[]{:S(2)}) copy-start(bf16[2,128,256]{2,1,0:T(8,128)(2,1)S(1)} %collective-permute-done.6.h) | copy-start | bytes 393220
  28.0 7.1 %collective-permute-start.10 = (bf16[2,128,256]{2,1,0:T(8,128)(2,1)S(1)}, bf16[2,128,256]{2,1,0:T(8,128)(2,1)S(1)}, u32[]{:S(2)}, u32[]{:S(2)}) collective-permute-start(bf16[2,128,256]{2,1,0:T(8,128)(2,1)S(1)} %collective-permute-done.9.f), channel_id=1, source_target_pairs={{16,20},{18,22},{20,24},{22,26},{24,28},{26,30},{17,21},{19,23},{2... | collective-permute-start | bytes 393224 | tf_op jit(solution)/shard_map/ppermute | solution.py:165
  29.9 14.2 %copy-start.10 = (bf16[2,128,256]{2,1,0:T(8,128)(2,1)}, bf16[2,128,256]{2,1,0:T(8,128)(2,1)S(1)}, u32[]{:S(2)}) copy-start(bf16[2,128,256]{2,1,0:T(8,128)(2,1)S(1)} %collective-permute-done.7.sf) | copy-start | bytes 393220
  30.0 14.2 %collective-permute-start.8 = (bf16[2,128,256]{2,1,0:T(8,128)(2,1)S(1)}, bf16[2,128,256]{2,1,0:T(8,128)(2,1)S(1)}, u32[]{:S(2)}, u32[]{:S(2)}) collective-permute-start(bf16[2,128,256]{2,1,0:T(8,128)(2,1)S(1)} %collective-permute-done.6.h), channel_id=1, source_target_pairs={{22,20},{26,24},{30,28},{23,21},{27,25},{31,29}} | collective-permute-start | bytes 393224 | tf_op jit(solution)/shard_map/ppermute | solution.py:165
  33.7 10.4 %copy-start.2 = (bf16[2,128,512]{2,1,0:T(8,128)(2,1)}, bf16[2,128,512]{2,1,0:T(8,128)(2,1)S(1)}, u32[]{:S(2)}) copy-start(bf16[2,128,512]{2,1,0:T(8,128)(2,1)S(1)} %collective-permute-done.1.sx) | copy-start | bytes 786436
  33.7 17.1 %collective-permute-start.11 = (bf16[2,128,256]{2,1,0:T(8,128)(2,1)S(1)}, bf16[2,128,256]{2,1,0:T(8,128)(2,1)S(1)}, u32[]{:S(2)}, u32[]{:S(2)}) collective-permute-start(bf16[2,128,256]{2,1,0:T(8,128)(2,1)S(1)} %collective-permute-done.9.f), channel_id=1, source_target_pairs={{16,18},{20,22},{24,26},{28,30},{17,19},{21,23},{25,27},{29,31}} | collective-permute-start | bytes 393224 | tf_op jit(solution)/shard_map/ppermute | solution.py:165
  35.1 9.1 %copy-start.9 = (bf16[2,128,256]{2,1,0:T(8,128)(2,1)}, bf16[2,128,256]{2,1,0:T(8,128)(2,1)S(1)}, u32[]{:S(2)}) copy-start(bf16[2,128,256]{2,1,0:T(8,128)(2,1)S(1)} %collective-permute-done.10.h) | copy-start | bytes 393220
  35.1 15.7 %collective-permute-start.12 = (bf16[2,128,256]{2,1,0:T(8,128)(2,1)S(1)}, bf16[2,128,256]{2,1,0:T(8,128)(2,1)S(1)}, u32[]{:S(2)}, u32[]{:S(2)}) collective-permute-start(bf16[2,128,256]{2,1,0:T(8,128)(2,1)S(1)} %collective-permute-done.10.h), channel_id=1, source_target_pairs={{22,20},{26,24},{30,28},{23,21},{27,25},{31,29}} | collective-permute-start | bytes 393224 | tf_op jit(solution)/shard_map/ppermute | solution.py:165
  49.5 12.7 %copy-start.14 = (bf16[64,1024]{1,0:T(8,128)(2,1)S(1)}, bf16[64,1024]{1,0:T(8,128)(2,1)}, u32[]{:S(2)}) copy-start(bf16[64,1024]{1,0:T(8,128)(2,1)} %get-tuple-element.14) | copy-start | bytes 393220
  49.5 9.0 %collective-permute-start.13 = (bf16[64,1024]{1,0:T(8,128)(2,1)}, bf16[64,1024]{1,0:T(8,128)(2,1)S(1)}, u32[]{:S(2)}, u32[]{:S(2)}) collective-permute-start(bf16[64,1024]{1,0:T(8,128)(2,1)} %get-tuple-element.16), channel_id=1, source_target_pairs={{0,1},{1,0},{2,3},{3,2},{4,5},{5,4},{6,7},{7,6},{8,9},{9,8},{10,11... | collective-permute-start | bytes 393224 | tf_op jit(solution)/shard_map/ppermute | solution.py:222
  56.5 5.7 %collective-permute-start.14 = (bf16[64,1024]{1,0:T(8,128)(2,1)}, bf16[64,1024]{1,0:T(8,128)(2,1)S(1)}, u32[]{:S(2)}, u32[]{:S(2)}) collective-permute-start(bf16[64,1024]{1,0:T(8,128)(2,1)} %get-tuple-element.17), channel_id=1, source_target_pairs={{0,1},{1,0},{2,3},{3,2},{4,5},{5,4},{6,7},{7,6},{8,9},{9,8},{10,11... | collective-permute-start | bytes 393224 | tf_op jit(solution)/shard_map/ppermute | solution.py:222
  (8 other events, 12.5 us)

commit v2 on v1

v2 whole, which is shorter than its diff:
```python
import functools
import math

import jax
import jax.numpy as jnp
from jax import lax
from jax.experimental import pallas as pl
from jax.experimental.pallas import tpu as pltpu
from jax.sharding import PartitionSpec as P

HD = 128
QB = 4
STEPS = 3
CHUNKS = ((0, 4),)
SCALE = 1.0 / math.sqrt(HD)
LN2 = math.log(2.0)
FACTOR = SCALE / LN2
NEG = -math.inf

SMEM = pl.BlockSpec(memory_space=pltpu.SMEM)
VMEM = pl.BlockSpec(memory_space=pltpu.VMEM)
PARAMS = pltpu.CompilerParams(vmem_limit_bytes=16 * 2**20)
COST = pl.CostEstimate(flops=1000, bytes_accessed=1000, transcendentals=0)
ANY = pl.BlockSpec(memory_space=pl.ANY)


def stacked(q_ref, kv_head, group):
    first = kv_head * group
    return jnp.concatenate(
        [q_ref[:, (first + j) * HD : (first + j + 1) * HD] for j in range(group)], axis=0
    )


def scores_of(keys, queries):
    return lax.dot_general(
        keys, queries, (((1,), (1,)), ((), ())), preferred_element_type=jnp.float32
    )


def mix(values, weights):
    return lax.dot_general(
        values,
        weights,
        (((0,), (0,)), ((), ())),
        preferred_element_type=jnp.float32,
    )


def local_kernel(half, entries, idx_ref, plan_ref, q_ref, k_ref, v_ref, held_ref, acc_ref, stat_ref, meta_ref):
    rows = q_ref.shape[0]
    kv_heads = k_ref.shape[1] // HD
    group = q_ref.shape[1] // k_ref.shape[1]
    device = idx_ref[0]
    for t in range(STEPS):
        meta_ref[t] = -1

    def scan(i, carry):
        @pl.when(plan_ref[i, 2] == device)
        def _():
            meta_ref[plan_ref[i, 0]] = plan_ref[i, 3]

        return carry

    lax.fori_loop(0, entries, scan, 0)
    held_bias = jnp.where(device >= half - 2, 0.0, NEG)
    key_pos = lax.broadcasted_iota(jnp.int32, (rows, group * rows), 0)
    row_pos = lax.broadcasted_iota(jnp.int32, (rows, group * rows), 1) % rows
    causal = key_pos <= row_pos
    for g in range(kv_heads):
        cols = slice(g * HD, (g + 1) * HD)
        queries = stacked(q_ref, g, group)
        own = jnp.where(causal, scores_of(k_ref[:, cols], queries), NEG)
        held = scores_of(held_ref[0, :, cols], queries) + held_bias
        top = jnp.maximum(
            jnp.max(own, axis=0, keepdims=True), jnp.max(held, axis=0, keepdims=True)
        )
        w_own = jnp.exp2((own - top) * FACTOR)
        w_held = jnp.exp2((held - top) * FACTOR)
        stat_ref[g, 0:1, :] = top
        stat_ref[g, 1:2, :] = jnp.sum(w_own, axis=0, keepdims=True) + jnp.sum(
            w_held, axis=0, keepdims=True
        )
        acc_ref[g] = mix(v_ref[:, cols], w_own.astype(jnp.bfloat16)) + mix(
            held_ref[1, :, cols], w_held.astype(jnp.bfloat16)
        )


def near_kernel(
    half, first, count,
    idx_ref, q_ref, acc_ref, stat_ref,
    n2, sx, sn2, f, sf,
    base_ref, log_ref, sub_ref,
    kv,
):
    rows = q_ref.shape[0]
    group = QB
    device = idx_ref[0]
    even = device % 2 == 0
    odd = jnp.logical_not(even)
    corner = device <= half + 1
    inner = jnp.logical_not(corner)
    pick = functools.partial(bring, kv, first, count)
    pick(0, sx, odd, True)
    pick(0, sf, even & corner, False)
    pick(0, sn2, even & inner, True)
    pick(1, f, corner, False)
    pick(1, n2, inner, True)
    first_key = lax.broadcasted_iota(jnp.int32, (2 * rows, 1), 0) < rows
    bias = jnp.where(
        first_key,
        jnp.where(device >= half - 1, 0.0, NEG),
        jnp.where(device >= half, 0.0, NEG),
    )
    sub = rows // QB
    for g in range(count):
        cols = slice(g * HD, (g + 1) * HD)
        queries = stacked(q_ref, first + g, group)
        scores = scores_of(kv[0, :, cols], queries) + bias
        old_top = stat_ref[first + g, 0:1, :]
        top = jnp.maximum(old_top, jnp.max(scores, axis=0, keepdims=True))
        keep = jnp.exp2((old_top - top) * FACTOR)
        weights = jnp.exp2((scores - top) * FACTOR)
        total = stat_ref[first + g, 1:2, :] * keep + jnp.sum(weights, axis=0, keepdims=True)
        inverse = 1.0 / total
        mixed = acc_ref[first + g] * (keep * inverse) + mix(
            kv[1, :, cols], (weights * inverse).astype(jnp.bfloat16)
        )
        logs = top * FACTOR + jnp.log2(total)
        for j in range(group):
            lanes = slice(j * rows, (j + 1) * rows)
            at = slice((g * group + j) * HD, (g * group + j + 1) * HD)
            base_ref[:, at] = jnp.transpose(mixed[:, lanes]).astype(jnp.bfloat16)
            log_ref[g * group + j : g * group + j + 1, :] = logs[:, lanes]
        for c in range(QB):
            part = [logs[:, j * rows + c * sub : j * rows + (c + 1) * sub] for j in range(group)]
            sub_ref[c * count + g : c * count + g + 1, :] = jnp.concatenate(part, axis=1)


def bring(kv, first, count, slot, source, when, whole):
    @pl.when(when)
    def _():
        rows = source.shape[1]
        at = slice(slot * rows, (slot + 1) * rows)
        if whole:
            kv[:, at, :] = source[:, :, first * HD : (first + count) * HD]
        else:
            kv[:, at, :] = source[...]


def far_kernel(
    half, first, count,
    idx_ref, meta_ref, q_ref, base_ref, sub_ref,
    n2, sn2, f, h, sf, sh,
    mine_ref, send_ref, new_ref,
    kv,
):
    rows = q_ref.shape[0]
    sub = rows // QB
    group = QB
    device = idx_ref[0]
    head = idx_ref[1]
    step_a = jnp.where(meta_ref[0] >= 0, 0, 1)
    step_b = jnp.where(meta_ref[2] >= 0, 2, 1)
    owner = device >= half

    @pl.when(owner)
    def _():
        even = device % 2 == 0
        odd = jnp.logical_not(even)
        corner = device <= half + 1
        inner = jnp.logical_not(corner)
        pick = functools.partial(bring, kv, first, count)
        pick(0, h, step_a == 0, False)
        pick(1, n2, (step_b == 2) & corner, True)
        pick(1, f, (step_b == 2) & inner, False)
        for slot, step in ((0, step_a), (1, step_b)):
            pick(slot, sh, (step == 1) & odd, False)
            pick(slot, sn2, (step == 1) & even & corner, True)
            pick(slot, sf, (step == 1) & even & inner, False)

    def half_rows(which):
        return pl.ds(pl.multiple_of(which * (rows // 2), rows // 2), rows // 2)

    mine_ref[...] = base_ref[half_rows(head), :]
    send_ref[...] = base_ref[half_rows(1 - head), :]

    @pl.when(owner)
    def _():
        chosen = [meta_ref[step_a], meta_ref[step_b]]
        at_rows = [pl.ds(pl.multiple_of(c * sub, sub), sub) for c in chosen]
        lanes = group * sub
        first_key = lax.broadcasted_iota(jnp.int32, (2 * rows, 2 * lanes), 0) < rows
        first_row = lax.broadcasted_iota(jnp.int32, (2 * rows, 2 * lanes), 1) < lanes
        bias = jnp.where(first_key == first_row, 0.0, jnp.where(chosen[0] == chosen[1], 0.0, NEG))
        results = []
        for g in range(count):
            cols = slice(g * HD, (g + 1) * HD)
            names = range(g * group, (g + 1) * group)

            def rows_of(ref, skip):
                parts = [ref[at, (skip + j) * HD : (skip + j + 1) * HD] for at in at_rows for j in names]
                return jnp.concatenate(parts, axis=0)

            scores = scores_of(kv[0, :, cols], rows_of(q_ref, first * group)) * FACTOR + bias
            old_log = jnp.concatenate([sub_ref[pl.ds(c * count + g, 1), :] for c in chosen], axis=1)
            top = jnp.maximum(old_log, jnp.max(scores, axis=0, keepdims=True))
            weights = jnp.exp2(scores - top)
            keep = jnp.exp2(old_log - top)
            total = keep + jnp.sum(weights, axis=0, keepdims=True)
            inverse = 1.0 / total
            share = jnp.transpose(jnp.broadcast_to(keep * inverse, (8, 2 * lanes)))[:, 0:1]
            final = mix((weights * inverse).astype(jnp.bfloat16), kv[1, :, cols]) + rows_of(base_ref, 0).astype(jnp.float32) * share
            new_log = top + jnp.log2(total)
            for slot in range(2):
                new_ref[slot * count + g : slot * count + g + 1, :] = new_log[:, slot * lanes : (slot + 1) * lanes]
                part = final[slot * lanes : (slot + 1) * lanes].astype(jnp.bfloat16)
                results.append((chosen[slot], names, part))
        for chosen, names, final in results:
            at_half = pl.ds(pl.multiple_of(chosen % (QB // 2) * sub, sub), sub)
            for target, here in ((mine_ref, True), (send_ref, False)):

                @pl.when((chosen // (QB // 2) == head) == here)
                def _():
                    for i, j in enumerate(names):
                        target[at_half, j * HD : (j + 1) * HD] = final[i * sub : (i + 1) * sub]


def log_kernel(chunks, meta_ref, *refs):
    n = len(chunks)
    logs, news, log_ref = refs[:n], refs[n : 2 * n], refs[2 * n]
    rows = log_ref.shape[1]
    sub = rows // QB
    step_a = jnp.where(meta_ref[0] >= 0, 0, 1)
    step_b = jnp.where(meta_ref[2] >= 0, 2, 1)
    row_sub = lax.broadcasted_iota(jnp.int32, (1, rows), 1) // sub
    for log, new, (first, count) in zip(logs, news, chunks):
        heads = log.shape[0]
        group = heads // count
        for j in range(heads):
            result = log[j : j + 1, :]
            for slot, step in ((0, step_a), (1, step_b)):
                chosen = meta_ref[step]
                at = slot * count + j // group
                moved = pltpu.roll(new[at : at + 1, :], (chosen + QB - j % group) % QB * sub, 1)
                result = jnp.where(row_sub == chosen, moved, result)
            log_ref[first * group + j : first * group + j + 1, :] = result * LN2


def shards(query, key, value, held_kv, plan):
    rows = query.shape[0]
    kv_heads = key.shape[1] // HD
    group = query.shape[1] // key.shape[1]
    size = lax.axis_size("ctx")
    half = size // 2
    device = lax.axis_index("ctx")
    head = lax.axis_index("head")
    idx = jnp.stack([device, head]).astype(jnp.int32)

    def send(x, route):
        return lax.ppermute(x, "ctx", route)

    swap = [(i, i ^ 1) for i in range(size)]
    onward = swap[:half] + [(i, half + (i - half + 2) % half) for i in range(half, size)]
    back = [(j, i) for i, j in onward]
    across = [(i, half + (i + 2) % half) for i in range(half)]
    across += [(j, i) for i, j in across]

    parts = [held_kv[:, :, a * HD : (a + n) * HD] for a, n in CHUNKS]
    n2 = send(held_kv, onward)
    sx = send(held_kv, swap)
    fs = [send(part, across) for part in parts]

    acc, stat, meta = pl.pallas_call(
        functools.partial(local_kernel, half, plan.shape[0]),
        out_shape=(
            jax.ShapeDtypeStruct((kv_heads, HD, group * rows), jnp.float32),
            jax.ShapeDtypeStruct((kv_heads, 2, group * rows), jnp.float32),
            jax.ShapeDtypeStruct((STEPS,), jnp.int32),
        ),
        in_specs=[SMEM, SMEM, VMEM, VMEM, VMEM, VMEM],
        out_specs=(VMEM, VMEM, SMEM),
        compiler_params=PARAMS,
        cost_estimate=COST,
        name="local",
    )(idx, plan, query, key, value, held_kv)

    fs, n2, acc, stat, meta = lax.optimization_barrier((fs, n2, acc, stat, meta))
    sn2 = send(n2, swap)

    def near(first, count, f, sf):
        wide = count * group * HD
        return pl.pallas_call(
            functools.partial(near_kernel, half, first, count),
            out_shape=(
                jax.ShapeDtypeStruct((rows, wide), jnp.bfloat16),
                jax.ShapeDtypeStruct((count * group, rows), jnp.float32),
                jax.ShapeDtypeStruct((QB * count, rows // QB * group), jnp.float32),
            ),
            in_specs=[SMEM] + [VMEM] * 8,
            out_specs=(VMEM,) * 3,
            scratch_shapes=[pltpu.VMEM((2, 2 * rows, count * HD), jnp.bfloat16)],
            compiler_params=PARAMS,
            cost_estimate=COST,
            name="near",
        )(idx, query, acc, stat, n2, sx, sn2, f, sf)

    def far(first, count, base, subs, f, h, sf, sh):
        wide = count * group * HD
        return pl.pallas_call(
            functools.partial(far_kernel, half, first, count),
            out_shape=(
                jax.ShapeDtypeStruct((rows // 2, wide), jnp.bfloat16),
                jax.ShapeDtypeStruct((rows // 2, wide), jnp.bfloat16),
                jax.ShapeDtypeStruct((2 * count, rows // QB * group), jnp.float32),
            ),
            in_specs=[SMEM, SMEM] + [VMEM] * 9,
            out_specs=(VMEM,) * 3,
            scratch_shapes=[pltpu.VMEM((2, 2 * rows, count * HD), jnp.bfloat16)],
            compiler_params=PARAMS,
            cost_estimate=COST,
            name="far",
        )(idx, meta, query, base, subs, n2, sn2, f, h, sf, sh)

    n = len(CHUNKS)
    sfs = [send(f, swap) for f in fs]
    hs, near_parts = [], []
    for k, (f, sf) in enumerate(zip(fs, sfs)):
        if k > 0:
            f, held_back = lax.optimization_barrier((f, near_parts[-1][0]))
            near_parts[-1] = (held_back, *near_parts[-1][1:])
        hs.append(send(f, back))
        near_parts.append(near(*CHUNKS[k], f, sf))
    hs[0], near_parts = lax.optimization_barrier((hs[0], near_parts))
    mine, news, there = [], [], []
    for k, (base, log, table) in enumerate(near_parts):
        h = hs[k]
        if k > 0:
            h, away = lax.optimization_barrier((h, away))
            there.append(lax.ppermute(away, "head", [(0, 1), (1, 0)]))
        sh = send(h, swap)
        piece, away, new = far(*CHUNKS[k], base, table, fs[k], h, sfs[k], sh)
        mine.append(piece)
        news.append(new)
    there.append(lax.ppermute(away, "head", [(0, 1), (1, 0)]))
    logs = [log for _, log, _ in near_parts]
    log_total = pl.pallas_call(
        functools.partial(log_kernel, CHUNKS),
        out_shape=jax.ShapeDtypeStruct((kv_heads * group, rows), jnp.float32),
        in_specs=[SMEM] + [VMEM] * (2 * n),
        out_specs=VMEM,
        compiler_params=PARAMS,
        cost_estimate=COST,
        name="logs",
    )(meta, *logs, *news)
    mine, there = jnp.concatenate(mine, axis=1), jnp.concatenate(there, axis=1)
    attended = jnp.where(
        head == 0,
        jnp.concatenate([mine, there], axis=1),
        jnp.concatenate([there, mine], axis=1),
    )
    return (attended, log_total)


def solution(mesh):
    return jax.shard_map(
        shards,
        mesh=mesh,
        in_specs=(
            P("ctx", "head"),
            P("ctx", "head"),
            P("ctx", "head"),
            P(None, "ctx", "head"),
            P(),
        ),
        out_specs=(P(("ctx", "head"), None), P("head", "ctx")),
        check_vma=False,
    )
```

time: 64.7 us -> 39.3 us (0.61)
  the two profiles are of different devices: /device:TPU:19 before, /device:TPU:30 now
where the time goes in v2:
time: 39.3 us; the launch traced here: 39 us
  waiting for transfers between devices  22.9 us (58%)
  Pallas kernels  8.27 us (21%)
  local copies, waits for them, and re-layouts  4.57 us (12%)
  starting transfers between devices  1.67 us (4%)
  other arithmetic  0.99 us (3%)
  between operations  0.66 us (2%)
    ppermute x7, waiting for transfers between devices, send(): return lax.ppermute(x, 'ctx', route)  16.3 us
    ppermute x1, waiting for transfers between devices, shards(): there.append(lax.ppermute(away, 'head', [(0, 1), (1, 0)]))  6.51 us
    unnamed x13, local copies, waits for them, and re-layouts  4.57 us
    pallas_call x1, Pallas kernels, shards(): pl.pallas_call(functools.partial(local_kernel, half, plan.shape[0]), out_...  2.5 us
    pallas_call x1, Pallas kernels, near(): pl.pallas_call(functools.partial(near_kernel, half, first, count), out_sh...  2.44 us
    pallas_call x1, Pallas kernels, far(): pl.pallas_call(functools.partial(far_kernel, half, first, count), out_sha...  2 us
    pallas_call x1, Pallas kernels, shards(): pl.pallas_call(functools.partial(log_kernel, CHUNKS), out_shape=jax.Shape...  1.33 us
    ppermute x7, starting transfers between devices, send(): return lax.ppermute(x, 'ctx', route)  1.1 us
  transfers between devices with their start and end apart: 8, of which 7 were waited for; matrix products, arithmetic and copies ran while one was open for 0% of the time, Pallas kernels for 16%

profile of v2, /device:TPU:30, one launch (start us, length us, event | category | flops | bytes accessed | tf_op | source)
XLA Modules:
  0.0 39.0 jit_solution(15782030989207180963)
XLA Ops:
  0.6 0.5 %collective-permute-start.1 = (bf16[2,128,512]{2,1,0:T(8,128)(2,1)}, bf16[2,128,512]{2,1,0:T(8,128)(2,1)S(1)}, u32[]{:S(2)}, u32[]{:S(2)}) collective-permute-start(bf16[2,128,512]{2,1,0:T(8,128)(2,1)} %held_ref.1), channel_id=1, source_target_pairs={{0,2},{2,0},{4,6},{6,4},{8,10},{10,8},{12,14},{14,12},{16,20},{18,... | collective-permute-start | bytes 786440 | tf_op jit(solution)/shard_map/ppermute | solution.py:260
  1.1 0.0 collective-permute-start
  1.1 0.1 collective-permute-start.3
  1.2 0.7 %copy-done.5 = s32[16,4]{0,1:T(4,128)S(1)} copy-done((s32[16,4]{0,1:T(4,128)S(1)}, s32[16,4]{0,1:T(4,128)}, u32[]{:S(2)}) %copy-start.5) | copy-done | bytes 280
  1.9 0.1 copy.7.plan_ref
  2.0 0.1 pad_add_fusion.idx_ref
  2.1 1.0 %copy-done = bf16[128,2048]{1,0:T(8,128)(2,1)S(1)} copy-done((bf16[128,2048]{1,0:T(8,128)(2,1)S(1)}, bf16[128,2048]{1,0:T(8,128)(2,1)}, u32[]{:S(2)}) %copy-start) | copy-done | bytes 524312
  3.1 0.9 %copy-done.2 = bf16[2,128,512]{2,1,0:T(8,128)(2,1)S(1)} copy-done((bf16[2,128,512]{2,1,0:T(8,128)(2,1)S(1)}, bf16[2,128,512]{2,1,0:T(8,128)(2,1)}, u32[]{:S(2)}) %copy-start.2) | copy-done | bytes 262168
  4.1 0.9 %copy-done.3 = bf16[128,512]{1,0:T(8,128)(2,1)S(1)} copy-done((bf16[128,512]{1,0:T(8,128)(2,1)S(1)}, bf16[128,512]{1,0:T(8,128)(2,1)}, u32[]{:S(2)}) %copy-start.3) | copy-done | bytes 131096
  5.0 0.9 %copy-done.4 = bf16[128,512]{1,0:T(8,128)(2,1)S(1)} copy-done((bf16[128,512]{1,0:T(8,128)(2,1)S(1)}, bf16[128,512]{1,0:T(8,128)(2,1)}, u32[]{:S(2)}) %copy-start.4) | copy-done | bytes 131096
  5.9 2.5 %local.1 = (f32[4,128,512]{2,1,0:T(8,128)S(1)}, f32[4,2,512]{2,1,0:T(2,128)S(1)}, s32[3]{0:T(128)S(1)}) custom-call(s32[2]{0:T(128)S(1)} %pad_add_fusion.idx_ref, s32[16,4]{1,0:T(8,128)S(1)} %copy.7.plan_ref, bf16[128,2048]{1,0:T(8,128)(2,1)S(1)} %copy-done, bf16[128,512]{1,0:T(8,128)(2,1)S(1)} %copy-done.3, bf16[128,512]{1,0:T(8,128)(2,1)S(1)} %copy-done.4, ...), custom_call_target="tpu_custom_call" | custom-call | flops 1000 | bytes 1000 | tf_op jit(solution)/shard_map/local/pallas_call | solution.py:273
  8.4 1.7 %collective-permute-done.1.n2 = bf16[2,128,512]{2,1,0:T(8,128)(2,1)S(1)} collective-permute-done((bf16[2,128,512]{2,1,0:T(8,128)(2,1)}, bf16[2,128,512]{2,1,0:T(8,128)(2,1)S(1)}, u32[]{:S(2)}, u32[]{:S(2)}) %collective-permute-start.1) | collective-permute-done | bytes 262176 | tf_op jit(solution)/shard_map/ppermute | solution.py:260
  10.1 6.4 %collective-permute-done.f = bf16[2,128,512]{2,1,0:T(8,128)(2,1)S(1)} collective-permute-done((bf16[2,128,512]{2,1,0:T(8,128)(2,1)}, bf16[2,128,512]{2,1,0:T(8,128)(2,1)S(1)}, u32[]{:S(2)}, u32[]{:S(2)}) %collective-permute-start) | collective-permute-done | bytes 262176 | tf_op jit(solution)/shard_map/ppermute | solution.py:260
  16.5 0.5 %collective-permute-start.5 = (bf16[2,128,512]{2,1,0:T(8,128)(2,1)S(1)}, bf16[2,128,512]{2,1,0:T(8,128)(2,1)S(1)}, u32[]{:S(2)}, u32[]{:S(2)}) collective-permute-start(bf16[2,128,512]{2,1,0:T(8,128)(2,1)S(1)} %collective-permute-done.f), channel_id=1, source_target_pairs={{0,2},{2,0},{4,6},{6,4},{8,10},{10,8},{12,14},{14,12},{16,18},{18,... | collective-permute-start | bytes 786440 | tf_op jit(solution)/shard_map/ppermute | solution.py:260
  17.0 1.0 %collective-permute-done.4.sn2 = bf16[2,128,512]{2,1,0:T(8,128)(2,1)S(1)} collective-permute-done((bf16[2,128,512]{2,1,0:T(8,128)(2,1)S(1)}, bf16[2,128,512]{2,1,0:T(8,128)(2,1)S(1)}, u32[]{:S(2)}, u32[]{:S(2)}) %collective-permute-start.4) | collective-permute-done | bytes 262176 | tf_op jit(solution)/shard_map/ppermute | solution.py:260
  18.1 0.4 collective-permute-done.5.sf
  18.4 2.4 %near.1 = (bf16[128,2048]{1,0:T(8,128)(2,1)S(1)}, f32[16,128]{1,0:T(8,128)S(1)}, f32[16,128]{1,0:T(8,128)S(1)}) custom-call(s32[2]{0:T(128)S(1)} %pad_add_fusion.idx_ref, bf16[128,2048]{1,0:T(8,128)(2,1)S(1)} %copy-done.1, f32[4,128,512]{2,1,0:T(8,128)S(1)} %get-tuple-element.25.acc_ref, f32[4,2,512]{2,1,0:T(2,128)S(1)} %get-tuple-element.26.stat_ref, ...), custom_call_target="tpu_custom_call" | custom-call | flops 1000 | bytes 1000 | tf_op jit(solution)/shard_map/near/pallas_call | solution.py:292
  20.9 5.3 %collective-permute-done.2.h = bf16[2,128,512]{2,1,0:T(8,128)(2,1)S(1)} collective-permute-done((bf16[2,128,512]{2,1,0:T(8,128)(2,1)S(1)}, bf16[2,128,512]{2,1,0:T(8,128)(2,1)S(1)}, u32[]{:S(2)}, u32[]{:S(2)}) %collective-permute-start.2) | collective-permute-done | bytes 262176 | tf_op jit(solution)/shard_map/ppermute | solution.py:260
  26.1 1.5 %collective-permute-done.6.sh = bf16[2,128,512]{2,1,0:T(8,128)(2,1)S(1)} collective-permute-done((bf16[2,128,512]{2,1,0:T(8,128)(2,1)S(1)}, bf16[2,128,512]{2,1,0:T(8,128)(2,1)S(1)}, u32[]{:S(2)}, u32[]{:S(2)}) %collective-permute-start.6) | collective-permute-done | bytes 262176 | tf_op jit(solution)/shard_map/ppermute | solution.py:260
  27.7 2.0 %far.1 = (bf16[64,2048]{1,0:T(8,128)(2,1)S(1)}, bf16[64,2048]{1,0:T(8,128)(2,1)S(1)}, f32[8,128]{1,0:T(8,128)S(1)}) custom-call(s32[2]{0:T(128)S(1)} %pad_add_fusion.idx_ref, s32[3]{0:T(128)S(1)} %get-tuple-element.23.meta_ref, bf16[128,2048]{1,0:T(8,128)(2,1)S(1)} %copy-done.1, bf16[128,2048]{1,0:T(8,128)(2,1)S(1)} %get-tuple-element.31.base_ref, ...), custom_call_target="tpu_custom_call" | custom-call | flops 1000 | bytes 1000 | tf_op jit(solution)/shard_map/far/pallas_call | solution.py:309
  29.7 0.6 %collective-permute-start.7 = (bf16[64,2048]{1,0:T(8,128)(2,1)S(1)}, bf16[64,2048]{1,0:T(8,128)(2,1)S(1)}, u32[]{:S(2)}, u32[]{:S(2)}) collective-permute-start(bf16[64,2048]{1,0:T(8,128)(2,1)S(1)} %get-tuple-element.35), channel_id=1, source_target_pairs={{0,1},{1,0},{2,3},{3,2},{4,5},{5,4},{6,7},{7,6},{8,9},{9,8},{10,11... | collective-permute-start | bytes 786440 | tf_op jit(solution)/shard_map/ppermute | solution.py:344
  30.3 1.3 %logs.1 = f32[16,128]{1,0:T(8,128)} custom-call(s32[3]{0:T(128)S(1)} %get-tuple-element.23.meta_ref, f32[16,128]{1,0:T(8,128)S(1)} %get-tuple-element.36.refs_0_, f32[8,128]{1,0:T(8,128)S(1)} %get-tuple-element.37.refs_1_), custom_call_target="tpu_custom_call" | custom-call | flops 1000 | bytes 1000 | tf_op jit(solution)/shard_map/logs/pallas_call | solution.py:346
  31.6 6.5 %collective-permute-done.7 = bf16[64,2048]{1,0:T(8,128)(2,1)S(1)} collective-permute-done((bf16[64,2048]{1,0:T(8,128)(2,1)S(1)}, bf16[64,2048]{1,0:T(8,128)(2,1)S(1)}, u32[]{:S(2)}, u32[]{:S(2)}) %collective-permute-start.7) | collective-permute-done | bytes 262176 | tf_op jit(solution)/shard_map/ppermute | solution.py:344
  38.1 0.9 %maximum_select_fusion = bf16[64,4096]{1,0:T(8,128)(2,1)} fusion(bf16[64,2048]{1,0:T(8,128)(2,1)S(1)} %collective-permute-done.7, bf16[64,2048]{1,0:T(8,128)(2,1)S(1)} %get-tuple-element.34, pred[]{:T(512)S(6)} %eq.3), kind=kLoop, calls=%fused_computation | loop fusion | flops 2359296 | bytes 1048577 | tf_op jit(solution)/shard_map/jit(_where)/select_n | solution.py:356
  (11 shorter events, 0.0 us)
Async XLA Ops:
  0.6 9.4 %collective-permute-start.1 = (bf16[2,128,512]{2,1,0:T(8,128)(2,1)}, bf16[2,128,512]{2,1,0:T(8,128)(2,1)S(1)}, u32[]{:S(2)}, u32[]{:S(2)}) collective-permute-start(bf16[2,128,512]{2,1,0:T(8,128)(2,1)} %held_ref.1), channel_id=1, source_target_pairs={{0,2},{2,0},{4,6},{6,4},{8,10},{10,8},{12,14},{14,12},{16,20},{18,... | collective-permute-start | bytes 786440 | tf_op jit(solution)/shard_map/ppermute | solution.py:260
  1.1 15.4 %collective-permute-start = (bf16[2,128,512]{2,1,0:T(8,128)(2,1)}, bf16[2,128,512]{2,1,0:T(8,128)(2,1)S(1)}, u32[]{:S(2)}, u32[]{:S(2)}) collective-permute-start(bf16[2,128,512]{2,1,0:T(8,128)(2,1)} %held_ref.1), channel_id=1, source_target_pairs={{0,20},{2,22},{4,24},{6,26},{8,28},{10,30},{12,16},{14,18},{20,0},... | collective-permute-start | bytes 786440 | tf_op jit(solution)/shard_map/ppermute | solution.py:260
  1.1 15.9 %collective-permute-start.3 = (bf16[2,128,512]{2,1,0:T(8,128)(2,1)}, bf16[2,128,512]{2,1,0:T(8,128)(2,1)S(1)}, u32[]{:S(2)}, u32[]{:S(2)}) collective-permute-start(bf16[2,128,512]{2,1,0:T(8,128)(2,1)} %held_ref.1), channel_id=1, source_target_pairs={{0,2},{2,0},{4,6},{6,4},{8,10},{10,8},{12,14},{14,12},{16,18},{18,... | collective-permute-start | bytes 786440 | tf_op jit(solution)/shard_map/ppermute | solution.py:260
  1.2 0.7 %copy-start.5 = (s32[16,4]{0,1:T(4,128)S(1)}, s32[16,4]{0,1:T(4,128)}, u32[]{:S(2)}) copy-start(s32[16,4]{0,1:T(4,128)} %param.9) | copy-start | bytes 772
  2.1 1.0 %copy-start = (bf16[128,2048]{1,0:T(8,128)(2,1)S(1)}, bf16[128,2048]{1,0:T(8,128)(2,1)}, u32[]{:S(2)}) copy-start(bf16[128,2048]{1,0:T(8,128)(2,1)} %q_ref.5) | copy-start | bytes 1572868
  3.1 0.9 %copy-start.2 = (bf16[2,128,512]{2,1,0:T(8,128)(2,1)S(1)}, bf16[2,128,512]{2,1,0:T(8,128)(2,1)}, u32[]{:S(2)}) copy-start(bf16[2,128,512]{2,1,0:T(8,128)(2,1)} %held_ref.1) | copy-start | bytes 786436
  4.1 0.9 %copy-start.3 = (bf16[128,512]{1,0:T(8,128)(2,1)S(1)}, bf16[128,512]{1,0:T(8,128)(2,1)}, u32[]{:S(2)}) copy-start(bf16[128,512]{1,0:T(8,128)(2,1)} %k_ref.1) | copy-start | bytes 393220
  5.0 0.9 %copy-start.4 = (bf16[128,512]{1,0:T(8,128)(2,1)S(1)}, bf16[128,512]{1,0:T(8,128)(2,1)}, u32[]{:S(2)}) copy-start(bf16[128,512]{1,0:T(8,128)(2,1)} %v_ref.1) | copy-start | bytes 393220
  5.9 12.6 %copy-start.1 = (bf16[128,2048]{1,0:T(8,128)(2,1)S(1)}, bf16[128,2048]{1,0:T(8,128)(2,1)}, u32[]{:S(2)}) copy-start(bf16[128,2048]{1,0:T(8,128)(2,1)} %q_ref.5) | copy-start | bytes 1572868
  16.5 1.5 %collective-permute-start.4 = (bf16[2,128,512]{2,1,0:T(8,128)(2,1)S(1)}, bf16[2,128,512]{2,1,0:T(8,128)(2,1)S(1)}, u32[]{:S(2)}, u32[]{:S(2)}) collective-permute-start(bf16[2,128,512]{2,1,0:T(8,128)(2,1)S(1)} %collective-permute-done.1.n2), channel_id=1, source_target_pairs={{0,2},{2,0},{4,6},{6,4},{8,10},{10,8},{12,14},{14,12},{16,18},{18,... | collective-permute-start | bytes 786440 | tf_op jit(solution)/shard_map/ppermute | solution.py:260
  16.5 1.9 %collective-permute-start.5 = (bf16[2,128,512]{2,1,0:T(8,128)(2,1)S(1)}, bf16[2,128,512]{2,1,0:T(8,128)(2,1)S(1)}, u32[]{:S(2)}, u32[]{:S(2)}) collective-permute-start(bf16[2,128,512]{2,1,0:T(8,128)(2,1)S(1)} %collective-permute-done.f), channel_id=1, source_target_pairs={{0,2},{2,0},{4,6},{6,4},{8,10},{10,8},{12,14},{14,12},{16,18},{18,... | collective-permute-start | bytes 786440 | tf_op jit(solution)/shard_map/ppermute | solution.py:260
  17.0 9.1 %collective-permute-start.2 = (bf16[2,128,512]{2,1,0:T(8,128)(2,1)S(1)}, bf16[2,128,512]{2,1,0:T(8,128)(2,1)S(1)}, u32[]{:S(2)}, u32[]{:S(2)}) collective-permute-start(bf16[2,128,512]{2,1,0:T(8,128)(2,1)S(1)} %collective-permute-done.f), channel_id=1, source_target_pairs={{2,0},{0,2},{6,4},{4,6},{10,8},{8,10},{14,12},{12,14},{20,16},{22,... | collective-permute-start | bytes 786440 | tf_op jit(solution)/shard_map/ppermute | solution.py:260
  26.1 1.5 %collective-permute-start.6 = (bf16[2,128,512]{2,1,0:T(8,128)(2,1)S(1)}, bf16[2,128,512]{2,1,0:T(8,128)(2,1)S(1)}, u32[]{:S(2)}, u32[]{:S(2)}) collective-permute-start(bf16[2,128,512]{2,1,0:T(8,128)(2,1)S(1)} %collective-permute-done.2.h), channel_id=1, source_target_pairs={{0,2},{2,0},{4,6},{6,4},{8,10},{10,8},{12,14},{14,12},{16,18},{18,... | collective-permute-start | bytes 786440 | tf_op jit(solution)/shard_map/ppermute | solution.py:260
  29.7 8.4 %collective-permute-start.7 = (bf16[64,2048]{1,0:T(8,128)(2,1)S(1)}, bf16[64,2048]{1,0:T(8,128)(2,1)S(1)}, u32[]{:S(2)}, u32[]{:S(2)}) collective-permute-start(bf16[64,2048]{1,0:T(8,128)(2,1)S(1)} %get-tuple-element.35), channel_id=1, source_target_pairs={{0,1},{1,0},{2,3},{3,2},{4,5},{5,4},{6,7},{7,6},{8,9},{9,8},{10,11... | collective-permute-start | bytes 786440 | tf_op jit(solution)/shard_map/ppermute | solution.py:344

commit v3 on v0

v3 whole, which is shorter than its diff:
```python
import functools
import math

import jax
import jax.numpy as jnp
from jax import lax
from jax.experimental import pallas as pl
from jax.experimental.pallas import tpu as pltpu
from jax.sharding import PartitionSpec as P

HD = 128
QB = 4
STEPS = 3
LN2 = math.log(2.0)
FACTOR = 1.0 / (math.sqrt(HD) * LN2)
NEG = -math.inf

SMEM = pl.BlockSpec(memory_space=pltpu.SMEM)
VMEM = pl.BlockSpec(memory_space=pltpu.VMEM)
PARAMS = pltpu.CompilerParams(vmem_limit_bytes=16 * 2**20)
COST = pl.CostEstimate(flops=1000, bytes_accessed=1000, transcendentals=0)


def stacked(q_ref, kv_head, group):
    first = kv_head * group
    return jnp.concatenate([q_ref[:, (first + j) * HD : (first + j + 1) * HD] for j in range(group)], axis=0)


def scores_of(keys, queries):
    return lax.dot_general(keys, queries, (((1,), (1,)), ((), ())), preferred_element_type=jnp.float32)


def mix(left, right):
    return lax.dot_general(left, right, (((0,), (0,)), ((), ())), preferred_element_type=jnp.float32)


def local_kernel(half, entries, idx_ref, plan_ref, q_ref, k_ref, v_ref, held_ref, acc_ref, stat_ref, meta_ref):
    rows = q_ref.shape[0]
    kv_heads = k_ref.shape[1] // HD
    group = q_ref.shape[1] // k_ref.shape[1]
    device = idx_ref[0]
    for t in range(STEPS):
        meta_ref[t] = -1

    def scan(i, carry):
        @pl.when(plan_ref[i, 2] == device)
        def _():
            meta_ref[plan_ref[i, 0]] = plan_ref[i, 3]

        return carry

    lax.fori_loop(0, entries, scan, 0)
    held_bias = jnp.where(device >= half - 2, 0.0, NEG)
    key_pos = lax.broadcasted_iota(jnp.int32, (rows, group * rows), 0)
    row_pos = lax.broadcasted_iota(jnp.int32, (rows, group * rows), 1) % rows
    causal = key_pos <= row_pos
    for g in range(kv_heads):
        cols = slice(g * HD, (g + 1) * HD)
        queries = stacked(q_ref, g, group)
        own = jnp.where(causal, scores_of(k_ref[:, cols], queries), NEG)
        held = scores_of(held_ref[0, :, cols], queries) + held_bias
        top = jnp.maximum(jnp.max(own, axis=0, keepdims=True), jnp.max(held, axis=0, keepdims=True))
        w_own = jnp.exp2((own - top) * FACTOR)
        w_held = jnp.exp2((held - top) * FACTOR)
        stat_ref[g, 0:1, :] = top
        stat_ref[g, 1:2, :] = jnp.sum(w_own, axis=0, keepdims=True) + jnp.sum(w_held, axis=0, keepdims=True)
        acc_ref[g] = mix(v_ref[:, cols], w_own.astype(jnp.bfloat16)) + mix(
            held_ref[1, :, cols], w_held.astype(jnp.bfloat16)
        )


def near_kernel(half, idx_ref, q_ref, acc_ref, stat_ref, n2, sx, sn2, base_ref, log_ref, sub_ref, kv):
    rows = q_ref.shape[0]
    kv_heads = n2.shape[2] // HD
    group = q_ref.shape[1] // n2.shape[2]
    sub = rows // QB
    device = idx_ref[0]
    even = device % 2 == 0

    @pl.when(even)
    def _():
        kv[:, :rows, :] = sn2[...]

    @pl.when(jnp.logical_not(even))
    def _():
        kv[:, :rows, :] = sx[...]

    kv[:, rows:, :] = n2[...]
    first_key = lax.broadcasted_iota(jnp.int32, (2 * rows, 1), 0) < rows
    bias = jnp.where(
        first_key,
        jnp.where(device >= half - 1, 0.0, NEG),
        jnp.where(device >= half, 0.0, NEG),
    )
    for g in range(kv_heads):
        cols = slice(g * HD, (g + 1) * HD)
        scores = scores_of(kv[0, :, cols], stacked(q_ref, g, group)) + bias
        old_top = stat_ref[g, 0:1, :]
        top = jnp.maximum(old_top, jnp.max(scores, axis=0, keepdims=True))
        keep = jnp.exp2((old_top - top) * FACTOR)
        weights = jnp.exp2((scores - top) * FACTOR)
        total = stat_ref[g, 1:2, :] * keep + jnp.sum(weights, axis=0, keepdims=True)
        inverse = 1.0 / total
        mixed = acc_ref[g] * (keep * inverse) + mix(kv[1, :, cols], (weights * inverse).astype(jnp.bfloat16))
        logs = top * FACTOR + jnp.log2(total)
        for j in range(group):
            lanes = slice(j * rows, (j + 1) * rows)
            at = g * group + j
            base_ref[:, at * HD : (at + 1) * HD] = jnp.transpose(mixed[:, lanes]).astype(jnp.bfloat16)
            log_ref[at : at + 1, :] = logs[:, lanes]
        for c in range(QB):
            part = [logs[:, j * rows + c * sub : j * rows + (c + 1) * sub] for j in range(group)]
            sub_ref[c * kv_heads + g : c * kv_heads + g + 1, :] = jnp.concatenate(part, axis=1)


def helped(device, meta_ref):
    even = device % 2 == 0
    return meta_ref[1], jnp.where(even, meta_ref[0], meta_ref[2]), jnp.where(even, meta_ref[2], meta_ref[0])


def update(old_log, old, keys, values, queries, bias):
    scores = scores_of(keys, queries) * FACTOR
    if bias is not None:
        scores = scores + bias
    top = jnp.maximum(old_log, jnp.max(scores, axis=0, keepdims=True))
    weights = jnp.exp2(scores - top)
    keep = jnp.exp2(old_log - top)
    total = keep + jnp.sum(weights, axis=0, keepdims=True)
    inverse = 1.0 / total
    share = jnp.transpose(jnp.broadcast_to(keep * inverse, (8, keep.shape[1])))[:, 0:1]
    mixed = mix((weights * inverse).astype(jnp.bfloat16), values) + old.astype(jnp.float32) * share
    return mixed.astype(jnp.bfloat16), top + jnp.log2(total)


def rows_of(ref, starts, names):
    sub = ref.shape[0] // QB
    parts = [ref[pl.ds(pl.multiple_of(c * sub, sub), sub), j * HD : (j + 1) * HD] for c in starts for j in names]
    return jnp.concatenate(parts, axis=0)


def early_kernel(
    half, idx_ref, meta_ref, q_ref, base_ref, sub_ref, f, sf, g1, sg, full_ref, mine_ref, send_ref, new_ref, kv
):
    rows = q_ref.shape[0]
    sub = rows // QB
    kv_heads = f.shape[2] // HD
    group = q_ref.shape[1] // f.shape[2]
    device = idx_ref[0]
    head = idx_ref[1]
    full_ref[...] = base_ref[...]

    @pl.when(device >= half)
    def _():
        last = device == 2 * half - 1

        @pl.when(last)
        def _():
            kv[:, :rows, :] = g1[...]

        @pl.when(jnp.logical_not(last))
        def _():
            kv[:, :rows, :] = f[...]

        @pl.when(device == 2 * half - 2)
        def _():
            kv[:, rows:, :] = sg[...]

        @pl.when(device != 2 * half - 2)
        def _():
            kv[:, rows:, :] = sf[...]

        chosen = helped(device, meta_ref)[:2]
        starts = [jnp.maximum(c, 0) for c in chosen]
        lanes = group * sub
        first_key = lax.broadcasted_iota(jnp.int32, (2 * rows, 2 * lanes), 0) < rows
        first_row = lax.broadcasted_iota(jnp.int32, (2 * rows, 2 * lanes), 1) < lanes
        bias = jnp.where(first_key == first_row, 0.0, jnp.where(chosen[0] == chosen[1], 0.0, NEG))
        results = []
        for g in range(kv_heads):
            cols = slice(g * HD, (g + 1) * HD)
            names = range(g * group, (g + 1) * group)
            final, log = update(
                jnp.concatenate([sub_ref[pl.ds(c * kv_heads + g, 1), :] for c in starts], axis=1),
                rows_of(base_ref, starts, names),
                kv[0, :, cols],
                kv[1, :, cols],
                rows_of(q_ref, starts, names),
                bias,
            )
            for slot in range(2):
                part = slice(slot * lanes, (slot + 1) * lanes)
                new_ref[slot * kv_heads + g : slot * kv_heads + g + 1, :] = log[:, part]
                results.append((slot, names, final[part]))
        for slot in range(2):

            @pl.when(chosen[slot] >= 0)
            def _():
                at_rows = pl.ds(pl.multiple_of(starts[slot] * sub, sub), sub)
                for which, names, final in results:
                    if which == slot:
                        for i, j in enumerate(names):
                            full_ref[at_rows, j * HD : (j + 1) * HD] = final[i * sub : (i + 1) * sub]

    half_rows = rows // 2
    mine_ref[...] = full_ref[pl.ds(pl.multiple_of(head * half_rows, half_rows), half_rows), :]
    send_ref[...] = full_ref[pl.ds(pl.multiple_of((1 - head) * half_rows, half_rows), half_rows), :]


def late_kernel(half, idx_ref, meta_ref, q_ref, full_ref, sub_ref, new_ref, h, late_ref, log_ref):
    rows = q_ref.shape[0]
    sub = rows // QB
    kv_heads = h.shape[2] // HD
    group = q_ref.shape[1] // h.shape[2]
    device = idx_ref[0]
    first, second, chosen = helped(device, meta_ref)

    @pl.when(chosen >= 0)
    def _():
        for g in range(kv_heads):
            cols = slice(g * HD, (g + 1) * HD)
            names = range(g * group, (g + 1) * group)
            old_log = sub_ref[pl.ds(chosen * kv_heads + g, 1), :]
            old_log = jnp.where(first == chosen, new_ref[g : g + 1, :], old_log)
            old_log = jnp.where(second == chosen, new_ref[kv_heads + g : kv_heads + g + 1, :], old_log)
            final, log = update(
                old_log,
                rows_of(full_ref, [chosen], names),
                h[0, :, cols],
                h[1, :, cols],
                rows_of(q_ref, [chosen], names),
                None,
            )
            log_ref[g : g + 1, :] = log
            for i, j in enumerate(names):
                late_ref[:, j * HD : (j + 1) * HD] = final[i * sub : (i + 1) * sub]


def log_kernel(idx_ref, meta_ref, old_ref, new_ref, late_ref, log_ref):
    heads, rows = log_ref.shape
    kv_heads = late_ref.shape[0]
    group = heads // kv_heads
    sub = rows // QB
    row_sub = lax.broadcasted_iota(jnp.int32, (1, rows), 1) // sub
    first, second, third = helped(idx_ref[0], meta_ref)
    for j in range(heads):
        result = old_ref[j : j + 1, :]
        for chosen, source, at in (
            (first, new_ref, j // group),
            (second, new_ref, kv_heads + j // group),
            (third, late_ref, j // group),
        ):
            moved = pltpu.roll(source[at : at + 1, :], (chosen + QB - j % group) % QB * sub, 1)
            result = jnp.where(row_sub == chosen, moved, result)
        log_ref[j : j + 1, :] = result * LN2


def call(kernel, name, outs, scratch, *args, scalars):
    return pl.pallas_call(
        kernel,
        out_shape=outs,
        in_specs=[SMEM] * scalars + [VMEM] * (len(args) - scalars),
        out_specs=[SMEM if out.shape == (STEPS,) else VMEM for out in outs],
        scratch_shapes=scratch,
        compiler_params=PARAMS,
        cost_estimate=COST,
        name=name,
    )(*args)


def shards(query, key, value, held_kv, plan):
    rows = query.shape[0]
    sub = rows // QB
    wide = query.shape[1]
    kv_heads = key.shape[1] // HD
    group = wide // key.shape[1]
    size = lax.axis_size("ctx")
    half = size // 2
    device = lax.axis_index("ctx")
    head = lax.axis_index("head")
    idx = jnp.stack([device, head]).astype(jnp.int32)

    def send(x, route):
        return lax.ppermute(x, "ctx", route)

    def other_head(x):
        return lax.ppermute(x, "head", [(0, 1), (1, 0)])

    def f32(*shape):
        return jax.ShapeDtypeStruct(shape, jnp.float32)

    def b16(*shape):
        return jax.ShapeDtypeStruct(shape, jnp.bfloat16)

    swap = [(i, i ^ 1) for i in range(size)]
    two_on = swap[: half - 2] + [(i, i + 2) for i in range(half - 2, size - 2)]
    two_on += [(i, i - half) for i in range(size - 2, size)]
    across = [(i, i + half + 1) for i in range(half - 2)] + swap[half - 2 : half]
    across += [(i, i - half) for i in range(half, size - 2)] + [(size - 2, size - 1), (size - 1, half)]
    extra = [(half - 2, size - 1), (size - 1, size - 2), (size - 2, half - 1), (half - 1, half - 2)]
    moved = {i for i, _ in extra}
    extra += [(i, j) for i, j in swap if i not in moved]
    beside = swap[:half] + [(i, half + (i - half + (1 if i % 2 else -1)) % half) for i in range(half, size)]

    n2 = send(held_kv, two_on)
    sx = send(held_kv, swap)
    f = send(held_kv, across)
    acc, stat, meta = call(
        functools.partial(local_kernel, half, plan.shape[0]),
        "local",
        (f32(kv_heads, HD, group * rows), f32(kv_heads, 2, group * rows), jax.ShapeDtypeStruct((STEPS,), jnp.int32)),
        (),
        idx, plan, query, key, value, held_kv,
        scalars=2,
    )
    held_late, acc = lax.optimization_barrier((held_kv, acc))
    g1 = send(held_late, extra)
    pair = pltpu.VMEM((2, 2 * rows, key.shape[1]), jnp.bfloat16)
    outs = (b16(rows, wide), f32(kv_heads * group, rows), f32(QB * kv_heads, group * sub))

    def near(n2, sx, acc, stat):
        sn2 = send(n2, swap)
        return tuple(
            call(functools.partial(near_kernel, half), "near", outs, (pair,), idx, query, acc, stat, n2, sx, sn2, scalars=1)
        )

    def none(n2, sx, acc, stat):
        return tuple(jnp.zeros(out.shape, out.dtype) for out in outs)

    base, logs, table = lax.cond(plan[0, 0] >= 0, near, none, n2, sx, acc, stat)
    f, base = lax.optimization_barrier((f, base))
    h = send(f, beside)
    sf = send(f, swap)
    sg = send(g1, swap)
    full, mine, away, new = call(
        functools.partial(early_kernel, half),
        "early",
        (b16(rows, wide), b16(rows // 2, wide), b16(rows // 2, wide), f32(2 * kv_heads, group * sub)),
        (pair,),
        idx, meta, query, base, table, f, sf, g1, sg,
        scalars=2,
    )
    there = other_head(away)
    h, full = lax.optimization_barrier((h, full))
    late, late_log = call(
        functools.partial(late_kernel, half),
        "late",
        (b16(sub, wide), f32(kv_heads, group * sub)),
        (),
        idx, meta, query, full, table, new, h,
        scalars=2,
    )
    late_there = other_head(late)
    (log_total,) = call(
        log_kernel, "logs", (f32(kv_heads * group, rows),), (), idx, meta, logs, new, late_log, scalars=2
    )
    chosen = jnp.where(device % 2 == 0, meta[2], meta[0])
    row_sub = head * (QB // 2) + lax.broadcasted_iota(jnp.int32, (rows // 2, 1), 0) // sub
    mine = jnp.where(row_sub == chosen, jnp.concatenate([late] * (QB // 2), axis=0), mine)
    there = jnp.where(row_sub == chosen, jnp.concatenate([late_there] * (QB // 2), axis=0), there)
    attended = jnp.where(
        head == 0,
        jnp.concatenate([mine, there], axis=1),
        jnp.concatenate([there, mine], axis=1),
    )
    return (attended, log_total)


def solution(mesh):
    return jax.shard_map(
        shards,
        mesh=mesh,
        in_specs=(
            P("ctx", "head"),
            P("ctx", "head"),
            P("ctx", "head"),
            P(None, "ctx", "head"),
            P(),
        ),
        out_specs=(P(("ctx", "head"), None), P("head", "ctx")),
        check_vma=False,
    )
```

time: 116 us -> 36.8 us (0.32)
  the two profiles are of different devices: /device:TPU:16 before, /device:TPU:17 now
where the time goes in v3:
time: 36.8 us; the launch traced here: 36.5 us
  waiting for transfers between devices  12.8 us (35%)
  Pallas kernels  9.2 us (25%)
  starting transfers between devices  7.02 us (19%)
  local copies, waits for them, and re-layouts  3.64 us (10%)
  between operations  2.58 us (7%)
  other arithmetic  1.2 us (3%)
    ppermute x8, waiting for transfers between devices, send(): return lax.ppermute(x, 'ctx', route)  11.7 us
    pallas_call x5, Pallas kernels, call(): pl.pallas_call(kernel, out_shape=outs, in_specs=[SMEM] * scalars + [VMEM]...  9.2 us
    ppermute x8, starting transfers between devices, send(): return lax.ppermute(x, 'ctx', route)  4.4 us
    ppermute x2, starting transfers between devices, other_head(): return lax.ppermute(x, 'head', [(0, 1), (1, 0)])  2.62 us
    unnamed x9, local copies, waits for them, and re-layouts  2.5 us
    ppermute x2, waiting for transfers between devices, other_head(): return lax.ppermute(x, 'head', [(0, 1), (1, 0)])  1.07 us
    select_n x1, other arithmetic, shards(): jnp.where(head == 0, jnp.concatenate([mine, there], axis=1), jnp.concaten...  0.92 us
  transfers between devices with their start and end apart: 10, of which 6 were waited for; matrix products, arithmetic and copies ran while one was open for 4% of the time, Pallas kernels for 25%

profile of v3, /device:TPU:17, one launch (start us, length us, event | category | flops | bytes accessed | tf_op | source)
XLA Modules:
  0.0 36.5 jit_solution(14825431933593033714)
XLA Ops:
  0.6 1.3 %collective-permute-start.2 = (bf16[2,128,512]{2,1,0:T(8,128)(2,1)}, bf16[2,128,512]{2,1,0:T(8,128)(2,1)S(1)}, u32[]{:S(2)}, u32[]{:S(2)}) collective-permute-start(bf16[2,128,512]{2,1,0:T(8,128)(2,1)} %held_ref.1), channel_id=1, source_target_pairs={{0,2},{2,0},{4,6},{6,4},{8,10},{10,8},{12,16},{14,18},{16,20},{18,... | collective-permute-start | bytes 786440 | tf_op jit(solution)/shard_map/ppermute | solution.py:283
  1.9 1.0 %collective-permute-start.3 = (bf16[2,128,512]{2,1,0:T(8,128)(2,1)}, bf16[2,128,512]{2,1,0:T(8,128)(2,1)S(1)}, u32[]{:S(2)}, u32[]{:S(2)}) collective-permute-start(bf16[2,128,512]{2,1,0:T(8,128)(2,1)} %held_ref.1), channel_id=1, source_target_pairs={{0,2},{2,0},{4,6},{6,4},{8,10},{10,8},{12,14},{14,12},{16,18},{18,... | collective-permute-start | bytes 786440 | tf_op jit(solution)/shard_map/ppermute | solution.py:283
  2.9 0.6 %copy-done.3 = s32[16,4]{0,1:T(4,128)S(1)} copy-done((s32[16,4]{0,1:T(4,128)S(1)}, s32[16,4]{0,1:T(4,128)}, u32[]{:S(2)}) %copy-start.3) | copy-done | bytes 280
  3.6 0.9 %copy-done = bf16[128,512]{1,0:T(8,128)(2,1)S(1)} copy-done((bf16[128,512]{1,0:T(8,128)(2,1)S(1)}, bf16[128,512]{1,0:T(8,128)(2,1)}, u32[]{:S(2)}) %copy-start) | copy-done | bytes 131096
  4.5 0.9 %copy-done.1 = bf16[128,512]{1,0:T(8,128)(2,1)S(1)} copy-done((bf16[128,512]{1,0:T(8,128)(2,1)S(1)}, bf16[128,512]{1,0:T(8,128)(2,1)}, u32[]{:S(2)}) %copy-start.1) | copy-done | bytes 131096
  5.4 3.0 %local.1 = (f32[4,128,512]{2,1,0:T(8,128)S(1)}, f32[4,2,512]{2,1,0:T(2,128)S(1)}, s32[3]{0:T(128)S(1)}) custom-call(s32[2]{0:T(128)S(1)} %pad_add_fusion.idx_ref, s32[16,4]{1,0:T(8,128)S(1)} %copy.7.plan_ref, bf16[128,2048]{1,0:T(8,128)(2,1)} %q_ref.5, bf16[128,512]{1,0:T(8,128)(2,1)S(1)} %copy-done, bf16[128,512]{1,0:T(8,128)(2,1)S(1)} %copy-done.1, ...), custom_call_target="tpu_custom_call" | custom-call | flops 1000 | bytes 1000 | tf_op jit(solution)/shard_map/local/pallas_call | solution.py:258
  8.5 0.5 %slice.11 = s32[1,1]{0,1:T(1,128)} slice(s32[16,4]{0,1:T(4,128)S(1)} %copy-done.3), slice={[0:1], [0:1]} | slice | bytes 8 | tf_op jit(solution)/shard_map/slice | solution.py:329
  9.6 4.9 %collective-permute-done.2 = bf16[2,128,512]{2,1,0:T(8,128)(2,1)S(1)} collective-permute-done((bf16[2,128,512]{2,1,0:T(8,128)(2,1)}, bf16[2,128,512]{2,1,0:T(8,128)(2,1)S(1)}, u32[]{:S(2)}, u32[]{:S(2)}) %collective-permute-start.2) | collective-permute-done | bytes 262176 | tf_op jit(solution)/shard_map/ppermute | solution.py:283
  14.6 5.1 %conditional.1 = ((bf16[128,2048]{1,0:T(8,128)(2,1)S(1)}, f32[16,128]{1,0:T(8,128)S(1)}, f32[16,128]{1,0:T(8,128)S(1)})) conditional(s32[]{:T(128)} %bitcast.4, () %tuple.18, (bf16[2,128,512]{2,1,0:T(8,128)(2,1)S(1)}, s32[2]{0:T(128)S(1)}, bf16[128,2048]{1,0:T(8,128)(2,1)S(1)}, f32[4,128,512]{2,1,0:T(8,128)S(1)}, f32[4,2,512]{2,1,0:T(2,128)S(1)}, ...), branch_computations={%region_0.0_spmd, %region_1.0_spmd} | conditional | flops 1000 | bytes 1049624 | solution.py:329
  14.6 1.5 %collective-permute-start = (bf16[2,128,512]{2,1,0:T(8,128)(2,1)S(1)}, bf16[2,128,512]{2,1,0:T(8,128)(2,1)S(1)}, u32[]{:S(2)}, u32[]{:S(2)}) collective-permute-start(bf16[2,128,512]{2,1,0:T(8,128)(2,1)S(1)} %get-tuple-element.16.n2), channel_id=1, source_target_pairs={{0,2},{2,0},{4,6},{6,4},{8,10},{10,8},{12,14},{14,12},{16,18},{18,... | collective-permute-start | bytes 786440 | tf_op jit(solution)/shard_map/cond/branch_1_fun/ppermute | solution.py:283
  16.1 1.2 %collective-permute-done.sn2 = bf16[2,128,512]{2,1,0:T(8,128)(2,1)S(1)} collective-permute-done((bf16[2,128,512]{2,1,0:T(8,128)(2,1)S(1)}, bf16[2,128,512]{2,1,0:T(8,128)(2,1)S(1)}, u32[]{:S(2)}, u32[]{:S(2)}) %collective-permute-start) | collective-permute-done | bytes 262176 | tf_op jit(solution)/shard_map/cond/branch_1_fun/ppermute | solution.py:283
  17.3 2.4 %near.1 = (bf16[128,2048]{1,0:T(8,128)(2,1)S(1)}, f32[16,128]{1,0:T(8,128)S(1)}, f32[16,128]{1,0:T(8,128)S(1)}) custom-call(s32[2]{0:T(128)S(1)} %get-tuple-element.12.idx_ref, bf16[128,2048]{1,0:T(8,128)(2,1)S(1)} %get-tuple-element.13.q_ref, f32[4,128,512]{2,1,0:T(8,128)S(1)} %get-tuple-element.14.acc_ref, f32[4,2,512]{2,1,0:T(2,128)S(1)} %get-tuple-element.15.stat_ref, ...), custom_call_target="tpu_custom_call" | custom-call | flops 1000 | bytes 1000 | tf_op jit(solution)/shard_map/cond/branch_1_fun/near/pallas_call | solution.py:258
  19.7 0.4 %collective-permute-start.5 = (bf16[2,128,512]{2,1,0:T(8,128)(2,1)S(1)}, bf16[2,128,512]{2,1,0:T(8,128)(2,1)S(1)}, u32[]{:S(2)}, u32[]{:S(2)}) collective-permute-start(bf16[2,128,512]{2,1,0:T(8,128)(2,1)S(1)} %collective-permute-done.1.f), channel_id=1, source_target_pairs={{0,2},{2,0},{4,6},{6,4},{8,10},{10,8},{12,14},{14,12},{16,18},{18,... | collective-permute-start | bytes 786440 | tf_op jit(solution)/shard_map/ppermute | solution.py:283
  20.3 1.0 %collective-permute-done.5.sf = bf16[2,128,512]{2,1,0:T(8,128)(2,1)S(1)} collective-permute-done((bf16[2,128,512]{2,1,0:T(8,128)(2,1)S(1)}, bf16[2,128,512]{2,1,0:T(8,128)(2,1)S(1)}, u32[]{:S(2)}, u32[]{:S(2)}) %collective-permute-start.5) | collective-permute-done | bytes 262176 | tf_op jit(solution)/shard_map/ppermute | solution.py:283
  21.3 0.4 %collective-permute-done.7.sg = bf16[2,128,512]{2,1,0:T(8,128)(2,1)S(1)} collective-permute-done((bf16[2,128,512]{2,1,0:T(8,128)(2,1)S(1)}, bf16[2,128,512]{2,1,0:T(8,128)(2,1)S(1)}, u32[]{:S(2)}, u32[]{:S(2)}) %collective-permute-start.7) | collective-permute-done | bytes 262176 | tf_op jit(solution)/shard_map/ppermute | solution.py:283
  21.7 1.9 %early.1 = (bf16[128,2048]{1,0:T(8,128)(2,1)S(1)}, bf16[64,2048]{1,0:T(8,128)(2,1)S(1)}, bf16[64,2048]{1,0:T(8,128)(2,1)S(1)}, f32[8,128]{1,0:T(8,128)S(1)}) custom-call(s32[2]{0:T(128)S(1)} %pad_add_fusion.idx_ref, s32[3]{0:T(128)S(1)} %get-tuple-element.38.meta_ref, bf16[128,2048]{1,0:T(8,128)(2,1)S(1)} %copy-done.2, ...), custom_call_target="tpu_custom_call" | custom-call | flops 1000 | bytes 1000 | tf_op jit(solution)/shard_map/early/pallas_call | solution.py:258
  23.7 1.3 %collective-permute-start.9 = (bf16[64,2048]{1,0:T(8,128)(2,1)S(1)}, bf16[64,2048]{1,0:T(8,128)(2,1)S(1)}, u32[]{:S(2)}, u32[]{:S(2)}) collective-permute-start(bf16[64,2048]{1,0:T(8,128)(2,1)S(1)} %get-tuple-element.53), channel_id=1, source_target_pairs={{0,1},{1,0},{2,3},{3,2},{4,5},{5,4},{6,7},{7,6},{8,9},{9,8},{10,11... | collective-permute-start | bytes 786440 | tf_op jit(solution)/shard_map/ppermute | solution.py:286
  25.0 4.2 %collective-permute-done.4.h = bf16[2,128,512]{2,1,0:T(8,128)(2,1)S(1)} collective-permute-done((bf16[2,128,512]{2,1,0:T(8,128)(2,1)S(1)}, bf16[2,128,512]{2,1,0:T(8,128)(2,1)S(1)}, u32[]{:S(2)}, u32[]{:S(2)}) %collective-permute-start.4) | collective-permute-done | bytes 262176 | tf_op jit(solution)/shard_map/ppermute | solution.py:283
  29.2 0.6 %late.1 = (bf16[32,2048]{1,0:T(8,128)(2,1)S(1)}, f32[4,128]{1,0:T(4,128)S(1)}) custom-call(s32[2]{0:T(128)S(1)} %pad_add_fusion.idx_ref, s32[3]{0:T(128)S(1)} %get-tuple-element.38.meta_ref, bf16[128,2048]{1,0:T(8,128)(2,1)S(1)} %copy-done.2, bf16[128,2048]{1,0:T(8,128)(2,1)S(1)} %get-tuple-element.48.full_ref, f32[16,128]{1,0:T(8,128)S(1)} %get-tuple-element.45.sub_ref, ...), custom_call_target="tpu_custom_call" | custom-call | flops 1000 | bytes 1000 | tf_op jit(solution)/shard_map/late/pallas_call | solution.py:258
  29.8 1.3 %collective-permute-start.8 = (bf16[32,2048]{1,0:T(8,128)(2,1)S(1)}, bf16[32,2048]{1,0:T(8,128)(2,1)S(1)}, u32[]{:S(2)}, u32[]{:S(2)}) collective-permute-start(bf16[32,2048]{1,0:T(8,128)(2,1)S(1)} %get-tuple-element.51), channel_id=1, source_target_pairs={{0,1},{1,0},{2,3},{3,2},{4,5},{5,4},{6,7},{7,6},{8,9},{9,8},{10,11... | collective-permute-start | bytes 393224 | tf_op jit(solution)/shard_map/ppermute | solution.py:286
  31.1 0.6 %fusion.2 = (s32[1]{0:T(128)}, s32[1]{0:T(128)}) fusion(s32[3]{0:T(128)S(1)} %get-tuple-element.38.meta_ref), kind=kLoop, calls=%fused_computation.10 | loop fusion | bytes 16 | tf_op jit(solution)/shard_map/slice | solution.py:356
  33.0 1.3 %logs.1 = f32[16,128]{1,0:T(8,128)} custom-call(s32[2]{0:T(128)S(1)} %pad_add_fusion.idx_ref, s32[3]{0:T(128)S(1)} %get-tuple-element.38.meta_ref, f32[16,128]{1,0:T(8,128)S(1)} %get-tuple-element.54.old_ref, f32[8,128]{1,0:T(8,128)S(1)} %get-tuple-element.49.new_ref, f32[4,128]{1,0:T(4,128)S(1)} %get-tuple-element.55.late_ref), custom_call_target="tpu_custom_call" | custom-call | flops 1000 | bytes 1000 | tf_op jit(solution)/shard_map/logs/pallas_call | solution.py:258
  34.3 1.1 %collective-permute-done.8 = bf16[32,2048]{1,0:T(8,128)(2,1)S(1)} collective-permute-done((bf16[32,2048]{1,0:T(8,128)(2,1)S(1)}, bf16[32,2048]{1,0:T(8,128)(2,1)S(1)}, u32[]{:S(2)}, u32[]{:S(2)}) %collective-permute-start.8) | collective-permute-done | bytes 131104 | tf_op jit(solution)/shard_map/ppermute | solution.py:286
  35.5 0.9 %maximum_select_fusion = bf16[64,4096]{1,0:T(8,128)(2,1)} fusion(bf16[64,2048]{1,0:T(8,128)(2,1)S(1)} %get-tuple-element.57, bf16[64,2048]{1,0:T(8,128)(2,1)S(1)} %get-tuple-element.56, pred[]{:T(512)S(6)} %eq.21), kind=kLoop, calls=%fused_computation | loop fusion | flops 2359296 | bytes 1048577 | tf_op jit(solution)/shard_map/jit(_where)/select_n | solution.py:360
  (17 shorter events, 0.6 us)
Async XLA Ops:
  0.6 14.0 %collective-permute-start.2 = (bf16[2,128,512]{2,1,0:T(8,128)(2,1)}, bf16[2,128,512]{2,1,0:T(8,128)(2,1)S(1)}, u32[]{:S(2)}, u32[]{:S(2)}) collective-permute-start(bf16[2,128,512]{2,1,0:T(8,128)(2,1)} %held_ref.1), channel_id=1, source_target_pairs={{0,2},{2,0},{4,6},{6,4},{8,10},{10,8},{12,16},{14,18},{16,20},{18,... | collective-permute-start | bytes 786440 | tf_op jit(solution)/shard_map/ppermute | solution.py:283
  1.9 12.7 %collective-permute-start.3 = (bf16[2,128,512]{2,1,0:T(8,128)(2,1)}, bf16[2,128,512]{2,1,0:T(8,128)(2,1)S(1)}, u32[]{:S(2)}, u32[]{:S(2)}) collective-permute-start(bf16[2,128,512]{2,1,0:T(8,128)(2,1)} %held_ref.1), channel_id=1, source_target_pairs={{0,2},{2,0},{4,6},{6,4},{8,10},{10,8},{12,14},{14,12},{16,18},{18,... | collective-permute-start | bytes 786440 | tf_op jit(solution)/shard_map/ppermute | solution.py:283
  2.8 16.9 %collective-permute-start.1 = (bf16[2,128,512]{2,1,0:T(8,128)(2,1)}, bf16[2,128,512]{2,1,0:T(8,128)(2,1)S(1)}, u32[]{:S(2)}, u32[]{:S(2)}) collective-permute-start(bf16[2,128,512]{2,1,0:T(8,128)(2,1)} %held_ref.1), channel_id=1, source_target_pairs={{0,18},{2,20},{4,22},{6,24},{8,26},{10,28},{12,14},{14,12},{16,0},... | collective-permute-start | bytes 786440 | tf_op jit(solution)/shard_map/ppermute | solution.py:283
  2.9 0.7 %copy-start.3 = (s32[16,4]{0,1:T(4,128)S(1)}, s32[16,4]{0,1:T(4,128)}, u32[]{:S(2)}) copy-start(s32[16,4]{0,1:T(4,128)} %param.11) | copy-start | bytes 772
  3.6 0.9 %copy-start = (bf16[128,512]{1,0:T(8,128)(2,1)S(1)}, bf16[128,512]{1,0:T(8,128)(2,1)}, u32[]{:S(2)}) copy-start(bf16[128,512]{1,0:T(8,128)(2,1)} %k_ref.1) | copy-start | bytes 393220
  4.5 0.9 %copy-start.1 = (bf16[128,512]{1,0:T(8,128)(2,1)S(1)}, bf16[128,512]{1,0:T(8,128)(2,1)}, u32[]{:S(2)}) copy-start(bf16[128,512]{1,0:T(8,128)(2,1)} %v_ref.1) | copy-start | bytes 393220
  5.4 9.2 %copy-start.2 = (bf16[128,2048]{1,0:T(8,128)(2,1)S(1)}, bf16[128,2048]{1,0:T(8,128)(2,1)}, u32[]{:S(2)}) copy-start(bf16[128,2048]{1,0:T(8,128)(2,1)} %q_ref.5) | copy-start | bytes 1572868
  8.4 11.7 %collective-permute-start.6 = (bf16[2,128,512]{2,1,0:T(8,128)(2,1)}, bf16[2,128,512]{2,1,0:T(8,128)(2,1)S(1)}, u32[]{:S(2)}, u32[]{:S(2)}) collective-permute-start(bf16[2,128,512]{2,1,0:T(8,128)(2,1)} %held_ref.1), channel_id=1, source_target_pairs={{12,30},{30,28},{28,14},{14,12},{0,2},{2,0},{4,6},{6,4},{8,10},{10... | collective-permute-start | bytes 786440 | tf_op jit(solution)/shard_map/ppermute | solution.py:283
  14.6 2.7 %collective-permute-start = (bf16[2,128,512]{2,1,0:T(8,128)(2,1)S(1)}, bf16[2,128,512]{2,1,0:T(8,128)(2,1)S(1)}, u32[]{:S(2)}, u32[]{:S(2)}) collective-permute-start(bf16[2,128,512]{2,1,0:T(8,128)(2,1)S(1)} %get-tuple-element.16.n2), channel_id=1, source_target_pairs={{0,2},{2,0},{4,6},{6,4},{8,10},{10,8},{12,14},{14,12},{16,18},{18,... | collective-permute-start | bytes 786440 | tf_op jit(solution)/shard_map/cond/branch_1_fun/ppermute | solution.py:283
  19.7 1.6 %collective-permute-start.5 = (bf16[2,128,512]{2,1,0:T(8,128)(2,1)S(1)}, bf16[2,128,512]{2,1,0:T(8,128)(2,1)S(1)}, u32[]{:S(2)}, u32[]{:S(2)}) collective-permute-start(bf16[2,128,512]{2,1,0:T(8,128)(2,1)S(1)} %collective-permute-done.1.f), channel_id=1, source_target_pairs={{0,2},{2,0},{4,6},{6,4},{8,10},{10,8},{12,14},{14,12},{16,18},{18,... | collective-permute-start | bytes 786440 | tf_op jit(solution)/shard_map/ppermute | solution.py:283
  20.2 1.5 %collective-permute-start.7 = (bf16[2,128,512]{2,1,0:T(8,128)(2,1)S(1)}, bf16[2,128,512]{2,1,0:T(8,128)(2,1)S(1)}, u32[]{:S(2)}, u32[]{:S(2)}) collective-permute-start(bf16[2,128,512]{2,1,0:T(8,128)(2,1)S(1)} %collective-permute-done.6.g1), channel_id=1, source_target_pairs={{0,2},{2,0},{4,6},{6,4},{8,10},{10,8},{12,14},{14,12},{16,18},{18,... | collective-permute-start | bytes 786440 | tf_op jit(solution)/shard_map/ppermute | solution.py:283
  20.3 8.9 %collective-permute-start.4 = (bf16[2,128,512]{2,1,0:T(8,128)(2,1)S(1)}, bf16[2,128,512]{2,1,0:T(8,128)(2,1)S(1)}, u32[]{:S(2)}, u32[]{:S(2)}) collective-permute-start(bf16[2,128,512]{2,1,0:T(8,128)(2,1)S(1)} %collective-permute-done.1.f), channel_id=1, source_target_pairs={{0,2},{2,0},{4,6},{6,4},{8,10},{10,8},{12,14},{14,12},{16,30},{18,... | collective-permute-start | bytes 786440 | tf_op jit(solution)/shard_map/ppermute | solution.py:283
  23.7 11.7 %collective-permute-start.9 = (bf16[64,2048]{1,0:T(8,128)(2,1)S(1)}, bf16[64,2048]{1,0:T(8,128)(2,1)S(1)}, u32[]{:S(2)}, u32[]{:S(2)}) collective-permute-start(bf16[64,2048]{1,0:T(8,128)(2,1)S(1)} %get-tuple-element.53), channel_id=1, source_target_pairs={{0,1},{1,0},{2,3},{3,2},{4,5},{5,4},{6,7},{7,6},{8,9},{9,8},{10,11... | collective-permute-start | bytes 786440 | tf_op jit(solution)/shard_map/ppermute | solution.py:286
  29.8 5.6 %collective-permute-start.8 = (bf16[32,2048]{1,0:T(8,128)(2,1)S(1)}, bf16[32,2048]{1,0:T(8,128)(2,1)S(1)}, u32[]{:S(2)}, u32[]{:S(2)}) collective-permute-start(bf16[32,2048]{1,0:T(8,128)(2,1)S(1)} %get-tuple-element.51), channel_id=1, source_target_pairs={{0,1},{1,0},{2,3},{3,2},{4,5},{5,4},{6,7},{7,6},{8,9},{9,8},{10,11... | collective-permute-start | bytes 393224 | tf_op jit(solution)/shard_map/ppermute | solution.py:286

commit v4 on v3

--- a/solution.py
+++ b/solution.py
@@ -69,67 +69,80 @@
         )
 
 
-def near_kernel(half, idx_ref, q_ref, acc_ref, stat_ref, n2, sx, sn2, base_ref, log_ref, sub_ref, kv):
+def more(g, q_ref, acc_ref, stat_ref, keys, values, bias):
+    group = q_ref.shape[1] // (acc_ref.shape[0] * HD)
+    scores = scores_of(keys, stacked(q_ref, g, group)) + bias
+    old_top = stat_ref[g, 0:1, :]
+    top = jnp.maximum(old_top, jnp.max(scores, axis=0, keepdims=True))
+    keep = jnp.exp2((old_top - top) * FACTOR)
+    weights = jnp.exp2((scores - top) * FACTOR)
+    total = stat_ref[g, 1:2, :] * keep + jnp.sum(weights, axis=0, keepdims=True)
+    return top, total, acc_ref[g] * keep + mix(values, weights.astype(jnp.bfloat16))
+
+
+def two_back_kernel(half, idx_ref, q_ref, acc_ref, stat_ref, n2, out_acc_ref, out_stat_ref):
+    bias = jnp.where(idx_ref[0] >= half, 0.0, NEG)
+    for g in range(acc_ref.shape[0]):
+        cols = slice(g * HD, (g + 1) * HD)
+        top, total, mixed = more(g, q_ref, acc_ref, stat_ref, n2[0, :, cols], n2[1, :, cols], bias)
+        out_acc_ref[g] = mixed
+        out_stat_ref[g, 0:1, :] = top
+        out_stat_ref[g, 1:2, :] = total
+
+
+def near_kernel(half, idx_ref, q_ref, acc_ref, stat_ref, sx, sn2, base_ref, log_ref, sub_ref, kv):
     rows = q_ref.shape[0]
-    kv_heads = n2.shape[2] // HD
-    group = q_ref.shape[1] // n2.shape[2]
+    kv_heads = acc_ref.shape[0]
+    group = q_ref.shape[1] // (kv_heads * HD)
     sub = rows // QB
     device = idx_ref[0]
-    even = device % 2 == 0
-
-    @pl.when(even)
-    def _():
-        kv[:, :rows, :] = sn2[...]
-
-    @pl.when(jnp.logical_not(even))
-    def _():
-        kv[:, :rows, :] = sx[...]
-
-    kv[:, rows:, :] = n2[...]
-    first_key = lax.broadcasted_iota(jnp.int32, (2 * rows, 1), 0) < rows
-    bias = jnp.where(
-        first_key,
-        jnp.where(device >= half - 1, 0.0, NEG),
-        jnp.where(device >= half, 0.0, NEG),
-    )
+    choose(kv, slice(0, rows), device % 2 == 0, sn2, sx)
+    bias = jnp.where(device >= half - 1, 0.0, NEG)
     for g in range(kv_heads):
         cols = slice(g * HD, (g + 1) * HD)
-        scores = scores_of(kv[0, :, cols], stacked(q_ref, g, group)) + bias
-        old_top = stat_ref[g, 0:1, :]
-        top = jnp.maximum(old_top, jnp.max(scores, axis=0, keepdims=True))
-        keep = jnp.exp2((old_top - top) * FACTOR)
-        weights = jnp.exp2((scores - top) * FACTOR)
-        total = stat_ref[g, 1:2, :] * keep + jnp.sum(weights, axis=0, keepdims=True)
-        inverse = 1.0 / total
-        mixed = acc_ref[g] * (keep * inverse) + mix(kv[1, :, cols], (weights * inverse).astype(jnp.bfloat16))
+        top, total, mixed = more(g, q_ref, acc_ref, stat_ref, kv[0, :, cols], kv[1, :, cols], bias)
+        mixed = mixed * (1.0 / total)
         logs = top * FACTOR + jnp.log2(total)
         for j in range(group):
             lanes = slice(j * rows, (j + 1) * rows)
             at = g * group + j
-            base_ref[:, at * HD : (at + 1) * HD] = jnp.transpose(mixed[:, lanes]).astype(jnp.bfloat16)
+            base_ref[:, at * HD : (at + 1) * HD] = jnp.transpose(mixed[:, lanes].astype(jnp.bfloat16))
             log_ref[at : at + 1, :] = logs[:, lanes]
         for c in range(QB):
             part = [logs[:, j * rows + c * sub : j * rows + (c + 1) * sub] for j in range(group)]
             sub_ref[c * kv_heads + g : c * kv_heads + g + 1, :] = jnp.concatenate(part, axis=1)
 
 
+def choose(kv, at, when, one, other):
+    @pl.when(when)
+    def _():
+        kv[:, at, :] = one[...]
+
+    @pl.when(jnp.logical_not(when))
+    def _():
+        kv[:, at, :] = other[...]
+
+
 def helped(device, meta_ref):
     even = device % 2 == 0
     return meta_ref[1], jnp.where(even, meta_ref[0], meta_ref[2]), jnp.where(even, meta_ref[2], meta_ref[0])
 
 
-def update(old_log, old, keys, values, queries, bias):
-    scores = scores_of(keys, queries) * FACTOR
+def update(old_logs, olds, keys, values, queries, bias):
+    scores = [scores_of(k, q) * FACTOR for k, q in zip(keys, queries)]
     if bias is not None:
-        scores = scores + bias
-    top = jnp.maximum(old_log, jnp.max(scores, axis=0, keepdims=True))
-    weights = jnp.exp2(scores - top)
-    keep = jnp.exp2(old_log - top)
-    total = keep + jnp.sum(weights, axis=0, keepdims=True)
-    inverse = 1.0 / total
-    share = jnp.transpose(jnp.broadcast_to(keep * inverse, (8, keep.shape[1])))[:, 0:1]
-    mixed = mix((weights * inverse).astype(jnp.bfloat16), values) + old.astype(jnp.float32) * share
-    return mixed.astype(jnp.bfloat16), top + jnp.log2(total)
+        scores = [s + bias for s in scores]
+    tops = [jnp.maximum(o, jnp.max(s, axis=0, keepdims=True)) for o, s in zip(old_logs, scores)]
+    weights = [jnp.exp2(s - t) for s, t in zip(scores, tops)]
+    keeps = [jnp.exp2(o - t) for o, t in zip(old_logs, tops)]
+    totals = [k + jnp.sum(w, axis=0, keepdims=True) for k, w in zip(keeps, weights)]
+    inverses = [1.0 / t for t in totals]
+    shares = jnp.concatenate([k * i for k, i in zip(keeps, inverses)], axis=0)
+    pad = jnp.zeros((8 - shares.shape[0], shares.shape[1]), jnp.float32)
+    shares = jnp.transpose(jnp.concatenate([shares, pad], axis=0))
+    mixed = [mix((w * i).astype(jnp.bfloat16), v) for w, i, v in zip(weights, inverses, values)]
+    outs = [(m + o.astype(jnp.float32) * shares[:, g : g + 1]).astype(jnp.bfloat16) for g, (m, o) in enumerate(zip(mixed, olds))]
+    return outs, [t + jnp.log2(n) for t, n in zip(tops, totals)]
 
 
 def rows_of(ref, starts, names):
@@ -151,107 +164,91 @@
 
     @pl.when(device >= half)
     def _():
-        last = device == 2 * half - 1
-
-        @pl.when(last)
-        def _():
-            kv[:, :rows, :] = g1[...]
-
-        @pl.when(jnp.logical_not(last))
-        def _():
-            kv[:, :rows, :] = f[...]
-
-        @pl.when(device == 2 * half - 2)
-        def _():
-            kv[:, rows:, :] = sg[...]
-
-        @pl.when(device != 2 * half - 2)
-        def _():
-            kv[:, rows:, :] = sf[...]
-
+        choose(kv, slice(0, rows), device == 2 * half - 1, g1, f)
+        choose(kv, slice(rows, 2 * rows), device == 2 * half - 2, sg, sf)
         chosen = helped(device, meta_ref)[:2]
         starts = [jnp.maximum(c, 0) for c in chosen]
         lanes = group * sub
         first_key = lax.broadcasted_iota(jnp.int32, (2 * rows, 2 * lanes), 0) < rows
         first_row = lax.broadcasted_iota(jnp.int32, (2 * rows, 2 * lanes), 1) < lanes
         bias = jnp.where(first_key == first_row, 0.0, jnp.where(chosen[0] == chosen[1], 0.0, NEG))
-        results = []
-        for g in range(kv_heads):
-            cols = slice(g * HD, (g + 1) * HD)
-            names = range(g * group, (g + 1) * group)
-            final, log = update(
-                jnp.concatenate([sub_ref[pl.ds(c * kv_heads + g, 1), :] for c in starts], axis=1),
-                rows_of(base_ref, starts, names),
-                kv[0, :, cols],
-                kv[1, :, cols],
-                rows_of(q_ref, starts, names),
-                bias,
-            )
-            for slot in range(2):
-                part = slice(slot * lanes, (slot + 1) * lanes)
-                new_ref[slot * kv_heads + g : slot * kv_heads + g + 1, :] = log[:, part]
-                results.append((slot, names, final[part]))
+        names = [range(g * group, (g + 1) * group) for g in range(kv_heads)]
+        cols = [slice(g * HD, (g + 1) * HD) for g in range(kv_heads)]
+        finals, logs = update(
+            [
+                jnp.concatenate([sub_ref[pl.ds(c * kv_heads + g, 1), :] for c in starts], axis=1)
+                for g in range(kv_heads)
+            ],
+            [rows_of(base_ref, starts, n) for n in names],
+            [kv[0, :, c] for c in cols],
+            [kv[1, :, c] for c in cols],
+            [rows_of(q_ref, starts, n) for n in names],
+            bias,
+        )
         for slot in range(2):
+            at_rows = pl.ds(pl.multiple_of(starts[slot] * sub, sub), sub)
+            for g in range(kv_heads):
+                new_ref[slot * kv_heads + g : slot * kv_heads + g + 1, :] = logs[g][:, slot * lanes : (slot + 1) * lanes]
 
             @pl.when(chosen[slot] >= 0)
             def _():
-                at_rows = pl.ds(pl.multiple_of(starts[slot] * sub, sub), sub)
-                for which, names, final in results:
-                    if which == slot:
-                        for i, j in enumerate(names):
-                            full_ref[at_rows, j * HD : (j + 1) * HD] = final[i * sub : (i + 1) * sub]
+                for g in range(kv_heads):
+                    for i, j in enumerate(names[g]):
+                        at = slot * lanes + i * sub
+                        full_ref[at_rows, j * HD : (j + 1) * HD] = finals[g][at : at + sub]
 
     half_rows = rows // 2
     mine_ref[...] = full_ref[pl.ds(pl.multiple_of(head * half_rows, half_rows), half_rows), :]
     send_ref[...] = full_ref[pl.ds(pl.multiple_of((1 - head) * half_rows, half_rows), half_rows), :]
 
 
-def late_kernel(half, idx_ref, meta_ref, q_ref, full_ref, sub_ref, new_ref, h, late_ref, log_ref):
+def late_kernel(half, idx_ref, meta_ref, q_ref, full_ref, table_ref, new_ref, h, late_ref, log_ref):
     rows = q_ref.shape[0]
     sub = rows // QB
     kv_heads = h.shape[2] // HD
     group = q_ref.shape[1] // h.shape[2]
-    device = idx_ref[0]
-    first, second, chosen = helped(device, meta_ref)
+    first, second, chosen = helped(idx_ref[0], meta_ref)
 
     @pl.when(chosen >= 0)
     def _():
+        names = [range(g * group, (g + 1) * group) for g in range(kv_heads)]
+        cols = [slice(g * HD, (g + 1) * HD) for g in range(kv_heads)]
+        old_logs = []
         for g in range(kv_heads):
-            cols = slice(g * HD, (g + 1) * HD)
-            names = range(g * group, (g + 1) * group)
-            old_log = sub_ref[pl.ds(chosen * kv_heads + g, 1), :]
+            old_log = table_ref[pl.ds(chosen * kv_heads + g, 1), :]
             old_log = jnp.where(first == chosen, new_ref[g : g + 1, :], old_log)
-            old_log = jnp.where(second == chosen, new_ref[kv_heads + g : kv_heads + g + 1, :], old_log)
-            final, log = update(
-                old_log,
-                rows_of(full_ref, [chosen], names),
-                h[0, :, cols],
-                h[1, :, cols],
-                rows_of(q_ref, [chosen], names),
-                None,
-            )
-            log_ref[g : g + 1, :] = log
-            for i, j in enumerate(names):
-                late_ref[:, j * HD : (j + 1) * HD] = final[i * sub : (i + 1) * sub]
-
-
-def log_kernel(idx_ref, meta_ref, old_ref, new_ref, late_ref, log_ref):
+            old_logs.append(jnp.where(second == chosen, new_ref[kv_heads + g : kv_heads + g + 1, :], old_log))
+        finals, logs = update(
+            old_logs,
+            [rows_of(full_ref, [chosen], n) for n in names],
+            [h[0, :, c] for c in cols],
+            [h[1, :, c] for c in cols],
+            [rows_of(q_ref, [chosen], n) for n in names],
+            None,
+        )
+        for g in range(kv_heads):
+            log_ref[g : g + 1, :] = logs[g]
+            for i, j in enumerate(names[g]):
+                late_ref[:, j * HD : (j + 1) * HD] = finals[g][i * sub : (i + 1) * sub]
+
+
+def log_kernel(slots, scale, idx_ref, meta_ref, old_ref, new_ref, log_ref):
     heads, rows = log_ref.shape
-    kv_heads = late_ref.shape[0]
+    kv_heads = new_ref.shape[0] // len(slots)
     group = heads // kv_heads
     sub = rows // QB
     row_sub = lax.broadcasted_iota(jnp.int32, (1, rows), 1) // sub
-    first, second, third = helped(idx_ref[0], meta_ref)
+    results = [old_ref[j : j + 1, :] for j in range(heads)]
+    for at, slot in enumerate(slots):
+        chosen = helped(idx_ref[0], meta_ref)[slot]
+        source = new_ref[at * kv_heads : (at + 1) * kv_heads, :]
+        for i in range(group):
+            moved = pltpu.roll(source, (chosen + QB - i) % QB * sub, 1)
+            for g in range(kv_heads):
+                j = g * group + i
+                results[j] = jnp.where(row_sub == chosen, moved[g : g + 1, :], results[j])
     for j in range(heads):
-        result = old_ref[j : j + 1, :]
-        for chosen, source, at in (
-            (first, new_ref, j // group),
-            (second, new_ref, kv_heads + j // group),
-            (third, late_ref, j // group),
-        ):
-            moved = pltpu.roll(source[at : at + 1, :], (chosen + QB - j % group) % QB * sub, 1)
-            result = jnp.where(row_sub == chosen, moved, result)
-        log_ref[j : j + 1, :] = result * LN2
+        log_ref[j : j + 1, :] = results[j] * scale
 
 
 def call(kernel, name, outs, scratch, *args, scalars):
@@ -316,15 +313,25 @@
     g1 = send(held_late, extra)
     pair = pltpu.VMEM((2, 2 * rows, key.shape[1]), jnp.bfloat16)
     outs = (b16(rows, wide), f32(kv_heads * group, rows), f32(QB * kv_heads, group * sub))
+    state = (f32(kv_heads, HD, group * rows), f32(kv_heads, 2, group * rows))
+    held_late, acc = lax.optimization_barrier((held_kv, acc))
+    g1 = send(held_late, extra)
+    chosen = jnp.where(device % 2 == 0, meta[2], meta[0]) - head * (QB // 2)
+    row_sub = lax.broadcasted_iota(jnp.int32, (rows // 2, 1), 0) // sub
+    n2, acc, chosen = lax.optimization_barrier((n2, acc, chosen))
 
     def near(n2, sx, acc, stat):
         sn2 = send(n2, swap)
-        return tuple(
-            call(functools.partial(near_kernel, half), "near", outs, (pair,), idx, query, acc, stat, n2, sx, sn2, scalars=1)
+        acc, stat = call(
+            functools.partial(two_back_kernel, half), "two_back", state, (), idx, query, acc, stat, n2, scalars=1
+        )
+        one = pltpu.VMEM(held_kv.shape, jnp.bfloat16)
+        return list(
+            call(functools.partial(near_kernel, half), "near", outs, (one,), idx, query, acc, stat, sx, sn2, scalars=1)
         )
 
     def none(n2, sx, acc, stat):
-        return tuple(jnp.zeros(out.shape, out.dtype) for out in outs)
+        return [jnp.zeros(out.shape, out.dtype) for out in outs]
 
     base, logs, table = lax.cond(plan[0, 0] >= 0, near, none, n2, sx, acc, stat)
     f, base = lax.optimization_barrier((f, base))
@@ -340,7 +347,9 @@
         scalars=2,
     )
     there = other_head(away)
-    h, full = lax.optimization_barrier((h, full))
+    log_out = f32(kv_heads * group, rows)
+    (logs,) = call(functools.partial(log_kernel, (0, 1), 1.0), "logs", (log_out,), (), idx, meta, logs, new, scalars=2)
+    h, full, logs = lax.optimization_barrier((h, full, logs))
     late, late_log = call(
         functools.partial(late_kernel, half),
         "late",
@@ -351,12 +360,11 @@
     )
     late_there = other_head(late)
     (log_total,) = call(
-        log_kernel, "logs", (f32(kv_heads * group, rows),), (), idx, meta, logs, new, late_log, scalars=2
-    )
-    chosen = jnp.where(device % 2 == 0, meta[2], meta[0])
-    row_sub = head * (QB // 2) + lax.broadcasted_iota(jnp.int32, (rows // 2, 1), 0) // sub
-    mine = jnp.where(row_sub == chosen, jnp.concatenate([late] * (QB // 2), axis=0), mine)
-    there = jnp.where(row_sub == chosen, jnp.concatenate([late_there] * (QB // 2), axis=0), there)
+        functools.partial(log_kernel, (2,), LN2), "last_logs", (log_out,), (), idx, meta, logs, late_log, scalars=2
+    )
+    in_late = row_sub == chosen
+    mine = jnp.where(in_late, jnp.concatenate([late] * (QB // 2), axis=0), mine)
+    there = jnp.where(in_late, jnp.concatenate([late_there] * (QB // 2), axis=0), there)
     attended = jnp.where(
         head == 0,
         jnp.concatenate([mine, there], axis=1),

time: 36.8 us -> 35.6 us (0.967)
  waiting for transfers between devices: 12.8 us -> 9.72 us
  Pallas kernels: 9.2 us -> 11.2 us
    ppermute x8, waiting for transfers between devices: 11.7 us -> 8.37 us  [send(): return lax.ppermute(x, 'ctx', route)]
    pallas_call x5 -> x7, Pallas kernels: 9.2 us -> 11.2 us  [call(): pl.pallas_call(kernel, out_shape=outs, in_specs=[SMEM] * scalars + [VMEM]...]
  transfers between devices with their start and end apart: 10 -> 10, of which waited for: 6 -> 5; matrix products, arithmetic and copies ran while one was open for 4% -> 4% of each run, Pallas kernels for 25% -> 32%
where the time goes in v4:
time: 35.6 us; the launch traced here: 35.4 us
  Pallas kernels  11.2 us (31%)
  waiting for transfers between devices  9.72 us (27%)
  starting transfers between devices  7 us (20%)
  local copies, waits for them, and re-layouts  3.66 us (10%)
  between operations  2.63 us (7%)
  other arithmetic  1.2 us (3%)
    pallas_call x7, Pallas kernels, call(): pl.pallas_call(kernel, out_shape=outs, in_specs=[SMEM] * scalars + [VMEM]...  11.2 us
    ppermute x8, waiting for transfers between devices, send(): return lax.ppermute(x, 'ctx', route)  8.37 us
    ppermute x8, starting transfers between devices, send(): return lax.ppermute(x, 'ctx', route)  4.39 us
    ppermute x2, starting transfers between devices, other_head(): return lax.ppermute(x, 'head', [(0, 1), (1, 0)])  2.61 us
    unnamed x9, local copies, waits for them, and re-layouts  2.5 us
    ppermute x2, waiting for transfers between devices, other_head(): return lax.ppermute(x, 'head', [(0, 1), (1, 0)])  1.35 us
    select_n x1, other arithmetic, shards(): jnp.where(head == 0, jnp.concatenate([mine, there], axis=1), jnp.concaten...  0.92 us
  transfers between devices with their start and end apart: 10, of which 5 were waited for; matrix products, arithmetic and copies ran while one was open for 4% of the time, Pallas kernels for 32%

profile of v4, /device:TPU:17, one launch (start us, length us, event | category | flops | bytes accessed | tf_op | source)
XLA Modules:
  0.0 35.4 jit_solution(9677050157928217468)
XLA Ops:
  0.6 1.3 %collective-permute-start.1 = (bf16[2,128,512]{2,1,0:T(8,128)(2,1)}, bf16[2,128,512]{2,1,0:T(8,128)(2,1)S(1)}, u32[]{:S(2)}, u32[]{:S(2)}) collective-permute-start(bf16[2,128,512]{2,1,0:T(8,128)(2,1)} %held_ref.1), channel_id=1, source_target_pairs={{0,2},{2,0},{4,6},{6,4},{8,10},{10,8},{12,16},{14,18},{16,20},{18,... | collective-permute-start | bytes 786440 | tf_op jit(solution)/shard_map/ppermute | solution.py:280
  1.9 1.0 %collective-permute-start.3 = (bf16[2,128,512]{2,1,0:T(8,128)(2,1)}, bf16[2,128,512]{2,1,0:T(8,128)(2,1)S(1)}, u32[]{:S(2)}, u32[]{:S(2)}) collective-permute-start(bf16[2,128,512]{2,1,0:T(8,128)(2,1)} %held_ref.1), channel_id=1, source_target_pairs={{0,2},{2,0},{4,6},{6,4},{8,10},{10,8},{12,14},{14,12},{16,18},{18,... | collective-permute-start | bytes 786440 | tf_op jit(solution)/shard_map/ppermute | solution.py:280
  2.9 0.6 %copy-done.3 = s32[16,4]{0,1:T(4,128)S(1)} copy-done((s32[16,4]{0,1:T(4,128)S(1)}, s32[16,4]{0,1:T(4,128)}, u32[]{:S(2)}) %copy-start.3) | copy-done | bytes 280
  3.6 0.9 %copy-done = bf16[128,512]{1,0:T(8,128)(2,1)S(1)} copy-done((bf16[128,512]{1,0:T(8,128)(2,1)S(1)}, bf16[128,512]{1,0:T(8,128)(2,1)}, u32[]{:S(2)}) %copy-start) | copy-done | bytes 131096
  4.5 0.9 %copy-done.1 = bf16[128,512]{1,0:T(8,128)(2,1)S(1)} copy-done((bf16[128,512]{1,0:T(8,128)(2,1)S(1)}, bf16[128,512]{1,0:T(8,128)(2,1)}, u32[]{:S(2)}) %copy-start.1) | copy-done | bytes 131096
  5.4 3.0 %local.1 = (f32[4,128,512]{2,1,0:T(8,128)S(1)}, f32[4,2,512]{2,1,0:T(2,128)S(1)}, s32[3]{0:T(128)S(1)}) custom-call(s32[2]{0:T(128)S(1)} %pad_add_fusion.idx_ref, s32[16,4]{1,0:T(8,128)S(1)} %copy.7.plan_ref, bf16[128,2048]{1,0:T(8,128)(2,1)} %q_ref.5, bf16[128,512]{1,0:T(8,128)(2,1)S(1)} %copy-done, bf16[128,512]{1,0:T(8,128)(2,1)S(1)} %copy-done.1, ...), custom_call_target="tpu_custom_call" | custom-call | flops 1000 | bytes 1000 | tf_op jit(solution)/shard_map/local/pallas_call | solution.py:255
  8.5 0.5 %slice.11 = s32[1,1]{0,1:T(1,128)} slice(s32[16,4]{0,1:T(4,128)S(1)} %copy-done.3), slice={[0:1], [0:1]} | slice | bytes 8 | tf_op jit(solution)/shard_map/slice | solution.py:336
  9.7 0.6 %fusion.1 = (s32[1]{0:T(128)}, s32[1]{0:T(128)}) fusion(s32[3]{0:T(128)S(1)} %get-tuple-element.48.meta_ref), kind=kLoop, calls=%fused_computation.9 | loop fusion | bytes 16 | tf_op jit(solution)/shard_map/slice | solution.py:319
  11.6 3.0 %collective-permute-done.1 = bf16[2,128,512]{2,1,0:T(8,128)(2,1)S(1)} collective-permute-done((bf16[2,128,512]{2,1,0:T(8,128)(2,1)}, bf16[2,128,512]{2,1,0:T(8,128)(2,1)S(1)}, u32[]{:S(2)}, u32[]{:S(2)}) %collective-permute-start.1) | collective-permute-done | bytes 262176 | tf_op jit(solution)/shard_map/ppermute | solution.py:280
  14.6 5.2 %conditional.1 = ((bf16[128,2048]{1,0:T(8,128)(2,1)S(1)}, f32[16,128]{1,0:T(8,128)S(1)}, f32[16,128]{1,0:T(8,128)S(1)})) conditional(s32[]{:T(128)} %bitcast.4, () %tuple.23, (s32[2]{0:T(128)S(1)}, bf16[128,2048]{1,0:T(8,128)(2,1)S(1)}, f32[4,128,512]{2,1,0:T(8,128)S(1)}, f32[4,2,512]{2,1,0:T(2,128)S(1)}, bf16[2,128,512]{2,1,0:T(8,128)(2,1)S(1)}, ...), branch_computations={%region_0.1_spmd, %region_1.2_spmd} | conditional | flops 2000 | bytes 1050624 | solution.py:336
  14.6 1.5 %collective-permute-start = (bf16[2,128,512]{2,1,0:T(8,128)(2,1)S(1)}, bf16[2,128,512]{2,1,0:T(8,128)(2,1)S(1)}, u32[]{:S(2)}, u32[]{:S(2)}) collective-permute-start(bf16[2,128,512]{2,1,0:T(8,128)(2,1)S(1)} %get-tuple-element.16.n2), channel_id=1, source_target_pairs={{0,2},{2,0},{4,6},{6,4},{8,10},{10,8},{12,14},{14,12},{16,18},{18,... | collective-permute-start | bytes 786440 | tf_op jit(solution)/shard_map/cond/branch_1_fun/ppermute | solution.py:280
  16.1 1.7 %two_back.1 = (f32[4,128,512]{2,1,0:T(8,128)S(1)}, f32[4,2,512]{2,1,0:T(2,128)S(1)}) custom-call(s32[2]{0:T(128)S(1)} %get-tuple-element.12.idx_ref, bf16[128,2048]{1,0:T(8,128)(2,1)S(1)} %get-tuple-element.13.q_ref, f32[4,128,512]{2,1,0:T(8,128)S(1)} %get-tuple-element.14.acc_ref, f32[4,2,512]{2,1,0:T(2,128)S(1)} %get-tuple-element.15.stat_ref, ...), custom_call_target="tpu_custom_call" | custom-call | flops 1000 | bytes 1000 | tf_op jit(solution)/shard_map/cond/branch_1_fun/two_back/pallas_call | solution.py:255
  17.9 1.9 %near.1 = (bf16[128,2048]{1,0:T(8,128)(2,1)S(1)}, f32[16,128]{1,0:T(8,128)S(1)}, f32[16,128]{1,0:T(8,128)S(1)}) custom-call(s32[2]{0:T(128)S(1)} %get-tuple-element.12.idx_ref, bf16[128,2048]{1,0:T(8,128)(2,1)S(1)} %get-tuple-element.13.q_ref, f32[4,128,512]{2,1,0:T(8,128)S(1)} %get-tuple-element.17.acc_ref, f32[4,2,512]{2,1,0:T(2,128)S(1)} %get-tuple-element.18.stat_ref, ...), custom_call_target="tpu_custom_call" | custom-call | flops 1000 | bytes 1000 | tf_op jit(solution)/shard_map/cond/branch_1_fun/near/pallas_call | solution.py:255
  19.9 0.5 %collective-permute-start.7 = (bf16[2,128,512]{2,1,0:T(8,128)(2,1)S(1)}, bf16[2,128,512]{2,1,0:T(8,128)(2,1)S(1)}, u32[]{:S(2)}, u32[]{:S(2)}) collective-permute-start(bf16[2,128,512]{2,1,0:T(8,128)(2,1)S(1)} %collective-permute-done.6.g1), channel_id=1, source_target_pairs={{0,2},{2,0},{4,6},{6,4},{8,10},{10,8},{12,14},{14,12},{16,18},{18,... | collective-permute-start | bytes 786440 | tf_op jit(solution)/shard_map/ppermute | solution.py:280
  20.4 1.0 %collective-permute-done.5.sf = bf16[2,128,512]{2,1,0:T(8,128)(2,1)S(1)} collective-permute-done((bf16[2,128,512]{2,1,0:T(8,128)(2,1)S(1)}, bf16[2,128,512]{2,1,0:T(8,128)(2,1)S(1)}, u32[]{:S(2)}, u32[]{:S(2)}) %collective-permute-start.5) | collective-permute-done | bytes 262176 | tf_op jit(solution)/shard_map/ppermute | solution.py:280
  21.8 1.6 %early.1 = (bf16[128,2048]{1,0:T(8,128)(2,1)S(1)}, bf16[64,2048]{1,0:T(8,128)(2,1)S(1)}, bf16[64,2048]{1,0:T(8,128)(2,1)S(1)}, f32[8,128]{1,0:T(8,128)S(1)}) custom-call(s32[2]{0:T(128)S(1)} %pad_add_fusion.idx_ref, s32[3]{0:T(128)S(1)} %get-tuple-element.48.meta_ref, bf16[128,2048]{1,0:T(8,128)(2,1)S(1)} %copy-done.2, ...), custom_call_target="tpu_custom_call" | custom-call | flops 1000 | bytes 1000 | tf_op jit(solution)/shard_map/early/pallas_call | solution.py:255
  23.4 1.3 %collective-permute-start.9 = (bf16[64,2048]{1,0:T(8,128)(2,1)S(1)}, bf16[64,2048]{1,0:T(8,128)(2,1)S(1)}, u32[]{:S(2)}, u32[]{:S(2)}) collective-permute-start(bf16[64,2048]{1,0:T(8,128)(2,1)S(1)} %get-tuple-element.65), channel_id=1, source_target_pairs={{0,1},{1,0},{2,3},{3,2},{4,5},{5,4},{6,7},{7,6},{8,9},{9,8},{10,11... | collective-permute-start | bytes 786440 | tf_op jit(solution)/shard_map/ppermute | solution.py:283
  24.7 0.6 %logs.1.old_ref = f32[16,128]{1,0:T(8,128)S(1)} custom-call(s32[2]{0:T(128)S(1)} %pad_add_fusion.idx_ref, s32[3]{0:T(128)S(1)} %get-tuple-element.48.meta_ref, f32[16,128]{1,0:T(8,128)S(1)} %get-tuple-element.59.old_ref, f32[8,128]{1,0:T(8,128)S(1)} %get-tuple-element.60.new_ref), custom_call_target="tpu_custom_call" | custom-call | flops 1000 | bytes 1000 | tf_op jit(solution)/shard_map/logs/pallas_call | solution.py:255
  25.3 4.0 %collective-permute-done.4.h = bf16[2,128,512]{2,1,0:T(8,128)(2,1)S(1)} collective-permute-done((bf16[2,128,512]{2,1,0:T(8,128)(2,1)S(1)}, bf16[2,128,512]{2,1,0:T(8,128)(2,1)S(1)}, u32[]{:S(2)}, u32[]{:S(2)}) %collective-permute-start.4) | collective-permute-done | bytes 262176 | tf_op jit(solution)/shard_map/ppermute | solution.py:280
  29.3 1.1 %late.1 = (bf16[32,2048]{1,0:T(8,128)(2,1)S(1)}, f32[4,128]{1,0:T(4,128)S(1)}) custom-call(s32[2]{0:T(128)S(1)} %pad_add_fusion.idx_ref, s32[3]{0:T(128)S(1)} %get-tuple-element.48.meta_ref, bf16[128,2048]{1,0:T(8,128)(2,1)S(1)} %copy-done.2, bf16[128,2048]{1,0:T(8,128)(2,1)S(1)} %get-tuple-element.61.full_ref, ...), custom_call_target="tpu_custom_call" | custom-call | flops 1000 | bytes 1000 | tf_op jit(solution)/shard_map/late/pallas_call | solution.py:255
  30.4 1.3 %collective-permute-start.8 = (bf16[32,2048]{1,0:T(8,128)(2,1)S(1)}, bf16[32,2048]{1,0:T(8,128)(2,1)S(1)}, u32[]{:S(2)}, u32[]{:S(2)}) collective-permute-start(bf16[32,2048]{1,0:T(8,128)(2,1)S(1)} %get-tuple-element.63), channel_id=1, source_target_pairs={{0,1},{1,0},{2,3},{3,2},{4,5},{5,4},{6,7},{7,6},{8,9},{9,8},{10,11... | collective-permute-start | bytes 393224 | tf_op jit(solution)/shard_map/ppermute | solution.py:283
  31.7 1.2 %last_logs.1 = f32[16,128]{1,0:T(8,128)} custom-call(s32[2]{0:T(128)S(1)} %pad_add_fusion.idx_ref, s32[3]{0:T(128)S(1)} %get-tuple-element.48.meta_ref, f32[16,128]{1,0:T(8,128)S(1)} %logs.1.old_ref, f32[4,128]{1,0:T(4,128)S(1)} %get-tuple-element.67.new_ref), custom_call_target="tpu_custom_call" | custom-call | flops 1000 | bytes 1000 | tf_op jit(solution)/shard_map/last_logs/pallas_call | solution.py:255
  32.9 1.3 %collective-permute-done.8 = bf16[32,2048]{1,0:T(8,128)(2,1)S(1)} collective-permute-done((bf16[32,2048]{1,0:T(8,128)(2,1)S(1)}, bf16[32,2048]{1,0:T(8,128)(2,1)S(1)}, u32[]{:S(2)}, u32[]{:S(2)}) %collective-permute-start.8) | collective-permute-done | bytes 131104 | tf_op jit(solution)/shard_map/ppermute | solution.py:283
  34.5 0.9 %maximum_select_fusion = bf16[64,4096]{1,0:T(8,128)(2,1)} fusion(bf16[64,2048]{1,0:T(8,128)(2,1)S(1)} %get-tuple-element.69, bf16[64,2048]{1,0:T(8,128)(2,1)S(1)} %get-tuple-element.68, pred[]{:T(512)S(6)} %eq.19), kind=kLoop, calls=%fused_computation | loop fusion | flops 2359296 | bytes 1048577 | tf_op jit(solution)/shard_map/jit(_where)/select_n | solution.py:368
  (19 shorter events, 0.9 us)
Async XLA Ops:
  0.6 14.0 %collective-permute-start.1 = (bf16[2,128,512]{2,1,0:T(8,128)(2,1)}, bf16[2,128,512]{2,1,0:T(8,128)(2,1)S(1)}, u32[]{:S(2)}, u32[]{:S(2)}) collective-permute-start(bf16[2,128,512]{2,1,0:T(8,128)(2,1)} %held_ref.1), channel_id=1, source_target_pairs={{0,2},{2,0},{4,6},{6,4},{8,10},{10,8},{12,16},{14,18},{16,20},{18,... | collective-permute-start | bytes 786440 | tf_op jit(solution)/shard_map/ppermute | solution.py:280
  1.9 12.7 %collective-permute-start.3 = (bf16[2,128,512]{2,1,0:T(8,128)(2,1)}, bf16[2,128,512]{2,1,0:T(8,128)(2,1)S(1)}, u32[]{:S(2)}, u32[]{:S(2)}) collective-permute-start(bf16[2,128,512]{2,1,0:T(8,128)(2,1)} %held_ref.1), channel_id=1, source_target_pairs={{0,2},{2,0},{4,6},{6,4},{8,10},{10,8},{12,14},{14,12},{16,18},{18,... | collective-permute-start | bytes 786440 | tf_op jit(solution)/shard_map/ppermute | solution.py:280
  2.8 16.9 %collective-permute-start.2 = (bf16[2,128,512]{2,1,0:T(8,128)(2,1)}, bf16[2,128,512]{2,1,0:T(8,128)(2,1)S(1)}, u32[]{:S(2)}, u32[]{:S(2)}) collective-permute-start(bf16[2,128,512]{2,1,0:T(8,128)(2,1)} %held_ref.1), channel_id=1, source_target_pairs={{0,18},{2,20},{4,22},{6,24},{8,26},{10,28},{12,14},{14,12},{16,0},... | collective-permute-start | bytes 786440 | tf_op jit(solution)/shard_map/ppermute | solution.py:280
  2.9 0.7 %copy-start.3 = (s32[16,4]{0,1:T(4,128)S(1)}, s32[16,4]{0,1:T(4,128)}, u32[]{:S(2)}) copy-start(s32[16,4]{0,1:T(4,128)} %param.11) | copy-start | bytes 772
  3.6 0.9 %copy-start = (bf16[128,512]{1,0:T(8,128)(2,1)S(1)}, bf16[128,512]{1,0:T(8,128)(2,1)}, u32[]{:S(2)}) copy-start(bf16[128,512]{1,0:T(8,128)(2,1)} %k_ref.1) | copy-start | bytes 393220
  4.5 0.9 %copy-start.1 = (bf16[128,512]{1,0:T(8,128)(2,1)S(1)}, bf16[128,512]{1,0:T(8,128)(2,1)}, u32[]{:S(2)}) copy-start(bf16[128,512]{1,0:T(8,128)(2,1)} %v_ref.1) | copy-start | bytes 393220
  5.4 9.2 %copy-start.2 = (bf16[128,2048]{1,0:T(8,128)(2,1)S(1)}, bf16[128,2048]{1,0:T(8,128)(2,1)}, u32[]{:S(2)}) copy-start(bf16[128,2048]{1,0:T(8,128)(2,1)} %q_ref.5) | copy-start | bytes 1572868
  8.4 11.4 %collective-permute-start.6 = (bf16[2,128,512]{2,1,0:T(8,128)(2,1)}, bf16[2,128,512]{2,1,0:T(8,128)(2,1)S(1)}, u32[]{:S(2)}, u32[]{:S(2)}) collective-permute-start(bf16[2,128,512]{2,1,0:T(8,128)(2,1)} %held_ref.1), channel_id=1, source_target_pairs={{12,30},{30,28},{28,14},{14,12},{0,2},{2,0},{4,6},{6,4},{8,10},{10... | collective-permute-start | bytes 786440 | tf_op jit(solution)/shard_map/ppermute | solution.py:280
  14.6 3.3 %collective-permute-start = (bf16[2,128,512]{2,1,0:T(8,128)(2,1)S(1)}, bf16[2,128,512]{2,1,0:T(8,128)(2,1)S(1)}, u32[]{:S(2)}, u32[]{:S(2)}) collective-permute-start(bf16[2,128,512]{2,1,0:T(8,128)(2,1)S(1)} %get-tuple-element.16.n2), channel_id=1, source_target_pairs={{0,2},{2,0},{4,6},{6,4},{8,10},{10,8},{12,14},{14,12},{16,18},{18,... | collective-permute-start | bytes 786440 | tf_op jit(solution)/shard_map/cond/branch_1_fun/ppermute | solution.py:280
  19.8 1.6 %collective-permute-start.5 = (bf16[2,128,512]{2,1,0:T(8,128)(2,1)S(1)}, bf16[2,128,512]{2,1,0:T(8,128)(2,1)S(1)}, u32[]{:S(2)}, u32[]{:S(2)}) collective-permute-start(bf16[2,128,512]{2,1,0:T(8,128)(2,1)S(1)} %collective-permute-done.2.f), channel_id=1, source_target_pairs={{0,2},{2,0},{4,6},{6,4},{8,10},{10,8},{12,14},{14,12},{16,18},{18,... | collective-permute-start | bytes 786440 | tf_op jit(solution)/shard_map/ppermute | solution.py:280
  19.9 1.9 %collective-permute-start.7 = (bf16[2,128,512]{2,1,0:T(8,128)(2,1)S(1)}, bf16[2,128,512]{2,1,0:T(8,128)(2,1)S(1)}, u32[]{:S(2)}, u32[]{:S(2)}) collective-permute-start(bf16[2,128,512]{2,1,0:T(8,128)(2,1)S(1)} %collective-permute-done.6.g1), channel_id=1, source_target_pairs={{0,2},{2,0},{4,6},{6,4},{8,10},{10,8},{12,14},{14,12},{16,18},{18,... | collective-permute-start | bytes 786440 | tf_op jit(solution)/shard_map/ppermute | solution.py:280
  20.4 8.9 %collective-permute-start.4 = (bf16[2,128,512]{2,1,0:T(8,128)(2,1)S(1)}, bf16[2,128,512]{2,1,0:T(8,128)(2,1)S(1)}, u32[]{:S(2)}, u32[]{:S(2)}) collective-permute-start(bf16[2,128,512]{2,1,0:T(8,128)(2,1)S(1)} %collective-permute-done.2.f), channel_id=1, source_target_pairs={{0,2},{2,0},{4,6},{6,4},{8,10},{10,8},{12,14},{14,12},{16,30},{18,... | collective-permute-start | bytes 786440 | tf_op jit(solution)/shard_map/ppermute | solution.py:280
  23.4 10.9 %collective-permute-start.9 = (bf16[64,2048]{1,0:T(8,128)(2,1)S(1)}, bf16[64,2048]{1,0:T(8,128)(2,1)S(1)}, u32[]{:S(2)}, u32[]{:S(2)}) collective-permute-start(bf16[64,2048]{1,0:T(8,128)(2,1)S(1)} %get-tuple-element.65), channel_id=1, source_target_pairs={{0,1},{1,0},{2,3},{3,2},{4,5},{5,4},{6,7},{7,6},{8,9},{9,8},{10,11... | collective-permute-start | bytes 786440 | tf_op jit(solution)/shard_map/ppermute | solution.py:283
  30.4 3.9 %collective-permute-start.8 = (bf16[32,2048]{1,0:T(8,128)(2,1)S(1)}, bf16[32,2048]{1,0:T(8,128)(2,1)S(1)}, u32[]{:S(2)}, u32[]{:S(2)}) collective-permute-start(bf16[32,2048]{1,0:T(8,128)(2,1)S(1)} %get-tuple-element.63), channel_id=1, source_target_pairs={{0,1},{1,0},{2,3},{3,2},{4,5},{5,4},{6,7},{7,6},{8,9},{9,8},{10,11... | collective-permute-start | bytes 393224 | tf_op jit(solution)/shard_map/ppermute | solution.py:283

commit v5 on v4

--- a/solution.py
+++ b/solution.py
@@ -67,6 +67,11 @@
         acc_ref[g] = mix(v_ref[:, cols], w_own.astype(jnp.bfloat16)) + mix(
             held_ref[1, :, cols], w_held.astype(jnp.bfloat16)
         )
+
+
+def last_sent(device, head, meta_ref):
+    chosen = helped(device, meta_ref)[2] - (1 - head) * (QB // 2)
+    return jnp.where((chosen >= 0) & (chosen < QB // 2), chosen, 1)
 
 
 def more(g, q_ref, acc_ref, stat_ref, keys, values, bias):
@@ -199,15 +204,20 @@
 
     half_rows = rows // 2
     mine_ref[...] = full_ref[pl.ds(pl.multiple_of(head * half_rows, half_rows), half_rows), :]
-    send_ref[...] = full_ref[pl.ds(pl.multiple_of((1 - head) * half_rows, half_rows), half_rows), :]
-
-
-def late_kernel(half, idx_ref, meta_ref, q_ref, full_ref, table_ref, new_ref, h, late_ref, log_ref):
+    first = (1 - last_sent(device, head, meta_ref)) * sub + (1 - head) * half_rows
+    send_ref[...] = full_ref[pl.ds(pl.multiple_of(first, sub), sub), :]
+
+
+def late_kernel(half, idx_ref, meta_ref, q_ref, full_ref, table_ref, new_ref, h, late_ref, send_ref, log_ref):
     rows = q_ref.shape[0]
     sub = rows // QB
     kv_heads = h.shape[2] // HD
     group = q_ref.shape[1] // h.shape[2]
-    first, second, chosen = helped(idx_ref[0], meta_ref)
+    device = idx_ref[0]
+    head = idx_ref[1]
+    first, second, chosen = helped(device, meta_ref)
+    at_send = last_sent(device, head, meta_ref) * sub + (1 - head) * (rows // 2)
+    send_ref[...] = full_ref[pl.ds(pl.multiple_of(at_send, sub), sub), :]
 
     @pl.when(chosen >= 0)
     def _():
@@ -228,8 +238,19 @@
         )
         for g in range(kv_heads):
             log_ref[g : g + 1, :] = logs[g]
-            for i, j in enumerate(names[g]):
-                late_ref[:, j * HD : (j + 1) * HD] = finals[g][i * sub : (i + 1) * sub]
+        here = chosen // (QB // 2) == head
+
+        @pl.when(here)
+        def _():
+            for g in range(kv_heads):
+                for i, j in enumerate(names[g]):
+                    late_ref[:, j * HD : (j + 1) * HD] = finals[g][i * sub : (i + 1) * sub]
+
+        @pl.when(jnp.logical_not(here))
+        def _():
+            for g in range(kv_heads):
+                for i, j in enumerate(names[g]):
+                    send_ref[:, j * HD : (j + 1) * HD] = finals[g][i * sub : (i + 1) * sub]
 
 
 def log_kernel(slots, scale, idx_ref, meta_ref, old_ref, new_ref, log_ref):
@@ -318,30 +339,30 @@
     g1 = send(held_late, extra)
     chosen = jnp.where(device % 2 == 0, meta[2], meta[0]) - head * (QB // 2)
     row_sub = lax.broadcasted_iota(jnp.int32, (rows // 2, 1), 0) // sub
-    n2, acc, chosen = lax.optimization_barrier((n2, acc, chosen))
-
-    def near(n2, sx, acc, stat):
+    last = jnp.where((chosen >= 0) & (chosen < QB // 2), chosen, 1)
+    n2, acc, chosen, last = lax.optimization_barrier((n2, acc, chosen, last))
+
+    def two_back(n2, acc, stat):
         sn2 = send(n2, swap)
-        acc, stat = call(
-            functools.partial(two_back_kernel, half), "two_back", state, (), idx, query, acc, stat, n2, scalars=1
-        )
-        one = pltpu.VMEM(held_kv.shape, jnp.bfloat16)
-        return list(
-            call(functools.partial(near_kernel, half), "near", outs, (one,), idx, query, acc, stat, sx, sn2, scalars=1)
-        )
-
-    def none(n2, sx, acc, stat):
-        return [jnp.zeros(out.shape, out.dtype) for out in outs]
-
-    base, logs, table = lax.cond(plan[0, 0] >= 0, near, none, n2, sx, acc, stat)
-    f, base = lax.optimization_barrier((f, base))
+        args = (idx, query, acc, stat, n2)
+        return [sn2, *call(functools.partial(two_back_kernel, half), "two_back", state, (), *args, scalars=1)]
+
+    def none(n2, acc, stat):
+        return [n2, acc, stat]
+
+    sn2, acc, stat = lax.cond(plan[0, 0] >= 0, two_back, none, n2, acc, stat)
+    f, acc = lax.optimization_barrier((f, acc))
     h = send(f, beside)
     sf = send(f, swap)
     sg = send(g1, swap)
+    one = pltpu.VMEM(held_kv.shape, jnp.bfloat16)
+    base, logs, table = call(
+        functools.partial(near_kernel, half), "near", outs, (one,), idx, query, acc, stat, sx, sn2, scalars=1
+    )
     full, mine, away, new = call(
         functools.partial(early_kernel, half),
         "early",
-        (b16(rows, wide), b16(rows // 2, wide), b16(rows // 2, wide), f32(2 * kv_heads, group * sub)),
+        (b16(rows, wide), b16(rows // 2, wide), b16(sub, wide), f32(2 * kv_heads, group * sub)),
         (pair,),
         idx, meta, query, base, table, f, sf, g1, sg,
         scalars=2,
@@ -350,21 +371,25 @@
     log_out = f32(kv_heads * group, rows)
     (logs,) = call(functools.partial(log_kernel, (0, 1), 1.0), "logs", (log_out,), (), idx, meta, logs, new, scalars=2)
     h, full, logs = lax.optimization_barrier((h, full, logs))
-    late, late_log = call(
+    late, late_away, late_log = call(
         functools.partial(late_kernel, half),
         "late",
-        (b16(sub, wide), f32(kv_heads, group * sub)),
+        (b16(sub, wide), b16(sub, wide), f32(kv_heads, group * sub)),
         (),
         idx, meta, query, full, table, new, h,
         scalars=2,
     )
-    late_there = other_head(late)
+    late_away, there = lax.optimization_barrier((late_away, there))
+    late_there = other_head(late_away)
     (log_total,) = call(
         functools.partial(log_kernel, (2,), LN2), "last_logs", (log_out,), (), idx, meta, logs, late_log, scalars=2
     )
-    in_late = row_sub == chosen
-    mine = jnp.where(in_late, jnp.concatenate([late] * (QB // 2), axis=0), mine)
-    there = jnp.where(in_late, jnp.concatenate([late_there] * (QB // 2), axis=0), there)
+    mine = jnp.where(row_sub == chosen, jnp.concatenate([late] * (QB // 2), axis=0), mine)
+    there = jnp.where(
+        row_sub == last,
+        jnp.concatenate([late_there] * (QB // 2), axis=0),
+        jnp.concatenate([there] * (QB // 2), axis=0),
+    )
     attended = jnp.where(
         head == 0,
         jnp.concatenate([mine, there], axis=1),

time: 35.6 us -> 34.9 us (0.980)
  waiting for transfers between devices: 9.72 us -> 8.67 us
    ppermute x8, waiting for transfers between devices: 8.37 us -> 6.39 us  [send(): return lax.ppermute(x, 'ctx', route)]
    ppermute x2, waiting for transfers between devices: 1.35 us -> 2.28 us  [other_head(): return lax.ppermute(x, 'head', [(0, 1), (1, 0)])]
  transfers between devices with their start and end apart: 10 -> 10, of which waited for: 5 -> 3; matrix products, arithmetic and copies ran while one was open for 4% -> 4% of each run, Pallas kernels for 32% -> 32%
where the time goes in v5:
time: 34.9 us; the launch traced here: 34.7 us
  Pallas kernels  11.2 us (32%)
  waiting for transfers between devices  8.67 us (25%)
  starting transfers between devices  7.09 us (20%)
  local copies, waits for them, and re-layouts  3.75 us (11%)
  between operations  2.67 us (8%)
  other arithmetic  1.27 us (4%)
    pallas_call x7, Pallas kernels, call(): pl.pallas_call(kernel, out_shape=outs, in_specs=[SMEM] * scalars + [VMEM]...  11.2 us
    ppermute x8, waiting for transfers between devices, send(): return lax.ppermute(x, 'ctx', route)  6.39 us
    ppermute x8, starting transfers between devices, send(): return lax.ppermute(x, 'ctx', route)  4.48 us
    ppermute x2, starting transfers between devices, other_head(): return lax.ppermute(x, 'head', [(0, 1), (1, 0)])  2.62 us
    unnamed x9, local copies, waits for them, and re-layouts  2.5 us
    ppermute x2, waiting for transfers between devices, other_head(): return lax.ppermute(x, 'head', [(0, 1), (1, 0)])  2.28 us
    select_n x1, other arithmetic, shards(): jnp.where(head == 0, jnp.concatenate([mine, there], axis=1), jnp.concaten...  0.92 us
  transfers between devices with their start and end apart: 10, of which 3 were waited for; matrix products, arithmetic and copies ran while one was open for 4% of the time, Pallas kernels for 32%

profile of v5, /device:TPU:17, one launch (start us, length us, event | category | flops | bytes accessed | tf_op | source)
XLA Modules:
  0.0 34.7 jit_solution(13244333404684835747)
XLA Ops:
  0.6 1.3 %collective-permute-start.1 = (bf16[2,128,512]{2,1,0:T(8,128)(2,1)}, bf16[2,128,512]{2,1,0:T(8,128)(2,1)S(1)}, u32[]{:S(2)}, u32[]{:S(2)}) collective-permute-start(bf16[2,128,512]{2,1,0:T(8,128)(2,1)} %held_ref.1), channel_id=1, source_target_pairs={{0,2},{2,0},{4,6},{6,4},{8,10},{10,8},{12,16},{14,18},{16,20},{18,... | collective-permute-start | bytes 786440 | tf_op jit(solution)/shard_map/ppermute | solution.py:301
  2.0 0.6 %copy-done.3 = s32[16,4]{0,1:T(4,128)S(1)} copy-done((s32[16,4]{0,1:T(4,128)S(1)}, s32[16,4]{0,1:T(4,128)}, u32[]{:S(2)}) %copy-start.3) | copy-done | bytes 280
  2.7 0.9 %copy-done = bf16[128,512]{1,0:T(8,128)(2,1)S(1)} copy-done((bf16[128,512]{1,0:T(8,128)(2,1)S(1)}, bf16[128,512]{1,0:T(8,128)(2,1)}, u32[]{:S(2)}) %copy-start) | copy-done | bytes 131096
  3.6 0.9 %copy-done.1 = bf16[128,512]{1,0:T(8,128)(2,1)S(1)} copy-done((bf16[128,512]{1,0:T(8,128)(2,1)S(1)}, bf16[128,512]{1,0:T(8,128)(2,1)}, u32[]{:S(2)}) %copy-start.1) | copy-done | bytes 131096
  4.5 3.0 %local.1 = (f32[4,128,512]{2,1,0:T(8,128)S(1)}, f32[4,2,512]{2,1,0:T(2,128)S(1)}, s32[3]{0:T(128)S(1)}) custom-call(s32[2]{0:T(128)S(1)} %pad_add_fusion.idx_ref, s32[16,4]{1,0:T(8,128)S(1)} %copy.7.plan_ref, bf16[128,2048]{1,0:T(8,128)(2,1)} %q_ref.7, bf16[128,512]{1,0:T(8,128)(2,1)S(1)} %copy-done, bf16[128,512]{1,0:T(8,128)(2,1)S(1)} %copy-done.1, ...), custom_call_target="tpu_custom_call" | custom-call | flops 1000 | bytes 1000 | tf_op jit(solution)/shard_map/local/pallas_call | solution.py:276
  7.5 1.0 %collective-permute-start.6 = (bf16[2,128,512]{2,1,0:T(8,128)(2,1)}, bf16[2,128,512]{2,1,0:T(8,128)(2,1)S(1)}, u32[]{:S(2)}, u32[]{:S(2)}) collective-permute-start(bf16[2,128,512]{2,1,0:T(8,128)(2,1)} %held_ref.1), channel_id=1, source_target_pairs={{12,30},{30,28},{28,14},{14,12},{0,2},{2,0},{4,6},{6,4},{8,10},{10... | collective-permute-start | bytes 786440 | tf_op jit(solution)/shard_map/ppermute | solution.py:301
  8.6 0.6 %fusion = (s32[1]{0:T(128)}, s32[1]{0:T(128)}) fusion(s32[3]{0:T(128)S(1)} %get-tuple-element.58.meta_ref), kind=kLoop, calls=%fused_computation.10 | loop fusion | bytes 16 | tf_op jit(solution)/shard_map/slice | solution.py:340
  10.5 0.5 %slice.11 = s32[1,1]{0,1:T(1,128)} slice(s32[16,4]{0,1:T(4,128)S(1)} %copy-done.3), slice={[0:1], [0:1]} | slice | bytes 8 | tf_op jit(solution)/shard_map/slice | solution.py:353
  11.7 2.9 %collective-permute-done.1 = bf16[2,128,512]{2,1,0:T(8,128)(2,1)S(1)} collective-permute-done((bf16[2,128,512]{2,1,0:T(8,128)(2,1)}, bf16[2,128,512]{2,1,0:T(8,128)(2,1)S(1)}, u32[]{:S(2)}, u32[]{:S(2)}) %collective-permute-start.1) | collective-permute-done | bytes 262176 | tf_op jit(solution)/shard_map/ppermute | solution.py:301
  14.6 3.4 %conditional.1 = ((bf16[2,128,512]{2,1,0:T(8,128)(2,1)S(1)}, f32[4,128,512]{2,1,0:T(8,128)S(1)}, f32[4,2,512]{2,1,0:T(2,128)S(1)})) conditional(s32[]{:T(128)} %bitcast.4, (bf16[2,128,512]{2,1,0:T(8,128)(2,1)S(1)}, f32[4,128,512]{2,1,0:T(8,128)S(1)}, f32[4,2,512]{2,1,0:T(2,128)S(1)}) %tuple.24, (bf16[2,128,512]{2,1,0:T(8,128)(2,1)S(1)}, ...), branch_computations={%region_0.1_spmd, %region_1.2_spmd} | conditional | flops 1000 | bytes 3703856 | solution.py:353
  14.6 1.5 %collective-permute-start = (bf16[2,128,512]{2,1,0:T(8,128)(2,1)S(1)}, bf16[2,128,512]{2,1,0:T(8,128)(2,1)S(1)}, u32[]{:S(2)}, u32[]{:S(2)}) collective-permute-start(bf16[2,128,512]{2,1,0:T(8,128)(2,1)S(1)} %get-tuple-element.16.n2), channel_id=1, source_target_pairs={{0,2},{2,0},{4,6},{6,4},{8,10},{10,8},{12,14},{14,12},{16,18},{18,... | collective-permute-start | bytes 786440 | tf_op jit(solution)/shard_map/cond/branch_1_fun/ppermute | solution.py:301
  16.2 1.7 %two_back.1 = (f32[4,128,512]{2,1,0:T(8,128)S(1)}, f32[4,2,512]{2,1,0:T(2,128)S(1)}) custom-call(s32[2]{0:T(128)S(1)} %get-tuple-element.17.idx_ref, bf16[128,2048]{1,0:T(8,128)(2,1)S(1)} %get-tuple-element.18.q_ref, f32[4,128,512]{2,1,0:T(8,128)S(1)} %copy.16.acc_ref, f32[4,2,512]{2,1,0:T(2,128)S(1)} %copy.17.stat_ref, ...), custom_call_target="tpu_custom_call" | custom-call | flops 1000 | bytes 1000 | tf_op jit(solution)/shard_map/cond/branch_1_fun/two_back/pallas_call | solution.py:276
  18.1 0.5 %collective-permute-start.7 = (bf16[2,128,512]{2,1,0:T(8,128)(2,1)S(1)}, bf16[2,128,512]{2,1,0:T(8,128)(2,1)S(1)}, u32[]{:S(2)}, u32[]{:S(2)}) collective-permute-start(bf16[2,128,512]{2,1,0:T(8,128)(2,1)S(1)} %collective-permute-done.6.g1), channel_id=1, source_target_pairs={{0,2},{2,0},{4,6},{6,4},{8,10},{10,8},{12,14},{14,12},{16,18},{18,... | collective-permute-start | bytes 786440 | tf_op jit(solution)/shard_map/ppermute | solution.py:301
  18.6 1.9 %near.1 = (bf16[128,2048]{1,0:T(8,128)(2,1)S(1)}, f32[16,128]{1,0:T(8,128)S(1)}, f32[16,128]{1,0:T(8,128)S(1)}) custom-call(s32[2]{0:T(128)S(1)} %pad_add_fusion.idx_ref, bf16[128,2048]{1,0:T(8,128)(2,1)S(1)} %copy-done.2, f32[4,128,512]{2,1,0:T(8,128)S(1)} %get-tuple-element.65.acc_ref, f32[4,2,512]{2,1,0:T(2,128)S(1)} %get-tuple-element.66.stat_ref, ...), custom_call_target="tpu_custom_call" | custom-call | flops 1000 | bytes 1000 | tf_op jit(solution)/shard_map/near/pallas_call | solution.py:276
  20.5 1.6 %early.1 = (bf16[128,2048]{1,0:T(8,128)(2,1)S(1)}, bf16[64,2048]{1,0:T(8,128)(2,1)S(1)}, bf16[32,2048]{1,0:T(8,128)(2,1)S(1)}, f32[8,128]{1,0:T(8,128)S(1)}) custom-call(s32[2]{0:T(128)S(1)} %pad_add_fusion.idx_ref, s32[3]{0:T(128)S(1)} %get-tuple-element.58.meta_ref, bf16[128,2048]{1,0:T(8,128)(2,1)S(1)} %copy-done.2, ...), custom_call_target="tpu_custom_call" | custom-call | flops 1000 | bytes 1000 | tf_op jit(solution)/shard_map/early/pallas_call | solution.py:276
  22.1 1.3 %collective-permute-start.8 = (bf16[32,2048]{1,0:T(8,128)(2,1)S(1)}, bf16[32,2048]{1,0:T(8,128)(2,1)S(1)}, u32[]{:S(2)}, u32[]{:S(2)}) collective-permute-start(bf16[32,2048]{1,0:T(8,128)(2,1)S(1)} %get-tuple-element.80), channel_id=1, source_target_pairs={{0,1},{1,0},{2,3},{3,2},{4,5},{5,4},{6,7},{7,6},{8,9},{9,8},{10,11... | collective-permute-start | bytes 393224 | tf_op jit(solution)/shard_map/ppermute | solution.py:304
  23.4 0.6 %logs.1.old_ref = f32[16,128]{1,0:T(8,128)S(1)} custom-call(s32[2]{0:T(128)S(1)} %pad_add_fusion.idx_ref, s32[3]{0:T(128)S(1)} %get-tuple-element.58.meta_ref, f32[16,128]{1,0:T(8,128)S(1)} %get-tuple-element.72.old_ref, f32[8,128]{1,0:T(8,128)S(1)} %get-tuple-element.73.new_ref), custom_call_target="tpu_custom_call" | custom-call | flops 1000 | bytes 1000 | tf_op jit(solution)/shard_map/logs/pallas_call | solution.py:276
  24.1 3.4 %collective-permute-done.3.h = bf16[2,128,512]{2,1,0:T(8,128)(2,1)S(1)} collective-permute-done((bf16[2,128,512]{2,1,0:T(8,128)(2,1)S(1)}, bf16[2,128,512]{2,1,0:T(8,128)(2,1)S(1)}, u32[]{:S(2)}, u32[]{:S(2)}) %collective-permute-start.3) | collective-permute-done | bytes 262176 | tf_op jit(solution)/shard_map/ppermute | solution.py:301
  27.5 1.1 %late.1 = (bf16[32,2048]{1,0:T(8,128)(2,1)S(1)}, bf16[32,2048]{1,0:T(8,128)(2,1)S(1)}, f32[4,128]{1,0:T(4,128)S(1)}) custom-call(s32[2]{0:T(128)S(1)} %pad_add_fusion.idx_ref, s32[3]{0:T(128)S(1)} %get-tuple-element.58.meta_ref, bf16[128,2048]{1,0:T(8,128)(2,1)S(1)} %copy-done.2, bf16[128,2048]{1,0:T(8,128)(2,1)S(1)} %get-tuple-element.74.full_ref, ...), custom_call_target="tpu_custom_call" | custom-call | flops 1000 | bytes 1000 | tf_op jit(solution)/shard_map/late/pallas_call | solution.py:276
  28.6 1.3 %collective-permute-start.9 = (bf16[32,2048]{1,0:T(8,128)(2,1)S(1)}, bf16[32,2048]{1,0:T(8,128)(2,1)S(1)}, u32[]{:S(2)}, u32[]{:S(2)}) collective-permute-start(bf16[32,2048]{1,0:T(8,128)(2,1)S(1)} %get-tuple-element.81), channel_id=1, source_target_pairs={{0,1},{1,0},{2,3},{3,2},{4,5},{5,4},{6,7},{7,6},{8,9},{9,8},{10,11... | collective-permute-start | bytes 393224 | tf_op jit(solution)/shard_map/ppermute | solution.py:304
  30.1 1.2 %last_logs.1 = f32[16,128]{1,0:T(8,128)} custom-call(s32[2]{0:T(128)S(1)} %pad_add_fusion.idx_ref, s32[3]{0:T(128)S(1)} %get-tuple-element.58.meta_ref, f32[16,128]{1,0:T(8,128)S(1)} %logs.1.old_ref, f32[4,128]{1,0:T(4,128)S(1)} %get-tuple-element.84.new_ref), custom_call_target="tpu_custom_call" | custom-call | flops 1000 | bytes 1000 | tf_op jit(solution)/shard_map/last_logs/pallas_call | solution.py:276
  31.3 2.3 %collective-permute-done.9 = bf16[32,2048]{1,0:T(8,128)(2,1)S(1)} collective-permute-done((bf16[32,2048]{1,0:T(8,128)(2,1)S(1)}, bf16[32,2048]{1,0:T(8,128)(2,1)S(1)}, u32[]{:S(2)}, u32[]{:S(2)}) %collective-permute-start.9) | collective-permute-done | bytes 131104 | tf_op jit(solution)/shard_map/ppermute | solution.py:304
  33.6 0.1 maximum_select_fusion.2
  33.7 0.9 %maximum_select_fusion = bf16[64,4096]{1,0:T(8,128)(2,1)} fusion(bf16[64,2048]{1,0:T(8,128)(2,1)S(1)} %maximum_select_fusion.2, bf16[64,2048]{1,0:T(8,128)(2,1)S(1)} %maximum_select_fusion.1, pred[]{:T(512)S(6)} %eq.30), kind=kLoop, calls=%fused_computation | loop fusion | flops 2359296 | bytes 1048577 | tf_op jit(solution)/shard_map/jit(_where)/select_n | solution.py:393
  (23 shorter events, 0.6 us)
Async XLA Ops:
  0.6 14.0 %collective-permute-start.1 = (bf16[2,128,512]{2,1,0:T(8,128)(2,1)}, bf16[2,128,512]{2,1,0:T(8,128)(2,1)S(1)}, u32[]{:S(2)}, u32[]{:S(2)}) collective-permute-start(bf16[2,128,512]{2,1,0:T(8,128)(2,1)} %held_ref.1), channel_id=1, source_target_pairs={{0,2},{2,0},{4,6},{6,4},{8,10},{10,8},{12,16},{14,18},{16,20},{18,... | collective-permute-start | bytes 786440 | tf_op jit(solution)/shard_map/ppermute | solution.py:301
  1.9 16.1 %collective-permute-start.2 = (bf16[2,128,512]{2,1,0:T(8,128)(2,1)}, bf16[2,128,512]{2,1,0:T(8,128)(2,1)S(1)}, u32[]{:S(2)}, u32[]{:S(2)}) collective-permute-start(bf16[2,128,512]{2,1,0:T(8,128)(2,1)} %held_ref.1), channel_id=1, source_target_pairs={{0,18},{2,20},{4,22},{6,24},{8,26},{10,28},{12,14},{14,12},{16,0},... | collective-permute-start | bytes 786440 | tf_op jit(solution)/shard_map/ppermute | solution.py:301
  1.9 0.7 %copy-start.3 = (s32[16,4]{0,1:T(4,128)S(1)}, s32[16,4]{0,1:T(4,128)}, u32[]{:S(2)}) copy-start(s32[16,4]{0,1:T(4,128)} %param.11) | copy-start | bytes 772
  2.7 0.9 %copy-start = (bf16[128,512]{1,0:T(8,128)(2,1)S(1)}, bf16[128,512]{1,0:T(8,128)(2,1)}, u32[]{:S(2)}) copy-start(bf16[128,512]{1,0:T(8,128)(2,1)} %k_ref.1) | copy-start | bytes 393220
  3.6 0.9 %copy-start.1 = (bf16[128,512]{1,0:T(8,128)(2,1)S(1)}, bf16[128,512]{1,0:T(8,128)(2,1)}, u32[]{:S(2)}) copy-start(bf16[128,512]{1,0:T(8,128)(2,1)} %v_ref.1) | copy-start | bytes 393220
  4.5 10.1 %copy-start.2 = (bf16[128,2048]{1,0:T(8,128)(2,1)S(1)}, bf16[128,2048]{1,0:T(8,128)(2,1)}, u32[]{:S(2)}) copy-start(bf16[128,2048]{1,0:T(8,128)(2,1)} %q_ref.7) | copy-start | bytes 1572868
  7.5 10.6 %collective-permute-start.6 = (bf16[2,128,512]{2,1,0:T(8,128)(2,1)}, bf16[2,128,512]{2,1,0:T(8,128)(2,1)S(1)}, u32[]{:S(2)}, u32[]{:S(2)}) collective-permute-start(bf16[2,128,512]{2,1,0:T(8,128)(2,1)} %held_ref.1), channel_id=1, source_target_pairs={{12,30},{30,28},{28,14},{14,12},{0,2},{2,0},{4,6},{6,4},{8,10},{10... | collective-permute-start | bytes 786440 | tf_op jit(solution)/shard_map/ppermute | solution.py:301
  8.5 10.1 %collective-permute-start.4 = (bf16[2,128,512]{2,1,0:T(8,128)(2,1)}, bf16[2,128,512]{2,1,0:T(8,128)(2,1)S(1)}, u32[]{:S(2)}, u32[]{:S(2)}) collective-permute-start(bf16[2,128,512]{2,1,0:T(8,128)(2,1)} %held_ref.1), channel_id=1, source_target_pairs={{0,2},{2,0},{4,6},{6,4},{8,10},{10,8},{12,14},{14,12},{16,18},{18,... | collective-permute-start | bytes 786440 | tf_op jit(solution)/shard_map/ppermute | solution.py:301
  14.6 3.4 %collective-permute-start = (bf16[2,128,512]{2,1,0:T(8,128)(2,1)S(1)}, bf16[2,128,512]{2,1,0:T(8,128)(2,1)S(1)}, u32[]{:S(2)}, u32[]{:S(2)}) collective-permute-start(bf16[2,128,512]{2,1,0:T(8,128)(2,1)S(1)} %get-tuple-element.16.n2), channel_id=1, source_target_pairs={{0,2},{2,0},{4,6},{6,4},{8,10},{10,8},{12,14},{14,12},{16,18},{18,... | collective-permute-start | bytes 786440 | tf_op jit(solution)/shard_map/cond/branch_1_fun/ppermute | solution.py:301
  18.0 2.5 %collective-permute-start.5 = (bf16[2,128,512]{2,1,0:T(8,128)(2,1)S(1)}, bf16[2,128,512]{2,1,0:T(8,128)(2,1)S(1)}, u32[]{:S(2)}, u32[]{:S(2)}) collective-permute-start(bf16[2,128,512]{2,1,0:T(8,128)(2,1)S(1)} %collective-permute-done.2.f), channel_id=1, source_target_pairs={{0,2},{2,0},{4,6},{6,4},{8,10},{10,8},{12,14},{14,12},{16,18},{18,... | collective-permute-start | bytes 786440 | tf_op jit(solution)/shard_map/ppermute | solution.py:301
  18.1 2.4 %collective-permute-start.7 = (bf16[2,128,512]{2,1,0:T(8,128)(2,1)S(1)}, bf16[2,128,512]{2,1,0:T(8,128)(2,1)S(1)}, u32[]{:S(2)}, u32[]{:S(2)}) collective-permute-start(bf16[2,128,512]{2,1,0:T(8,128)(2,1)S(1)} %collective-permute-done.6.g1), channel_id=1, source_target_pairs={{0,2},{2,0},{4,6},{6,4},{8,10},{10,8},{12,14},{14,12},{16,18},{18,... | collective-permute-start | bytes 786440 | tf_op jit(solution)/shard_map/ppermute | solution.py:301
  18.6 8.9 %collective-permute-start.3 = (bf16[2,128,512]{2,1,0:T(8,128)(2,1)S(1)}, bf16[2,128,512]{2,1,0:T(8,128)(2,1)S(1)}, u32[]{:S(2)}, u32[]{:S(2)}) collective-permute-start(bf16[2,128,512]{2,1,0:T(8,128)(2,1)S(1)} %collective-permute-done.2.f), channel_id=1, source_target_pairs={{0,2},{2,0},{4,6},{6,4},{8,10},{10,8},{12,14},{14,12},{16,30},{18,... | collective-permute-start | bytes 786440 | tf_op jit(solution)/shard_map/ppermute | solution.py:301
  22.1 6.5 %collective-permute-start.8 = (bf16[32,2048]{1,0:T(8,128)(2,1)S(1)}, bf16[32,2048]{1,0:T(8,128)(2,1)S(1)}, u32[]{:S(2)}, u32[]{:S(2)}) collective-permute-start(bf16[32,2048]{1,0:T(8,128)(2,1)S(1)} %get-tuple-element.80), channel_id=1, source_target_pairs={{0,1},{1,0},{2,3},{3,2},{4,5},{5,4},{6,7},{7,6},{8,9},{9,8},{10,11... | collective-permute-start | bytes 393224 | tf_op jit(solution)/shard_map/ppermute | solution.py:304
  28.6 5.0 %collective-permute-start.9 = (bf16[32,2048]{1,0:T(8,128)(2,1)S(1)}, bf16[32,2048]{1,0:T(8,128)(2,1)S(1)}, u32[]{:S(2)}, u32[]{:S(2)}) collective-permute-start(bf16[32,2048]{1,0:T(8,128)(2,1)S(1)} %get-tuple-element.81), channel_id=1, source_target_pairs={{0,1},{1,0},{2,3},{3,2},{4,5},{5,4},{6,7},{7,6},{8,9},{9,8},{10,11... | collective-permute-start | bytes 393224 | tf_op jit(solution)/shard_map/ppermute | solution.py:304

commit v6 on v5

--- a/solution.py
+++ b/solution.py
@@ -253,23 +253,22 @@
                     send_ref[:, j * HD : (j + 1) * HD] = finals[g][i * sub : (i + 1) * sub]
 
 
-def log_kernel(slots, scale, idx_ref, meta_ref, old_ref, new_ref, log_ref):
+def log_kernel(idx_ref, meta_ref, old_ref, new_ref, late_ref, log_ref):
     heads, rows = log_ref.shape
-    kv_heads = new_ref.shape[0] // len(slots)
+    kv_heads = late_ref.shape[0]
     group = heads // kv_heads
     sub = rows // QB
     row_sub = lax.broadcasted_iota(jnp.int32, (1, rows), 1) // sub
     results = [old_ref[j : j + 1, :] for j in range(heads)]
-    for at, slot in enumerate(slots):
-        chosen = helped(idx_ref[0], meta_ref)[slot]
-        source = new_ref[at * kv_heads : (at + 1) * kv_heads, :]
+    sources = (new_ref[:kv_heads, :], new_ref[kv_heads:, :], late_ref[...])
+    for chosen, source in zip(helped(idx_ref[0], meta_ref), sources):
         for i in range(group):
             moved = pltpu.roll(source, (chosen + QB - i) % QB * sub, 1)
             for g in range(kv_heads):
                 j = g * group + i
                 results[j] = jnp.where(row_sub == chosen, moved[g : g + 1, :], results[j])
     for j in range(heads):
-        log_ref[j : j + 1, :] = results[j] * scale
+        log_ref[j : j + 1, :] = results[j] * LN2
 
 
 def call(kernel, name, outs, scratch, *args, scalars):
@@ -368,9 +367,7 @@
         scalars=2,
     )
     there = other_head(away)
-    log_out = f32(kv_heads * group, rows)
-    (logs,) = call(functools.partial(log_kernel, (0, 1), 1.0), "logs", (log_out,), (), idx, meta, logs, new, scalars=2)
-    h, full, logs = lax.optimization_barrier((h, full, logs))
+    h, full = lax.optimization_barrier((h, full))
     late, late_away, late_log = call(
         functools.partial(late_kernel, half),
         "late",
@@ -379,10 +376,10 @@
         idx, meta, query, full, table, new, h,
         scalars=2,
     )
-    late_away, there = lax.optimization_barrier((late_away, there))
     late_there = other_head(late_away)
+    new, there = lax.optimization_barrier((new, there))
     (log_total,) = call(
-        functools.partial(log_kernel, (2,), LN2), "last_logs", (log_out,), (), idx, meta, logs, late_log, scalars=2
+        log_kernel, "logs", (f32(kv_heads * group, rows),), (), idx, meta, logs, new, late_log, scalars=2
     )
     mine = jnp.where(row_sub == chosen, jnp.concatenate([late] * (QB // 2), axis=0), mine)
     there = jnp.where(

time: 34.9 us -> 33.8 us (0.968)
  Pallas kernels: 11.2 us -> 10.6 us
  waiting for transfers between devices: 8.67 us -> 8.21 us
    ppermute x2, waiting for transfers between devices: 2.28 us -> 1.17 us  [other_head(): return lax.ppermute(x, 'head', [(0, 1), (1, 0)])]
    ppermute x8, waiting for transfers between devices: 6.39 us -> 7.04 us  [send(): return lax.ppermute(x, 'ctx', route)]
    pallas_call x7 -> x6, Pallas kernels: 11.2 us -> 10.6 us  [call(): pl.pallas_call(kernel, out_shape=outs, in_specs=[SMEM] * scalars + [VMEM]...]
  transfers between devices with their start and end apart: 10 -> 10, of which waited for: 3 -> 3; matrix products, arithmetic and copies ran while one was open for 4% -> 5% of each run, Pallas kernels for 32% -> 31%
where the time goes in v6:
time: 33.8 us; the launch traced here: 33.6 us
  Pallas kernels  10.6 us (31%)
  waiting for transfers between devices  8.21 us (24%)
  starting transfers between devices  7.07 us (21%)
  local copies, waits for them, and re-layouts  3.77 us (11%)
  between operations  2.68 us (8%)
  other arithmetic  1.27 us (4%)
    pallas_call x6, Pallas kernels, call(): pl.pallas_call(kernel, out_shape=outs, in_specs=[SMEM] * scalars + [VMEM]...  10.6 us
    ppermute x8, waiting for transfers between devices, send(): return lax.ppermute(x, 'ctx', route)  7.04 us
    ppermute x8, starting transfers between devices, send(): return lax.ppermute(x, 'ctx', route)  4.46 us
    ppermute x2, starting transfers between devices, other_head(): return lax.ppermute(x, 'head', [(0, 1), (1, 0)])  2.62 us
    unnamed x9, local copies, waits for them, and re-layouts  2.5 us
    ppermute x2, waiting for transfers between devices, other_head(): return lax.ppermute(x, 'head', [(0, 1), (1, 0)])  1.17 us
    select_n x1, other arithmetic, shards(): jnp.where(head == 0, jnp.concatenate([mine, there], axis=1), jnp.concaten...  0.92 us
  transfers between devices with their start and end apart: 10, of which 3 were waited for; matrix products, arithmetic and copies ran while one was open for 5% of the time, Pallas kernels for 31%

profile of v6, /device:TPU:17, one launch (start us, length us, event | category | flops | bytes accessed | tf_op | source)
XLA Modules:
  0.0 33.6 jit_solution(8656410331570730456)
XLA Ops:
  0.6 1.3 %collective-permute-start.1 = (bf16[2,128,512]{2,1,0:T(8,128)(2,1)}, bf16[2,128,512]{2,1,0:T(8,128)(2,1)S(1)}, u32[]{:S(2)}, u32[]{:S(2)}) collective-permute-start(bf16[2,128,512]{2,1,0:T(8,128)(2,1)} %held_ref.1), channel_id=1, source_target_pairs={{0,2},{2,0},{4,6},{6,4},{8,10},{10,8},{12,16},{14,18},{16,20},{18,... | collective-permute-start | bytes 786440 | tf_op jit(solution)/shard_map/ppermute | solution.py:300
  2.0 0.6 %copy-done.3 = s32[16,4]{0,1:T(4,128)S(1)} copy-done((s32[16,4]{0,1:T(4,128)S(1)}, s32[16,4]{0,1:T(4,128)}, u32[]{:S(2)}) %copy-start.3) | copy-done | bytes 280
  2.7 0.9 %copy-done = bf16[128,512]{1,0:T(8,128)(2,1)S(1)} copy-done((bf16[128,512]{1,0:T(8,128)(2,1)S(1)}, bf16[128,512]{1,0:T(8,128)(2,1)}, u32[]{:S(2)}) %copy-start) | copy-done | bytes 131096
  3.6 0.9 %copy-done.1 = bf16[128,512]{1,0:T(8,128)(2,1)S(1)} copy-done((bf16[128,512]{1,0:T(8,128)(2,1)S(1)}, bf16[128,512]{1,0:T(8,128)(2,1)}, u32[]{:S(2)}) %copy-start.1) | copy-done | bytes 131096
  4.5 3.0 %local.1 = (f32[4,128,512]{2,1,0:T(8,128)S(1)}, f32[4,2,512]{2,1,0:T(2,128)S(1)}, s32[3]{0:T(128)S(1)}) custom-call(s32[2]{0:T(128)S(1)} %pad_add_fusion.idx_ref, s32[16,4]{1,0:T(8,128)S(1)} %copy.7.plan_ref, bf16[128,2048]{1,0:T(8,128)(2,1)} %q_ref.7, bf16[128,512]{1,0:T(8,128)(2,1)S(1)} %copy-done, bf16[128,512]{1,0:T(8,128)(2,1)S(1)} %copy-done.1, ...), custom_call_target="tpu_custom_call" | custom-call | flops 1000 | bytes 1000 | tf_op jit(solution)/shard_map/local/pallas_call | solution.py:275
  7.5 1.0 %collective-permute-start.6 = (bf16[2,128,512]{2,1,0:T(8,128)(2,1)}, bf16[2,128,512]{2,1,0:T(8,128)(2,1)S(1)}, u32[]{:S(2)}, u32[]{:S(2)}) collective-permute-start(bf16[2,128,512]{2,1,0:T(8,128)(2,1)} %held_ref.1), channel_id=1, source_target_pairs={{12,30},{30,28},{28,14},{14,12},{0,2},{2,0},{4,6},{6,4},{8,10},{10... | collective-permute-start | bytes 786440 | tf_op jit(solution)/shard_map/ppermute | solution.py:300
  8.6 0.6 %fusion = (s32[1]{0:T(128)}, s32[1]{0:T(128)}) fusion(s32[3]{0:T(128)S(1)} %get-tuple-element.57.meta_ref), kind=kLoop, calls=%fused_computation.10 | loop fusion | bytes 16 | tf_op jit(solution)/shard_map/slice | solution.py:339
  10.5 0.5 %slice.11 = s32[1,1]{0,1:T(1,128)} slice(s32[16,4]{0,1:T(4,128)S(1)} %copy-done.3), slice={[0:1], [0:1]} | slice | bytes 8 | tf_op jit(solution)/shard_map/slice | solution.py:352
  11.7 2.9 %collective-permute-done.1 = bf16[2,128,512]{2,1,0:T(8,128)(2,1)S(1)} collective-permute-done((bf16[2,128,512]{2,1,0:T(8,128)(2,1)}, bf16[2,128,512]{2,1,0:T(8,128)(2,1)S(1)}, u32[]{:S(2)}, u32[]{:S(2)}) %collective-permute-start.1) | collective-permute-done | bytes 262176 | tf_op jit(solution)/shard_map/ppermute | solution.py:300
  14.6 3.4 %conditional.1 = ((bf16[2,128,512]{2,1,0:T(8,128)(2,1)S(1)}, f32[4,128,512]{2,1,0:T(8,128)S(1)}, f32[4,2,512]{2,1,0:T(2,128)S(1)})) conditional(s32[]{:T(128)} %bitcast.4, (bf16[2,128,512]{2,1,0:T(8,128)(2,1)S(1)}, f32[4,128,512]{2,1,0:T(8,128)S(1)}, f32[4,2,512]{2,1,0:T(2,128)S(1)}) %tuple.24, (bf16[2,128,512]{2,1,0:T(8,128)(2,1)S(1)}, ...), branch_computations={%region_0.1_spmd, %region_1.2_spmd} | conditional | flops 1000 | bytes 3703856 | solution.py:352
  14.6 1.5 %collective-permute-start = (bf16[2,128,512]{2,1,0:T(8,128)(2,1)S(1)}, bf16[2,128,512]{2,1,0:T(8,128)(2,1)S(1)}, u32[]{:S(2)}, u32[]{:S(2)}) collective-permute-start(bf16[2,128,512]{2,1,0:T(8,128)(2,1)S(1)} %get-tuple-element.16.n2), channel_id=1, source_target_pairs={{0,2},{2,0},{4,6},{6,4},{8,10},{10,8},{12,14},{14,12},{16,18},{18,... | collective-permute-start | bytes 786440 | tf_op jit(solution)/shard_map/cond/branch_1_fun/ppermute | solution.py:300
  16.2 1.7 %two_back.1 = (f32[4,128,512]{2,1,0:T(8,128)S(1)}, f32[4,2,512]{2,1,0:T(2,128)S(1)}) custom-call(s32[2]{0:T(128)S(1)} %get-tuple-element.17.idx_ref, bf16[128,2048]{1,0:T(8,128)(2,1)S(1)} %get-tuple-element.18.q_ref, f32[4,128,512]{2,1,0:T(8,128)S(1)} %copy.16.acc_ref, f32[4,2,512]{2,1,0:T(2,128)S(1)} %copy.17.stat_ref, ...), custom_call_target="tpu_custom_call" | custom-call | flops 1000 | bytes 1000 | tf_op jit(solution)/shard_map/cond/branch_1_fun/two_back/pallas_call | solution.py:275
  18.1 0.5 %collective-permute-start.7 = (bf16[2,128,512]{2,1,0:T(8,128)(2,1)S(1)}, bf16[2,128,512]{2,1,0:T(8,128)(2,1)S(1)}, u32[]{:S(2)}, u32[]{:S(2)}) collective-permute-start(bf16[2,128,512]{2,1,0:T(8,128)(2,1)S(1)} %collective-permute-done.6.g1), channel_id=1, source_target_pairs={{0,2},{2,0},{4,6},{6,4},{8,10},{10,8},{12,14},{14,12},{16,18},{18,... | collective-permute-start | bytes 786440 | tf_op jit(solution)/shard_map/ppermute | solution.py:300
  18.6 1.9 %near.1 = (bf16[128,2048]{1,0:T(8,128)(2,1)S(1)}, f32[16,128]{1,0:T(8,128)S(1)}, f32[16,128]{1,0:T(8,128)S(1)}) custom-call(s32[2]{0:T(128)S(1)} %pad_add_fusion.idx_ref, bf16[128,2048]{1,0:T(8,128)(2,1)S(1)} %copy-done.2, f32[4,128,512]{2,1,0:T(8,128)S(1)} %get-tuple-element.64.acc_ref, f32[4,2,512]{2,1,0:T(2,128)S(1)} %get-tuple-element.65.stat_ref, ...), custom_call_target="tpu_custom_call" | custom-call | flops 1000 | bytes 1000 | tf_op jit(solution)/shard_map/near/pallas_call | solution.py:275
  20.5 1.6 %early.1 = (bf16[128,2048]{1,0:T(8,128)(2,1)S(1)}, bf16[64,2048]{1,0:T(8,128)(2,1)S(1)}, bf16[32,2048]{1,0:T(8,128)(2,1)S(1)}, f32[8,128]{1,0:T(8,128)S(1)}) custom-call(s32[2]{0:T(128)S(1)} %pad_add_fusion.idx_ref, s32[3]{0:T(128)S(1)} %get-tuple-element.57.meta_ref, bf16[128,2048]{1,0:T(8,128)(2,1)S(1)} %copy-done.2, ...), custom_call_target="tpu_custom_call" | custom-call | flops 1000 | bytes 1000 | tf_op jit(solution)/shard_map/early/pallas_call | solution.py:275
  22.1 1.3 %collective-permute-start.9 = (bf16[32,2048]{1,0:T(8,128)(2,1)S(1)}, bf16[32,2048]{1,0:T(8,128)(2,1)S(1)}, u32[]{:S(2)}, u32[]{:S(2)}) collective-permute-start(bf16[32,2048]{1,0:T(8,128)(2,1)S(1)} %get-tuple-element.78), channel_id=1, source_target_pairs={{0,1},{1,0},{2,3},{3,2},{4,5},{5,4},{6,7},{7,6},{8,9},{9,8},{10,11... | collective-permute-start | bytes 393224 | tf_op jit(solution)/shard_map/ppermute | solution.py:303
  23.4 4.1 %collective-permute-done.3.h = bf16[2,128,512]{2,1,0:T(8,128)(2,1)S(1)} collective-permute-done((bf16[2,128,512]{2,1,0:T(8,128)(2,1)S(1)}, bf16[2,128,512]{2,1,0:T(8,128)(2,1)S(1)}, u32[]{:S(2)}, u32[]{:S(2)}) %collective-permute-start.3) | collective-permute-done | bytes 262176 | tf_op jit(solution)/shard_map/ppermute | solution.py:300
  27.5 1.1 %late.1 = (bf16[32,2048]{1,0:T(8,128)(2,1)S(1)}, bf16[32,2048]{1,0:T(8,128)(2,1)S(1)}, f32[4,128]{1,0:T(4,128)S(1)}) custom-call(s32[2]{0:T(128)S(1)} %pad_add_fusion.idx_ref, s32[3]{0:T(128)S(1)} %get-tuple-element.57.meta_ref, bf16[128,2048]{1,0:T(8,128)(2,1)S(1)} %copy-done.2, bf16[128,2048]{1,0:T(8,128)(2,1)S(1)} %get-tuple-element.71.full_ref, ...), custom_call_target="tpu_custom_call" | custom-call | flops 1000 | bytes 1000 | tf_op jit(solution)/shard_map/late/pallas_call | solution.py:275
  28.7 1.3 %collective-permute-start.8 = (bf16[32,2048]{1,0:T(8,128)(2,1)S(1)}, bf16[32,2048]{1,0:T(8,128)(2,1)S(1)}, u32[]{:S(2)}, u32[]{:S(2)}) collective-permute-start(bf16[32,2048]{1,0:T(8,128)(2,1)S(1)} %get-tuple-element.77), channel_id=1, source_target_pairs={{0,1},{1,0},{2,3},{3,2},{4,5},{5,4},{6,7},{7,6},{8,9},{9,8},{10,11... | collective-permute-start | bytes 393224 | tf_op jit(solution)/shard_map/ppermute | solution.py:303
  30.0 0.1 maximum_select_fusion.1
  30.1 1.3 %logs.1 = f32[16,128]{1,0:T(8,128)} custom-call(s32[2]{0:T(128)S(1)} %pad_add_fusion.idx_ref, s32[3]{0:T(128)S(1)} %get-tuple-element.57.meta_ref, f32[16,128]{1,0:T(8,128)S(1)} %get-tuple-element.80.old_ref, f32[8,128]{1,0:T(8,128)S(1)} %get-tuple-element.81.new_ref, f32[4,128]{1,0:T(4,128)S(1)} %get-tuple-element.82.late_ref), custom_call_target="tpu_custom_call" | custom-call | flops 1000 | bytes 1000 | tf_op jit(solution)/shard_map/logs/pallas_call | solution.py:275
  31.4 1.2 %collective-permute-done.8 = bf16[32,2048]{1,0:T(8,128)(2,1)S(1)} collective-permute-done((bf16[32,2048]{1,0:T(8,128)(2,1)S(1)}, bf16[32,2048]{1,0:T(8,128)(2,1)S(1)}, u32[]{:S(2)}, u32[]{:S(2)}) %collective-permute-start.8) | collective-permute-done | bytes 131104 | tf_op jit(solution)/shard_map/ppermute | solution.py:303
  32.5 0.1 maximum_select_fusion.2
  32.7 0.9 %maximum_select_fusion = bf16[64,4096]{1,0:T(8,128)(2,1)} fusion(bf16[64,2048]{1,0:T(8,128)(2,1)S(1)} %maximum_select_fusion.2, bf16[64,2048]{1,0:T(8,128)(2,1)S(1)} %maximum_select_fusion.1, pred[]{:T(512)S(6)} %eq.30), kind=kLoop, calls=%fused_computation | loop fusion | flops 2359296 | bytes 1048577 | tf_op jit(solution)/shard_map/jit(_where)/select_n | solution.py:390
  (22 shorter events, 0.5 us)
Async XLA Ops:
  0.6 14.0 %collective-permute-start.1 = (bf16[2,128,512]{2,1,0:T(8,128)(2,1)}, bf16[2,128,512]{2,1,0:T(8,128)(2,1)S(1)}, u32[]{:S(2)}, u32[]{:S(2)}) collective-permute-start(bf16[2,128,512]{2,1,0:T(8,128)(2,1)} %held_ref.1), channel_id=1, source_target_pairs={{0,2},{2,0},{4,6},{6,4},{8,10},{10,8},{12,16},{14,18},{16,20},{18,... | collective-permute-start | bytes 786440 | tf_op jit(solution)/shard_map/ppermute | solution.py:300
  1.9 16.1 %collective-permute-start.2 = (bf16[2,128,512]{2,1,0:T(8,128)(2,1)}, bf16[2,128,512]{2,1,0:T(8,128)(2,1)S(1)}, u32[]{:S(2)}, u32[]{:S(2)}) collective-permute-start(bf16[2,128,512]{2,1,0:T(8,128)(2,1)} %held_ref.1), channel_id=1, source_target_pairs={{0,18},{2,20},{4,22},{6,24},{8,26},{10,28},{12,14},{14,12},{16,0},... | collective-permute-start | bytes 786440 | tf_op jit(solution)/shard_map/ppermute | solution.py:300
  1.9 0.7 %copy-start.3 = (s32[16,4]{0,1:T(4,128)S(1)}, s32[16,4]{0,1:T(4,128)}, u32[]{:S(2)}) copy-start(s32[16,4]{0,1:T(4,128)} %param.11) | copy-start | bytes 772
  2.7 0.9 %copy-start = (bf16[128,512]{1,0:T(8,128)(2,1)S(1)}, bf16[128,512]{1,0:T(8,128)(2,1)}, u32[]{:S(2)}) copy-start(bf16[128,512]{1,0:T(8,128)(2,1)} %k_ref.1) | copy-start | bytes 393220
  3.6 0.9 %copy-start.1 = (bf16[128,512]{1,0:T(8,128)(2,1)S(1)}, bf16[128,512]{1,0:T(8,128)(2,1)}, u32[]{:S(2)}) copy-start(bf16[128,512]{1,0:T(8,128)(2,1)} %v_ref.1) | copy-start | bytes 393220
  4.5 10.1 %copy-start.2 = (bf16[128,2048]{1,0:T(8,128)(2,1)S(1)}, bf16[128,2048]{1,0:T(8,128)(2,1)}, u32[]{:S(2)}) copy-start(bf16[128,2048]{1,0:T(8,128)(2,1)} %q_ref.7) | copy-start | bytes 1572868
  7.5 10.6 %collective-permute-start.6 = (bf16[2,128,512]{2,1,0:T(8,128)(2,1)}, bf16[2,128,512]{2,1,0:T(8,128)(2,1)S(1)}, u32[]{:S(2)}, u32[]{:S(2)}) collective-permute-start(bf16[2,128,512]{2,1,0:T(8,128)(2,1)} %held_ref.1), channel_id=1, source_target_pairs={{12,30},{30,28},{28,14},{14,12},{0,2},{2,0},{4,6},{6,4},{8,10},{10... | collective-permute-start | bytes 786440 | tf_op jit(solution)/shard_map/ppermute | solution.py:300
  8.5 10.2 %collective-permute-start.4 = (bf16[2,128,512]{2,1,0:T(8,128)(2,1)}, bf16[2,128,512]{2,1,0:T(8,128)(2,1)S(1)}, u32[]{:S(2)}, u32[]{:S(2)}) collective-permute-start(bf16[2,128,512]{2,1,0:T(8,128)(2,1)} %held_ref.1), channel_id=1, source_target_pairs={{0,2},{2,0},{4,6},{6,4},{8,10},{10,8},{12,14},{14,12},{16,18},{18,... | collective-permute-start | bytes 786440 | tf_op jit(solution)/shard_map/ppermute | solution.py:300
  14.6 3.4 %collective-permute-start = (bf16[2,128,512]{2,1,0:T(8,128)(2,1)S(1)}, bf16[2,128,512]{2,1,0:T(8,128)(2,1)S(1)}, u32[]{:S(2)}, u32[]{:S(2)}) collective-permute-start(bf16[2,128,512]{2,1,0:T(8,128)(2,1)S(1)} %get-tuple-element.16.n2), channel_id=1, source_target_pairs={{0,2},{2,0},{4,6},{6,4},{8,10},{10,8},{12,14},{14,12},{16,18},{18,... | collective-permute-start | bytes 786440 | tf_op jit(solution)/shard_map/cond/branch_1_fun/ppermute | solution.py:300
  18.0 2.5 %collective-permute-start.5 = (bf16[2,128,512]{2,1,0:T(8,128)(2,1)S(1)}, bf16[2,128,512]{2,1,0:T(8,128)(2,1)S(1)}, u32[]{:S(2)}, u32[]{:S(2)}) collective-permute-start(bf16[2,128,512]{2,1,0:T(8,128)(2,1)S(1)} %collective-permute-done.2.f), channel_id=1, source_target_pairs={{0,2},{2,0},{4,6},{6,4},{8,10},{10,8},{12,14},{14,12},{16,18},{18,... | collective-permute-start | bytes 786440 | tf_op jit(solution)/shard_map/ppermute | solution.py:300
  18.1 2.4 %collective-permute-start.7 = (bf16[2,128,512]{2,1,0:T(8,128)(2,1)S(1)}, bf16[2,128,512]{2,1,0:T(8,128)(2,1)S(1)}, u32[]{:S(2)}, u32[]{:S(2)}) collective-permute-start(bf16[2,128,512]{2,1,0:T(8,128)(2,1)S(1)} %collective-permute-done.6.g1), channel_id=1, source_target_pairs={{0,2},{2,0},{4,6},{6,4},{8,10},{10,8},{12,14},{14,12},{16,18},{18,... | collective-permute-start | bytes 786440 | tf_op jit(solution)/shard_map/ppermute | solution.py:300
  18.6 8.9 %collective-permute-start.3 = (bf16[2,128,512]{2,1,0:T(8,128)(2,1)S(1)}, bf16[2,128,512]{2,1,0:T(8,128)(2,1)S(1)}, u32[]{:S(2)}, u32[]{:S(2)}) collective-permute-start(bf16[2,128,512]{2,1,0:T(8,128)(2,1)S(1)} %collective-permute-done.2.f), channel_id=1, source_target_pairs={{0,2},{2,0},{4,6},{6,4},{8,10},{10,8},{12,14},{14,12},{16,30},{18,... | collective-permute-start | bytes 786440 | tf_op jit(solution)/shard_map/ppermute | solution.py:300
  22.1 8.0 %collective-permute-start.9 = (bf16[32,2048]{1,0:T(8,128)(2,1)S(1)}, bf16[32,2048]{1,0:T(8,128)(2,1)S(1)}, u32[]{:S(2)}, u32[]{:S(2)}) collective-permute-start(bf16[32,2048]{1,0:T(8,128)(2,1)S(1)} %get-tuple-element.78), channel_id=1, source_target_pairs={{0,1},{1,0},{2,3},{3,2},{4,5},{5,4},{6,7},{7,6},{8,9},{9,8},{10,11... | collective-permute-start | bytes 393224 | tf_op jit(solution)/shard_map/ppermute | solution.py:303
  28.7 3.9 %collective-permute-start.8 = (bf16[32,2048]{1,0:T(8,128)(2,1)S(1)}, bf16[32,2048]{1,0:T(8,128)(2,1)S(1)}, u32[]{:S(2)}, u32[]{:S(2)}) collective-permute-start(bf16[32,2048]{1,0:T(8,128)(2,1)S(1)} %get-tuple-element.77), channel_id=1, source_target_pairs={{0,1},{1,0},{2,3},{3,2},{4,5},{5,4},{6,7},{7,6},{8,9},{9,8},{10,11... | collective-permute-start | bytes 393224 | tf_op jit(solution)/shard_map/ppermute | solution.py:303
